TPU v7x, 512 devices: a whole 4x8x8 slice. The times are simulated.
512 devices in a mesh: dp: 128 (over z, x, y_hi, core), mp: 4 (over y_lo).
Axes of the slice: x: 4, y: 8 (y_hi: 2, y_lo: 4; y = y_hi * 4 + y_lo), z: 8, core: 2. Of those that a mesh axis runs over, the one named last changes fastest.
Arguments:
- query_tokens: bfloat16 [128, 257, 5120], P('dp', None, 'mp'), may hold values from -200 to 200
- key_tokens: bfloat16 [128, 257, 5120], P('dp', None, 'mp'), may hold values from -6.5 to 6.5
- value_tokens: bfloat16 [128, 257, 5120], P('dp', None, 'mp'), may hold values from -6 to 6
- head_weight: bfloat16 [5120, 1024], P('mp', 'dp'), may hold values from -0.078125 to 0.078125
- image_cache: bfloat16 [4096, 1024], P(('dp', 'mp')), may hold values from -6 to 6
- text_embed: bfloat16 [4096, 1024], P(('dp', 'mp')), may hold values from -6 to 6
- text_pair: int32 [4096], P(('dp', 'mp')), may hold values from 0 to 4095, as said below
- image_group: int32 [4096], P(('dp', 'mp')), may hold values from 0 to 2047
- text_group: int32 [4096], P(('dp', 'mp')), may hold values from 0 to 2047
- logit_scale: float32 [], replicated, may hold values from 2.6 to 2.8
- logit_bias: float32 [], replicated, may hold values from -9 to -8
Outputs:
- query_grad: bfloat16 [128, 257, 5120], P('dp', None, 'mp')
- key_grad: bfloat16 [128, 257, 5120], P('dp', None, 'mp')
- value_grad: bfloat16 [128, 257, 5120], P('dp', None, 'mp')
- image_grad: float32 [4096, 1024], P(('dp', 'mp'))
- text_grad: float32 [4096, 1024], P(('dp', 'mp'))
- row_loss: float32 [4096], P(('dp', 'mp'))
Inputs may be any that keep to these rules, and one draw needn't show every extreme that they name: Text j is the caption of image text_pair[j]; every image has exactly one such text.
All inputs are finite; a program needn't handle non-finite values.
Results may differ from a plain program's by a relative error of at most 0.012.
Values may be sent and summed in bfloat16 or wider, within the bound.
No kernel may reach another device: no remote copies, remote signals or barrier semaphores. Data moves between devices by JAX's collectives and lax.ppermute only.
A program may use at most 64 MiB of HBM per device.

v0:
```python
import math

import jax
import jax.numpy as jnp
from jax import lax
from jax.sharding import PartitionSpec as P

HEAD_DIM = 128


loss_scale = 8192.0


def broadcast(block, axis, owner):
    block = jnp.where(lax.axis_index(axis) == owner, block, jnp.zeros_like(block))
    return lax.psum(block, axis)


def pair_terms(left_rows, right_rows, labels, temper, offset):
    scores = lax.dot_general(
        left_rows, right_rows, (((1,), (1,)), ((), ())), preferred_element_type=jnp.float32
    )
    logits = temper * scores + offset
    signed = jnp.where(labels, 1.0, -1.0).astype(jnp.float32)
    margin = signed * logits
    losses = -jnp.sum(jax.nn.log_sigmoid(margin), axis=1)
    coeffs = (temper * (-signed * jax.nn.sigmoid(-margin))).astype(jnp.bfloat16)
    return (coeffs, losses)


def unit_rows(raw_rows):
    row_norm = lax.rsqrt(jnp.sum(raw_rows * raw_rows, axis=1, keepdims=True) + 1e-06)
    return (raw_rows * row_norm, row_norm)


def on_device(
    query_tokens,
    key_tokens,
    value_tokens,
    head_weight,
    image_cache,
    text_embed,
    text_pair,
    image_group,
    text_group,
    logit_scale,
    logit_bias,
):
    images_here, seq_len, width_here = query_tokens.shape
    heads_here = width_here // HEAD_DIM
    shaped = (images_here, seq_len, heads_here, HEAD_DIM)
    queries = query_tokens.reshape(shaped)
    key_heads = key_tokens.reshape(shaped)
    value_heads = value_tokens.reshape(shaped)
    inv_root = 1.0 / math.sqrt(HEAD_DIM)
    raw_scores = (
        jnp.einsum("bihd,bjhd->bhij", queries, key_heads, preferred_element_type=jnp.float32)
        * inv_root
    )
    attn_probs = jax.nn.softmax(raw_scores, axis=-1)
    probs_low = attn_probs.astype(jnp.bfloat16)
    attended = jnp.einsum(
        "bhij,bjhd->bihd", probs_low, value_heads, preferred_element_type=jnp.float32
    )
    pooled = jnp.mean(attended, axis=1).reshape(images_here, width_here).astype(jnp.bfloat16)
    full_weight = lax.all_gather(head_weight, "dp", axis=1, tiled=True)
    partial_value = jnp.dot(pooled, full_weight, preferred_element_type=jnp.float32)
    fresh = lax.psum(partial_value, "mp")
    mp_index = lax.axis_index("mp")
    dp_index = lax.axis_index("dp")
    rows = image_cache.shape[0]
    block = rows * lax.axis_size("mp")
    is_fresh = (jnp.arange(rows) == 0) & (mp_index == 0)
    raw_image = jnp.where(is_fresh[:, None], fresh, image_cache.astype(jnp.float32))
    unit_image, image_norm = unit_rows(raw_image)
    unit_text, text_norm = unit_rows(text_embed.astype(jnp.float32))
    image_low = unit_image.astype(jnp.bfloat16)
    text_low = unit_text.astype(jnp.bfloat16)
    group_images, group_texts, group_igroups, group_pairs, group_tgroups = (
        lax.all_gather(image_low, "mp", axis=0, tiled=True),
        lax.all_gather(text_low, "mp", axis=0, tiled=True),
        lax.all_gather(image_group, "mp", axis=0, tiled=True),
        lax.all_gather(text_pair, "mp", axis=0, tiled=True),
        lax.all_gather(text_group, "mp", axis=0, tiled=True),
    )
    group_index = dp_index * block + jnp.arange(block)
    temper = jnp.exp(logit_scale)
    piece_images = lax.all_gather(image_low, "dp", axis=0, tiled=True)
    piece_texts = lax.all_gather(text_low, "dp", axis=0, tiled=True)
    piece_igroups = lax.all_gather(image_group, "dp", axis=0, tiled=True)
    piece_pairs = lax.all_gather(text_pair, "dp", axis=0, tiled=True)
    piece_tgroups = lax.all_gather(text_group, "dp", axis=0, tiled=True)
    labels = (piece_pairs[None, :] == group_index[:, None]) | (
        group_igroups[:, None] == piece_tgroups[None, :]
    )
    coeffs, losses = pair_terms(group_images, piece_texts, labels, temper, logit_bias)
    image_part, losses = (jnp.dot(coeffs, piece_texts, preferred_element_type=jnp.float32), losses)
    count = piece_images.shape[0]
    spots = jnp.arange(count)
    piece_index = spots // rows * block + mp_index * rows + spots % rows
    labels_back = (group_pairs[:, None] == piece_index[None, :]) | (
        group_tgroups[:, None] == piece_igroups[None, :]
    )
    coeffs_back, unused = pair_terms(group_texts, piece_images, labels_back, temper, logit_bias)
    text_part = jnp.dot(coeffs_back, piece_images, preferred_element_type=jnp.float32)
    image_dir, text_dir, row_loss = (
        lax.psum_scatter(image_part, "mp", scatter_dimension=0, tiled=True),
        lax.psum_scatter(text_part, "mp", scatter_dimension=0, tiled=True),
        lax.psum_scatter(losses, "mp", scatter_dimension=0, tiled=True),
    )
    image_grad = (
        image_dir - unit_image * jnp.sum(unit_image * image_dir, axis=1, keepdims=True)
    ) * image_norm
    text_grad = (
        text_dir - unit_text * jnp.sum(unit_text * text_dir, axis=1, keepdims=True)
    ) * text_norm
    fresh_low = broadcast(image_grad[0:1].astype(jnp.bfloat16), "mp", 0)
    pooled_grad = lax.dot_general(
        fresh_low, full_weight, (((1,), (1,)), ((), ())), preferred_element_type=jnp.float32
    )
    cotangent = (
        (pooled_grad * (loss_scale / seq_len))
        .astype(jnp.bfloat16)
        .reshape(images_here, heads_here, HEAD_DIM)
    )
    prob_grad = jnp.einsum(
        "bhd,bjhd->bhj", cotangent, value_heads, preferred_element_type=jnp.float32
    )
    centre = jnp.sum(attn_probs * prob_grad[:, :, None, :], axis=-1, keepdims=True)
    score_grad = (attn_probs * (prob_grad[:, :, None, :] - centre)).astype(jnp.bfloat16)
    query_grad = (
        jnp.einsum("bhij,bjhd->bihd", score_grad, key_heads, preferred_element_type=jnp.float32)
        * inv_root
    )
    key_grad = (
        jnp.einsum("bhij,bihd->bjhd", score_grad, queries, preferred_element_type=jnp.float32)
        * inv_root
    )
    column_mass = jnp.sum(probs_low, axis=2, dtype=jnp.float32)
    value_grad = jnp.einsum("bhj,bhd->bjhd", column_mass, cotangent.astype(jnp.float32))
    out_shape = (images_here, seq_len, width_here)
    return (
        query_grad.reshape(out_shape).astype(jnp.bfloat16),
        key_grad.reshape(out_shape).astype(jnp.bfloat16),
        value_grad.reshape(out_shape).astype(jnp.bfloat16),
        image_grad,
        text_grad,
        row_loss,
    )


def solution(mesh):
    return jax.shard_map(
        on_device,
        mesh=mesh,
        in_specs=(
            P("dp", None, "mp"),
            P("dp", None, "mp"),
            P("dp", None, "mp"),
            P("mp", "dp"),
            P(("dp", "mp"), None),
            P(("dp", "mp"), None),
            P(("dp", "mp")),
            P(("dp", "mp")),
            P(("dp", "mp")),
            P(),
            P(),
        ),
        out_specs=(
            P("dp", None, "mp"),
            P("dp", None, "mp"),
            P("dp", None, "mp"),
            P(("dp", "mp"), None),
            P(("dp", "mp"), None),
            P(("dp", "mp")),
        ),
        check_vma=False,
    )
```

profile of v0, /device:TPU:2, one launch (start us, length us, event | category | flops | bytes accessed | tf_op | source)
XLA Modules:
  0.0 1060.5 jit_solution(14718007973828458825)
XLA Ops:
  7.2 0.0 all-gather.4.cloned.1.call-start
  7.2 0.7 all-gather.4.cloned.1.call-update
  7.9 0.0 all-gather.6.cloned.1.call-start
  8.0 0.8 fusion.61
  8.8 1.4 fusion.57
  10.2 0.0 all-gather.6.cloned.1.call-update
  10.2 0.0 reduce-scatter.3.cloned.1.call-start
  10.3 1.5 reshape.207
  11.8 0.4 reshape.208
  12.2 1.8 reshape.209
  14.0 0.9 fusion.26
  14.9 3.0 fusion.84
  18.0 0.0 copy-start.16
  18.0 1.2 convolution_reduce_fusion
  19.2 0.6 copy-done
  19.9 1.3 dynamic-slice
  21.1 0.6 fusion.83
  23.1 0.2 dynamic-update-slice.3
  23.3 0.2 dynamic-update-slice.4
  23.5 0.2 dynamic-update-slice
  23.7 0.2 dynamic-update-slice.2
  24.0 0.2 dynamic-update-slice.1
  24.2 0.2 dynamic-update-slice.5
  25.7 8.5 all-reduce.8
  34.2 797.0 %all-reduce.7 = (s32[1024]{0:T(1024)S(1)}, s32[1024]{0:T(1024)S(1)}, s32[1024]{0:T(1024)S(1)}) all-reduce(s32[1024]{0:T(1024)S(1)} %dynamic-update-slice.2, s32[1024]{0:T(1024)S(1)} %dynamic-update-slice, s32[1024]{0:T(1024)S(1)} %dynamic-update-slice.5), channel_id=1, replica_groups=mesh['dp'=128,'mp'=4] {'dp'}, use_global_device_ids=true, to_apply=%add.2 | all-reduce | flops 3072 | bytes 24576
  831.2 0.0 all-gather.4.cloned.1.call-done
  831.2 2.5 fusion.85
  833.7 10.9 %psum.14 = f32[1024]{0:T(1024)S(1)} all-reduce(f32[1024]{0:T(1024)S(1)} %bitcast.43), channel_id=1, replica_groups=mesh['dp'=128,'mp'=4] {'mp'}, use_global_device_ids=true, to_apply=%region_3.0 | all-reduce | flops 1024 | bytes 8192 | tf_op jit(solution)/shard_map/psum | solution.py:68
  844.6 0.2 multiply_reduce_fusion.3
  844.8 0.1 fusion.63
  844.9 13.1 %all_gather.37 = bf16[32,1024]{1,0:T(8,128)(2,1)S(1)} all-gather(bf16[8,1024]{1,0:T(8,128)(2,1)S(1)} %fusion.63), channel_id=1, replica_groups=mesh['dp'=128,'mp'=4] {'mp'}, dimensions={0}, use_global_device_ids=true | all-gather | bytes 81920 | tf_op jit(solution)/shard_map/all_gather | solution.py:80
  858.1 2.6 fusion.34
  860.7 1.2 fusion.38
  861.9 0.0 reduce-scatter.3.cloned.1.call-update
  861.9 0.0 all-gather.8.cloned.1.call-start
  862.0 0.5 all-gather.8.cloned.1.call-update
  862.5 0.0 reduce-scatter.5.cloned.1.call-start
  863.2 13.1 %all_gather.42 = bf16[32,1024]{1,0:T(8,128)(2,1)S(1)} all-gather(bf16[8,1024]{1,0:T(8,128)(2,1)S(1)} %copy-done.13), channel_id=1, replica_groups=mesh['dp'=128,'mp'=4] {'mp'}, dimensions={0}, use_global_device_ids=true | all-gather | bytes 81920 | tf_op jit(solution)/shard_map/all_gather | solution.py:81
  876.3 10.1 all-reduce.6
  886.4 0.6 dynamic-slice.7
  887.0 6.6 reduce-scatter.3.cloned.1.call-done
  893.6 0.9 multiply_reduce_fusion.2
  894.6 0.8 subtract_multiply_fusion
  895.5 9.1 psum.15
  904.6 0.5 convolution_reduce_fusion.1
  905.1 0.7 copy-done.5
  905.8 0.3 fusion.22
  906.1 3.0 convert_reduce_fusion
  909.1 0.3 copy-done.1
  909.5 1.4 fusion.7
  910.9 115.6 %all-gather.8.cloned.1.call-done = bf16[1024,1024]{1,0:T(8,128)(2,1)} async-done(((bf16[8,1024]{1,0:T(8,128)(2,1)}), bf16[1024,1024]{1,0:T(8,128)(2,1)}) %all-gather.8.cloned.1.call-update) | async-done | bytes 2097168 | tf_op jit(solution)/shard_map/all_gather | solution.py:88
  1026.6 4.1 fusion.19
  1030.6 0.0 reduce-scatter.5.cloned.1.call-update
  1030.7 3.7 fusion.8
  1034.4 0.1 copy.42
  1034.5 0.6 fusion.20
  1035.2 1.2 convert_element_type.135
  1036.4 0.2 copy.41
  1036.6 1.2 convert_element_type.130
  1037.8 0.2 copy.39
  1038.0 1.2 convert_element_type.125
  1039.2 12.4 %reduce-scatter.5.cloned.1.call-done = f32[8,1024]{1,0:T(8,128)} async-done(((f32[32,1024]{1,0:T(8,128)}), f32[8,1024]{1,0:T(8,128)}) %reduce-scatter.5.cloned.1.call-update) | async-done | bytes 32784 | tf_op jit(solution)/shard_map/reduce_scatter | solution.py:108
  1051.6 0.9 fusion.58
  1052.5 1.4 fusion.60
  (54 shorter events, 0.2 us)
Async XLA Ops:
  7.2 4.6 copy-start.10
  7.2 824.0 %all-gather.4.cloned.1.call-start = ((), (), s32[]{:S(2)}) async-start(), calls=%async_computation.2 | async-start | bytes 2641920 | tf_op jit(solution)/shard_map/all_gather | solution.py:66
  7.9 850.1 %all-gather.6.cloned.1.call-start = ((), (), s32[]{:S(2)}) async-start(), calls=%async_computation.3 | async-start | bytes 2113536 | tf_op jit(solution)/shard_map/all_gather | solution.py:89
  10.2 883.4 %reduce-scatter.3.cloned.1.call-start = ((), (), s32[]{:S(2)}) async-start(), calls=%async_computation.4 | async-start | bytes 163840 | tf_op jit(solution)/shard_map/reduce_scatter | solution.py:107
  11.8 3.1 copy-start.8
  12.2 2.7 copy-start.6
  14.0 4.0 copy-start.4
  17.9 1.9 copy-start
  18.0 3.2 copy-start.16
  18.0 5.1 copy-start.17
  18.0 5.3 copy-start.18
  18.0 6.0 copy-start.19
  19.8 824.8 %copy-start.12 = (bf16[8,1024]{1,0:T(8,128)(2,1)S(1)}, bf16[8,1024]{1,0:T(8,128)(2,1)}, u32[]{:S(2)}) copy-start(bf16[8,1024]{1,0:T(8,128)(2,1)} %param.15) | copy-start | bytes 49156
  844.9 17.0 %copy-start.14 = (bf16[8,1024]{1,0:T(8,128)(2,1)}, bf16[8,1024]{1,0:T(8,128)(2,1)S(1)}, u32[]{:S(2)}) copy-start(bf16[8,1024]{1,0:T(8,128)(2,1)S(1)} %fusion.63) | copy-start | bytes 49156
  858.1 2.6 copy-start.3
  858.1 5.1 copy-start.13
  858.1 46.5 %copy-start.2 = (bf16[1280,1024]{0,1:T(8,128)(2,1)S(1)}, bf16[1280,1024]{0,1:T(8,128)(2,1)}, u32[]{:S(2)}) copy-start(bf16[1280,1024]{0,1:T(8,128)(2,1)} %all-gather.4.cloned.1.call-done) | copy-start | bytes 7864324
  861.9 164.7 %all-gather.8.cloned.1.call-start = ((), (), s32[]{:S(2)}) async-start(), calls=%async_computation.5 | async-start | bytes 2113536 | tf_op jit(solution)/shard_map/all_gather | solution.py:88
  862.5 189.1 %reduce-scatter.5.cloned.1.call-start = ((), (), s32[]{:S(2)}) async-start(), calls=%async_computation.6 | async-start | bytes 163840 | tf_op jit(solution)/shard_map/reduce_scatter | solution.py:108
  895.4 13.7 %copy-start.15 = (f32[8,1024]{1,0:T(8,128)}, f32[8,1024]{1,0:T(8,128)S(1)}, u32[]{:S(2)}) copy-start(f32[8,1024]{1,0:T(8,128)S(1)} %subtract_multiply_fusion) | copy-start | bytes 98308
  904.6 1.2 copy-start.5
  904.6 4.6 copy-start.9
  906.1 3.4 copy-start.1
  1026.6 4.1 copy-start.7
  1037.8 13.8 %copy-start.11 = (bf16[8,1024]{1,0:T(8,128)(2,1)S(1)}, bf16[8,1024]{1,0:T(8,128)(2,1)}, u32[]{:S(2)}) copy-start(bf16[8,1024]{1,0:T(8,128)(2,1)} %param.16) | copy-start | bytes 49156
Sparse Core Ops, SparseCore 0:
  12.8 132.9 all-gather.3
  151.0 123.4 all-gather.5
  862.0 31.5 reduce-scatter.2
  899.5 127.0 all-gather.7
  1030.8 20.7 reduce-scatter.4
where the time goes:
time: 1060 us
  blocking collectives  862 us (81%)
  waiting for transfers between devices  136 us (13%)
  matrix products  18.4 us (2%)
  between operations  17.4 us (2%)
  other arithmetic  13.4 us (1%)
  local copies, waits for them, and re-layouts  13.3 us (1%)
    unnamed x3, blocking collectives  816 us
    all_gather x1, waiting for transfers between devices, on_device(): piece_images = lax.all_gather(image_low, 'dp', axis=0, tiled=True)  116 us
  transfers between devices with their start and end apart: 5, of which 3 were waited for; matrix products, arithmetic and copies ran while one was open for 3% of the time, Pallas kernels for 0%

commit v1 on v0

v1 whole, which is shorter than its diff:
```python
import math

import jax
import jax.numpy as jnp
from jax import lax
from jax.sharding import Mesh
from jax.sharding import PartitionSpec as P

HEAD_DIM = 128
LOSS_SCALE = 8192.0
EMBED = 1024
WIDTH = 1280
TAIL = 128
INV_ROOT = 1.0 / math.sqrt(HEAD_DIM)

TEXT_AXES = ("x", "h", "c")
IMAGE_AXES = ("z", "m")


def spread(block, axes, count):
    sent = jnp.broadcast_to(block[None], (count,) + block.shape)
    return lax.all_to_all(sent, axes, 0, 0)


def unit_rows(raw_rows):
    row_norm = lax.rsqrt(jnp.sum(raw_rows * raw_rows, axis=1, keepdims=True) + 1e-06)
    return raw_rows * row_norm, row_norm


def label_tail(*labels):
    parts = []
    for label in labels:
        parts += [label // 64, label % 64]
    tail = jnp.stack(parts, axis=1).astype(jnp.bfloat16)
    return jnp.pad(tail, ((0, 0), (0, TAIL - tail.shape[1])))


def label_of(tail, place):
    tail = tail.astype(jnp.float32)
    return (tail[:, 2 * place] * 64.0 + tail[:, 2 * place + 1]).astype(jnp.int32)


def pair_terms(left_rows, right_rows, labels, temper, offset):
    scores = lax.dot_general(
        left_rows, right_rows, (((1,), (1,)), ((), ())), preferred_element_type=jnp.float32
    )
    logits = temper * scores + offset
    signed = jnp.where(labels, 1.0, -1.0).astype(jnp.float32)
    margin = signed * logits
    losses = -jnp.sum(jax.nn.log_sigmoid(margin), axis=1, keepdims=True)
    coeffs = (temper * (-signed * jax.nn.sigmoid(-margin))).astype(jnp.bfloat16)
    return coeffs, losses


def on_device(
    query_tokens,
    key_tokens,
    value_tokens,
    head_weight,
    image_cache,
    text_embed,
    text_pair,
    image_group,
    text_group,
    logit_scale,
    logit_bias,
):
    z, m = lax.axis_index("z"), lax.axis_index("m")
    xhc = (lax.axis_index("x") * 2 + lax.axis_index("h")) * 2 + lax.axis_index("c")
    temper = jnp.exp(logit_scale)

    unit_text, text_norm = unit_rows(text_embed.astype(jnp.float32))
    text_message = jnp.concatenate(
        [unit_text.astype(jnp.bfloat16), label_tail(text_pair, text_group), head_weight.T], axis=1
    )
    text_got = spread(text_message, TEXT_AXES, 16).reshape(128, EMBED + TAIL + WIDTH)
    texts = text_got[:, :EMBED]
    text_tail = text_got[:, EMBED : EMBED + TAIL]
    weight_t = text_got[:, EMBED + TAIL :]
    pair_of, tgroup_of = label_of(text_tail, 0), label_of(text_tail, 1)

    cached, cached_norm = unit_rows(image_cache.astype(jnp.float32))
    image_message = jnp.concatenate(
        [cached.astype(jnp.bfloat16), label_tail(image_group)], axis=1
    )
    image_got = spread(image_message, IMAGE_AXES, 32).reshape(256, EMBED + TAIL)
    igroup_of = label_of(image_got[:, EMBED:], 0)
    spots = jnp.arange(256)
    image_index = ((spots // 32) * 16 + xhc) * 32 + spots % 32

    shaped = (257, 10, HEAD_DIM)
    queries, key_heads, value_heads = (
        t.reshape(shaped) for t in (query_tokens, key_tokens, value_tokens)
    )
    raw_scores = (
        jnp.einsum("ihd,jhd->hij", queries, key_heads, preferred_element_type=jnp.float32)
        * INV_ROOT
    )
    attn_probs = jax.nn.softmax(raw_scores, axis=-1)
    probs_low = attn_probs.astype(jnp.bfloat16)
    column_mass = jnp.sum(probs_low, axis=1, dtype=jnp.float32)
    pooled = jnp.sum(column_mass.T[:, :, None] * value_heads.astype(jnp.float32), axis=0) / 257.0
    pooled = pooled.reshape(1, WIDTH).astype(jnp.bfloat16)

    pooled_all = spread(pooled, "z", 8).reshape(8, WIDTH)
    partial_cols = lax.dot_general(
        pooled_all, weight_t, (((1,), (1,)), ((), ())), preferred_element_type=jnp.float32
    )
    fresh_got = spread(partial_cols, IMAGE_AXES, 32).reshape(8, 4, 8, 128)
    fresh = jnp.sum(fresh_got, axis=1).transpose(1, 0, 2).reshape(8, EMBED)
    fresh_unit, fresh_norm = unit_rows(fresh)
    fresh_low = fresh_unit.astype(jnp.bfloat16)

    labels = (pair_of[None, :] == image_index[::32, None]) | (
        igroup_of[::32, None] == tgroup_of[None, :]
    )
    coeffs, _ = pair_terms(fresh_low, texts, labels, temper, logit_bias)
    dir_part = jnp.dot(coeffs, texts, preferred_element_type=jnp.float32)
    dot_part = jnp.sum(dir_part * fresh_unit, axis=1, keepdims=True)
    back = jnp.concatenate(
        [
            dir_part.reshape(8, 8, 128).transpose(1, 0, 2),
            jnp.broadcast_to(dot_part[None], (8, 8, 128)),
        ],
        axis=1,
    )
    back = jnp.repeat(back, 4, axis=0)
    back_sum = jnp.sum(lax.all_to_all(back, IMAGE_AXES, 0, 0), axis=0)
    unit_cols = lax.dynamic_slice(fresh_unit, (0, z * 128), (8, 128))
    fresh_grad = ((back_sum[:8] - unit_cols * back_sum[8:]) * fresh_norm).astype(jnp.bfloat16)
    pooled_part = jnp.dot(fresh_grad, weight_t, preferred_element_type=jnp.float32)
    pooled_grad = jnp.sum(lax.all_to_all(pooled_part[:, None], "z", 0, 0), axis=0)

    is_fresh = spots % 32 == 0
    image_rows = jnp.where(
        is_fresh[:, None], jnp.repeat(fresh_low, 32, axis=0), image_got[:, :EMBED]
    )
    labels = (pair_of[None, :] == image_index[:, None]) | (igroup_of[:, None] == tgroup_of[None, :])
    coeffs, losses = pair_terms(image_rows, texts, labels, temper, logit_bias)
    image_part = jnp.dot(coeffs, texts, preferred_element_type=jnp.float32)
    text_part = lax.dot_general(
        coeffs, image_rows, (((0,), (0,)), ((), ())), preferred_element_type=jnp.float32
    )
    image_back = jnp.concatenate([image_part, jnp.broadcast_to(losses, (256, TAIL))], axis=1)
    image_sum = jnp.sum(
        lax.all_to_all(image_back.reshape(32, 8, EMBED + TAIL), IMAGE_AXES, 0, 0), axis=0
    )
    text_dir = jnp.sum(lax.all_to_all(text_part.reshape(16, 8, EMBED), TEXT_AXES, 0, 0), axis=0)
    image_dir, row_loss = image_sum[:, :EMBED], image_sum[:, EMBED]

    own_fresh = ((jnp.arange(8) == 0) & (m == 0))[:, None]
    unit_image = jnp.where(own_fresh, lax.dynamic_slice(fresh_unit, (z, 0), (1, EMBED)), cached)
    image_norm = jnp.where(own_fresh, lax.dynamic_slice(fresh_norm, (z, 0), (1, 1)), cached_norm)
    image_grad = (
        image_dir - unit_image * jnp.sum(unit_image * image_dir, axis=1, keepdims=True)
    ) * image_norm
    text_grad = (
        text_dir - unit_text * jnp.sum(unit_text * text_dir, axis=1, keepdims=True)
    ) * text_norm

    cotangent = (pooled_grad * (LOSS_SCALE / 257)).astype(jnp.bfloat16).reshape(10, HEAD_DIM)
    prob_grad = jnp.einsum("hd,jhd->hj", cotangent, value_heads, preferred_element_type=jnp.float32)
    centre = jnp.sum(attn_probs * prob_grad[:, None, :], axis=-1, keepdims=True)
    score_grad = (attn_probs * (prob_grad[:, None, :] - centre)).astype(jnp.bfloat16)
    query_grad = (
        jnp.einsum("hij,jhd->ihd", score_grad, key_heads, preferred_element_type=jnp.float32)
        * INV_ROOT
    )
    key_grad = (
        jnp.einsum("hij,ihd->jhd", score_grad, queries, preferred_element_type=jnp.float32)
        * INV_ROOT
    )
    value_grad = jnp.einsum("hj,hd->jhd", column_mass, cotangent.astype(jnp.float32))
    out_shape = (1, 257, WIDTH)
    return (
        query_grad.reshape(out_shape).astype(jnp.bfloat16),
        key_grad.reshape(out_shape).astype(jnp.bfloat16),
        value_grad.reshape(out_shape).astype(jnp.bfloat16),
        image_grad,
        text_grad,
        row_loss,
    )


def solution(mesh):
    fine = Mesh(mesh.devices.reshape(8, 4, 2, 2, 4), ("z", "x", "h", "c", "m"))
    dp, pairs = ("z", "x", "h", "c"), ("z", "x", "h", "c", "m")
    tokens = P(dp, None, "m")
    return jax.shard_map(
        on_device,
        mesh=fine,
        in_specs=(
            tokens,
            tokens,
            tokens,
            P("m", dp),
            P(pairs, None),
            P(pairs, None),
            P(pairs),
            P(pairs),
            P(pairs),
            P(),
            P(),
        ),
        out_specs=(tokens, tokens, tokens, P(pairs, None), P(pairs, None), P(pairs)),
        check_vma=False,
    )
```

time: 1060 us -> 196 us (0.18)
  the two profiles are of different devices: /device:TPU:2 before, /device:TPU:16 now
where the time goes in v1:
time: 196 us; the launch traced here: 195 us
  waiting for transfers between devices  102 us (52%)
  starting transfers between devices  45.6 us (23%)
  local copies, waits for them, and re-layouts  18.9 us (10%)
  other arithmetic  15.6 us (8%)
  matrix products  9.67 us (5%)
  between operations  2.46 us (1%)
    all_to_all x4, waiting for transfers between devices, spread(): return lax.all_to_all(sent, axes, 0, 0)  52.4 us
    all_to_all x4, starting transfers between devices, spread(): return lax.all_to_all(sent, axes, 0, 0)  28.9 us
    all_to_all x1, waiting for transfers between devices, on_device(): lax.all_to_all(image_back.reshape(32, 8, EMBED + TAIL), IMAGE_AXES, 0, 0)  17.8 us
    all_to_all x1, waiting for transfers between devices, on_device(): lax.all_to_all(text_part.reshape(16, 8, EMBED), TEXT_AXES, 0, 0)  16.2 us
    all_to_all x1, waiting for transfers between devices, on_device(): back_sum = jnp.sum(lax.all_to_all(back, IMAGE_AXES, 0, 0), axis=0)  9.15 us
    all_to_all x1, waiting for transfers between devices, on_device(): lax.all_to_all(pooled_part[:, None], 'z', 0, 0)  6.94 us
    all_to_all x1, starting transfers between devices, on_device(): back_sum = jnp.sum(lax.all_to_all(back, IMAGE_AXES, 0, 0), axis=0)  5.37 us
    all_to_all x1, starting transfers between devices, on_device(): lax.all_to_all(image_back.reshape(32, 8, EMBED + TAIL), IMAGE_AXES, 0, 0)  4.37 us
  transfers between devices with their start and end apart: 8, of which 8 were waited for; matrix products, arithmetic and copies ran while one was open for 11% of the time, Pallas kernels for 0%

profile of v1, /device:TPU:16, one launch (start us, length us, event | category | flops | bytes accessed | tf_op | source)
XLA Modules:
  0.0 194.7 jit_solution(13872639973915097078)
XLA Ops:
  0.6 1.5 reshape.238
  2.2 0.4 reshape.239
  2.6 0.9 fusion.24
  3.6 2.9 %fusion.108 = (f32[10,257]{1,0:T(8,128)S(1)}, f32[10,257,257]{1,2,0:T(8,128)S(1)}) fusion(f32[10,257,257]{1,2,0:T(8,128)S(1)} %fusion.24), kind=kOutput, calls=%fused_computation.180 | output fusion | flops 2642216 | bytes 5294200 | tf_op jit(solution)/shard_map/sub | solution.py:99
  6.6 1.9 copy-done
  8.5 0.6 convert_reduce_fusion
  9.2 0.6 mul.229
  9.8 0.2 mul.230
  10.1 1.3 multiply_reduce_fusion.2
  11.4 0.5 broadcast.295
  12.0 0.8 reduce.11
  12.7 0.6 reshape.258
  13.3 10.3 %all-to-all-start.2 = ((bf16[8,2,640]{2,1,0:T(2,128)(2,1)}), bf16[8,2,640]{2,1,0:T(2,128)(2,1)S(1)}, u32[]{:S(2)}, u32[]{:S(2)}) async-start(bf16[8,2,640]{2,1,0:T(2,128)(2,1)} %reshape.258), calls=%async_computation.2 | async-start | bytes 40960 | tf_op jit(solution)/shard_map/all_to_all | solution.py:22
  24.1 7.4 %all-to-all-done.2 = bf16[8,2,640]{2,1,0:T(2,128)(2,1)S(1)} async-done(((bf16[8,2,640]{2,1,0:T(2,128)(2,1)}), bf16[8,2,640]{2,1,0:T(2,128)(2,1)S(1)}, u32[]{:S(2)}, u32[]{:S(2)}) %all-to-all-start.2) | async-done | bytes 20512 | tf_op jit(solution)/shard_map/all_to_all | solution.py:22
  31.4 0.9 broadcast_in_dim.61
  32.3 8.0 %all-to-all-start = ((bf16[16,8,2432]{2,1,0:T(8,128)(2,1)}), bf16[16,8,2432]{2,1,0:T(8,128)(2,1)S(1)}, u32[]{:S(2)}, u32[]{:S(2)}) async-start(bf16[16,8,2432]{2,1,0:T(8,128)(2,1)} %broadcast_in_dim.61), calls=%async_computation | async-start | bytes 1245184 | tf_op jit(solution)/shard_map/all_to_all | solution.py:22
  40.3 22.5 %all-to-all-done = bf16[16,8,2432]{2,1,0:T(8,128)(2,1)S(1)} async-done(((bf16[16,8,2432]{2,1,0:T(8,128)(2,1)}), bf16[16,8,2432]{2,1,0:T(8,128)(2,1)S(1)}, u32[]{:S(2)}, u32[]{:S(2)}) %all-to-all-start) | async-done | bytes 622624 | tf_op jit(solution)/shard_map/all_to_all | solution.py:22
  63.0 0.7 broadcast_in_dim.75
  63.7 4.5 %all-to-all-start.3 = ((f32[32,8,128]{2,1,0:T(8,128)}), f32[32,8,128]{2,1,0:T(8,128)S(1)}, u32[]{:S(2)}, u32[]{:S(2)}) async-start(f32[32,8,128]{2,1,0:T(8,128)} %broadcast_in_dim.75), calls=%async_computation.3 | async-start | bytes 262144 | tf_op jit(solution)/shard_map/all_to_all | solution.py:22
  68.4 8.4 %all-to-all-done.3 = f32[32,8,128]{2,1,0:T(8,128)S(1)} async-done(((f32[32,8,128]{2,1,0:T(8,128)}), f32[32,8,128]{2,1,0:T(8,128)S(1)}, u32[]{:S(2)}, u32[]{:S(2)}) %all-to-all-start.3) | async-done | bytes 131104 | tf_op jit(solution)/shard_map/all_to_all | solution.py:22
  76.9 0.6 dynamic-slice.3
  77.5 1.2 broadcast_select_fusion
  78.7 0.9 broadcast_in_dim.68
  79.6 6.2 %all-to-all-start.1 = ((bf16[32,8,1152]{2,1,0:T(8,128)(2,1)}), bf16[32,8,1152]{2,1,0:T(8,128)(2,1)S(1)}, u32[]{:S(2)}, u32[]{:S(2)}) async-start(bf16[32,8,1152]{2,1,0:T(8,128)(2,1)} %broadcast_in_dim.68), calls=%async_computation.1 | async-start | bytes 1179648 | tf_op jit(solution)/shard_map/all_to_all | solution.py:22
  85.8 0.8 copy.68
  86.6 0.4 reshape.247
  88.4 0.2 fusion.47
  88.7 14.2 %all-to-all-done.1 = bf16[32,8,1152]{2,1,0:T(8,128)(2,1)S(1)} async-done(((bf16[32,8,1152]{2,1,0:T(8,128)(2,1)}), bf16[32,8,1152]{2,1,0:T(8,128)(2,1)S(1)}, u32[]{:S(2)}, u32[]{:S(2)}) %all-to-all-start.1) | async-done | bytes 589856 | tf_op jit(solution)/shard_map/all_to_all | solution.py:22
  102.9 0.2 fusion.41
  103.3 0.5 multiply_reduce_fusion.3
  104.0 0.7 broadcast_in_dim.77
  104.7 5.4 %all-to-all-start.4 = ((f32[32,16,128]{2,1,0:T(8,128)}), f32[32,16,128]{2,1,0:T(8,128)}, u32[]{:S(2)}, u32[]{:S(2)}) async-start(f32[32,16,128]{2,1,0:T(8,128)} %bitcast.15), calls=%async_computation.4 | async-start | bytes 524288 | tf_op jit(solution)/shard_map/all_to_all | solution.py:128
  110.1 1.0 fusion.39
  111.1 0.4 fusion.34
  111.5 9.2 %all-to-all-done.4 = f32[32,16,128]{2,1,0:T(8,128)} async-done(((f32[32,16,128]{2,1,0:T(8,128)}), f32[32,16,128]{2,1,0:T(8,128)}, u32[]{:S(2)}, u32[]{:S(2)}) %all-to-all-start.4) | async-done | bytes 262176 | tf_op jit(solution)/shard_map/all_to_all | solution.py:128
  120.6 1.0 reduce_sum.152
  121.6 0.2 convolution_bitcast_fusion
  121.8 0.7 copy.62
  122.5 3.3 %all-to-all-start.5 = ((f32[8,1,1280]{2,1,0:T(1,128)}), f32[8,1,1280]{2,1,0:T(1,128)S(1)}, u32[]{:S(2)}, u32[]{:S(2)}) async-start(f32[8,1,1280]{2,1,0:T(1,128)} %copy.62), calls=%async_computation.5 | async-start | bytes 81920 | tf_op jit(solution)/shard_map/all_to_all | solution.py:132
  125.9 1.1 convolution_bitcast_fusion.1
  126.9 6.9 %all-to-all-done.5 = f32[8,1,1280]{2,1,0:T(1,128)S(1)} async-done(((f32[8,1,1280]{2,1,0:T(1,128)}), f32[8,1,1280]{2,1,0:T(1,128)S(1)}, u32[]{:S(2)}, u32[]{:S(2)}) %all-to-all-start.5) | async-done | bytes 40992 | tf_op jit(solution)/shard_map/all_to_all | solution.py:132
  133.9 3.6 %all-to-all-start.7 = ((f32[16,8,1024]{2,1,0:T(8,128)}), f32[16,8,1024]{2,1,0:T(8,128)S(1)}, u32[]{:S(2)}, u32[]{:S(2)}) async-start(f32[16,8,1024]{2,1,0:T(8,128)} %convolution_bitcast_fusion.1), calls=%async_computation.7 | async-start | bytes 1048576 | tf_op jit(solution)/shard_map/all_to_all | solution.py:148
  137.5 0.8 broadcast_in_dim.130
  138.2 1.1 maximum_bitcast_fusion
  139.4 0.6 fusion.20
  140.0 1.2 convert_element_type.177
  141.3 0.3 fusion.21
  141.6 16.2 %all-to-all-done.7 = f32[16,8,1024]{2,1,0:T(8,128)S(1)} async-done(((f32[16,8,1024]{2,1,0:T(8,128)}), f32[16,8,1024]{2,1,0:T(8,128)S(1)}, u32[]{:S(2)}, u32[]{:S(2)}) %all-to-all-start.7) | async-done | bytes 524320 | tf_op jit(solution)/shard_map/all_to_all | solution.py:148
  157.8 0.8 copy-done.7
  158.6 4.4 %all-to-all-start.6 = ((f32[32,8,1152]{2,1,0:T(8,128)}), f32[32,8,1152]{2,1,0:T(8,128)S(1)}, u32[]{:S(2)}, u32[]{:S(2)}) async-start(f32[32,8,1152]{2,1,0:T(8,128)} %maximum_bitcast_fusion), calls=%async_computation.6 | async-start | bytes 2359296 | tf_op jit(solution)/shard_map/all_to_all | solution.py:146
  163.0 2.9 %multiply_reduce_fusion = f32[10,257]{1,0:T(8,128)S(1)} fusion(f32[10,257]{1,0:T(8,128)S(1)} %bitcast.70, f32[10,257,257]{1,2,0:T(8,128)} %copy-done, f32[10,257]{1,0:T(8,128)S(1)} %get-tuple-element.20), kind=kLoop, calls=%fused_computation.2 | loop fusion | flops 1978900 | bytes 2672800 | tf_op jit(solution)/shard_map/reduce_sum | solution.py:163
  165.9 0.4 copy-done.1
  166.3 1.4 fusion.7
  167.8 0.2 copy.67
  168.0 1.2 convert_element_type.174
  169.2 3.7 %fusion.8 = bf16[257,10,128]{2,0,1:T(8,128)(2,1)S(1)} fusion(f32[10,257]{1,0:T(8,128)S(1)} %multiply_reduce_fusion, f32[10,257]{1,0:T(8,128)S(1)} %bitcast.72, bf16[257,10,128]{2,1,0:T(8,128)(2,1)S(1)} %copy-done.3, f32[10,257,257]{1,2,0:T(8,128)} %copy-done, f32[10,257]{1,0:T(8,128)S(1)} %get-tuple-element.20), kind=kOutput, calls=%fused_computation.17 | convolution fusion | flops 172385312 | bytes 3988640 | tf_op jit(solution)/shard_map/hij,jhd->ihd/dot_general | solution.py:166
  172.9 0.2 copy.65
  173.1 1.2 convert_element_type.171
  174.4 0.2 fusion.61
  174.6 0.7 fusion.63
  175.3 17.8 %all-to-all-done.6 = f32[32,8,1152]{2,1,0:T(8,128)S(1)} async-done(((f32[32,8,1152]{2,1,0:T(8,128)}), f32[32,8,1152]{2,1,0:T(8,128)S(1)}, u32[]{:S(2)}, u32[]{:S(2)}) %all-to-all-start.6) | async-done | bytes 1179680 | tf_op jit(solution)/shard_map/all_to_all | solution.py:146
  193.1 0.6 slice_reduce_fusion
  193.8 0.2 fusion.58
  194.0 0.7 fusion.60
  (71 shorter events, 2.0 us)
Async XLA Ops:
  0.6 1.5 copy-start.9
  2.2 1.3 copy-start.4
  2.6 1.0 copy-start.2
  6.6 1.9 copy-start
  9.8 13.9 %copy-start.17 = (s32[8]{0:T(128)S(1)}, s32[8]{0:T(128)}, u32[]{:S(2)}) copy-start(s32[8]{0:T(128)} %param.17) | copy-start | bytes 100
  9.8 13.9 %copy-start.15 = (s32[8]{0:T(128)S(1)}, s32[8]{0:T(128)}, u32[]{:S(2)}) copy-start(s32[8]{0:T(128)} %param.18) | copy-start | bytes 100
  9.8 13.9 %copy-start.16 = (s32[8]{0:T(128)S(1)}, s32[8]{0:T(128)}, u32[]{:S(2)}) copy-start(s32[8]{0:T(128)} %param.19) | copy-start | bytes 100
  9.8 14.0 %copy-start.11 = (bf16[8,1024]{1,0:T(8,128)(2,1)S(1)}, bf16[8,1024]{1,0:T(8,128)(2,1)}, u32[]{:S(2)}) copy-start(bf16[8,1024]{1,0:T(8,128)(2,1)} %param.16) | copy-start | bytes 49156
  10.1 13.9 %copy-start.13 = (bf16[1280,8]{0,1:T(8,128)(2,1)S(1)}, bf16[1280,8]{0,1:T(8,128)(2,1)}, u32[]{:S(2)}) copy-start(bf16[1280,8]{0,1:T(8,128)(2,1)} %param.14) | copy-start | bytes 61444
  10.1 58.2 %copy-start.12 = (bf16[8,1024]{1,0:T(8,128)(2,1)S(1)}, bf16[8,1024]{1,0:T(8,128)(2,1)}, u32[]{:S(2)}) copy-start(bf16[8,1024]{1,0:T(8,128)(2,1)} %param.15) | copy-start | bytes 49156
  13.3 18.1 %all-to-all-start.2 = ((bf16[8,2,640]{2,1,0:T(2,128)(2,1)}), bf16[8,2,640]{2,1,0:T(2,128)(2,1)S(1)}, u32[]{:S(2)}, u32[]{:S(2)}) async-start(bf16[8,2,640]{2,1,0:T(2,128)(2,1)} %reshape.258), calls=%async_computation.2 | async-start | bytes 40960 | tf_op jit(solution)/shard_map/all_to_all | solution.py:22
  32.3 54.3 %copy-start.6 = (bf16[1,257,1280]{2,1,0:T(8,128)(2,1)S(1)}, bf16[1,257,1280]{2,1,0:T(8,128)(2,1)}, u32[]{:S(2)}) copy-start(bf16[1,257,1280]{2,1,0:T(8,128)(2,1)} %param.13) | copy-start | bytes 1973764
  32.3 30.5 %all-to-all-start = ((bf16[16,8,2432]{2,1,0:T(8,128)(2,1)}), bf16[16,8,2432]{2,1,0:T(8,128)(2,1)S(1)}, u32[]{:S(2)}, u32[]{:S(2)}) async-start(bf16[16,8,2432]{2,1,0:T(8,128)(2,1)} %broadcast_in_dim.61), calls=%async_computation | async-start | bytes 1245184 | tf_op jit(solution)/shard_map/all_to_all | solution.py:22
  63.7 13.1 %all-to-all-start.3 = ((f32[32,8,128]{2,1,0:T(8,128)}), f32[32,8,128]{2,1,0:T(8,128)S(1)}, u32[]{:S(2)}, u32[]{:S(2)}) async-start(f32[32,8,128]{2,1,0:T(8,128)} %broadcast_in_dim.75), calls=%async_computation.3 | async-start | bytes 262144 | tf_op jit(solution)/shard_map/all_to_all | solution.py:22
  79.6 23.3 %all-to-all-start.1 = ((bf16[32,8,1152]{2,1,0:T(8,128)(2,1)}), bf16[32,8,1152]{2,1,0:T(8,128)(2,1)S(1)}, u32[]{:S(2)}, u32[]{:S(2)}) async-start(bf16[32,8,1152]{2,1,0:T(8,128)(2,1)} %broadcast_in_dim.68), calls=%async_computation.1 | async-start | bytes 1179648 | tf_op jit(solution)/shard_map/all_to_all | solution.py:22
  104.7 15.9 %all-to-all-start.4 = ((f32[32,16,128]{2,1,0:T(8,128)}), f32[32,16,128]{2,1,0:T(8,128)}, u32[]{:S(2)}, u32[]{:S(2)}) async-start(f32[32,16,128]{2,1,0:T(8,128)} %bitcast.15), calls=%async_computation.4 | async-start | bytes 524288 | tf_op jit(solution)/shard_map/all_to_all | solution.py:128
  122.5 11.4 %all-to-all-start.5 = ((f32[8,1,1280]{2,1,0:T(1,128)}), f32[8,1,1280]{2,1,0:T(1,128)S(1)}, u32[]{:S(2)}, u32[]{:S(2)}) async-start(f32[8,1,1280]{2,1,0:T(1,128)} %copy.62), calls=%async_computation.5 | async-start | bytes 81920 | tf_op jit(solution)/shard_map/all_to_all | solution.py:132
  125.8 13.6 %copy-start.10 = (f32[10,257]{0,1:T(8,128)S(1)}, f32[10,257]{0,1:T(8,128)}, u32[]{:S(2)}) copy-start(f32[10,257]{0,1:T(8,128)} %copy.68) | copy-start | bytes 30844
  133.9 23.9 %all-to-all-start.7 = ((f32[16,8,1024]{2,1,0:T(8,128)}), f32[16,8,1024]{2,1,0:T(8,128)S(1)}, u32[]{:S(2)}, u32[]{:S(2)}) async-start(f32[16,8,1024]{2,1,0:T(8,128)} %convolution_bitcast_fusion.1), calls=%async_computation.7 | async-start | bytes 1048576 | tf_op jit(solution)/shard_map/all_to_all | solution.py:148
  157.8 0.8 copy-start.7
  157.8 8.1 %copy-start.5 = (bf16[257,10,128]{2,1,0:T(8,128)(2,1)S(1)}, bf16[257,10,128]{2,1,0:T(8,128)(2,1)}, u32[]{:S(2)}) copy-start(bf16[257,10,128]{2,1,0:T(8,128)(2,1)} %copy-done.4) | copy-start | bytes 1973764
  158.6 34.5 %all-to-all-start.6 = ((f32[32,8,1152]{2,1,0:T(8,128)}), f32[32,8,1152]{2,1,0:T(8,128)S(1)}, u32[]{:S(2)}, u32[]{:S(2)}) async-start(f32[32,8,1152]{2,1,0:T(8,128)} %maximum_bitcast_fusion), calls=%async_computation.6 | async-start | bytes 2359296 | tf_op jit(solution)/shard_map/all_to_all | solution.py:146
  163.0 3.4 %copy-start.1 = (f32[10,257,257]{1,2,0:T(8,128)S(1)}, f32[10,257,257]{1,2,0:T(8,128)}, u32[]{:S(2)}) copy-start(f32[10,257,257]{1,2,0:T(8,128)} %copy-done) | copy-start | bytes 7925884
  167.8 1.4 copy-start.3
  172.9 1.4 copy-start.8
  173.1 20.8 %copy-start.14 = (f32[8]{0:T(128)S(1)}, f32[8]{0:T(128)}, u32[]{:S(2)}) copy-start(f32[8]{0:T(128)} %get-tuple-element.12) | copy-start | bytes 100

commit v2 on v1

v2 whole, which is shorter than its diff:
```python
import math

import jax
import jax.numpy as jnp
from jax import lax
from jax.sharding import Mesh
from jax.sharding import PartitionSpec as P

HEAD_DIM = 128
LOSS_SCALE = 8192.0
EMBED = 1024
WIDTH = 1280
TAIL = 128
INV_ROOT = 1.0 / math.sqrt(HEAD_DIM)

TEXT_AXES = ("z", "h")
IMAGE_AXES = ("x", "m")
SWAP = [(0, 1), (1, 0)]
BF16, F32 = jnp.bfloat16, jnp.float32


def spread(block, axes, count):
    sent = jnp.broadcast_to(block[None], (count,) + block.shape)
    return lax.all_to_all(sent, axes, 0, 0)


def halves(value):
    high = value.astype(BF16)
    return high, (value - high.astype(F32)).astype(BF16)


def unit_rows(raw_rows):
    row_norm = lax.rsqrt(jnp.sum(raw_rows * raw_rows, axis=1, keepdims=True) + 1e-06)
    return raw_rows * row_norm, row_norm


def label_tail(*labels):
    parts = []
    for label in labels:
        parts += [label // 64, label % 64]
    tail = jnp.stack(parts, axis=1).astype(BF16)
    return jnp.pad(tail, ((0, 0), (0, TAIL - tail.shape[1])))


def label_of(tail, place):
    tail = tail.astype(F32)
    return (tail[:, 2 * place] * 64.0 + tail[:, 2 * place + 1]).astype(jnp.int32)


def contract(left, right, dims):
    return lax.dot_general(left, right, (dims, ((), ())), preferred_element_type=F32)


def on_device(
    query_tokens,
    key_tokens,
    value_tokens,
    head_weight,
    image_cache,
    text_embed,
    text_pair,
    image_group,
    text_group,
    logit_scale,
    logit_bias,
):
    z, x, h, c, m = (lax.axis_index(a) for a in ("z", "x", "h", "c", "m"))
    temper = jnp.exp(logit_scale)

    unit_text, text_norm = unit_rows(text_embed.astype(F32))
    text_message = jnp.concatenate(
        [unit_text.astype(BF16), label_tail(text_pair, text_group), head_weight.T], axis=1
    )
    text_near = spread(text_message, TEXT_AXES, 16)
    text_far = lax.ppermute(text_near, "c", SWAP)
    text_got = jnp.concatenate([text_near, text_far], axis=0).reshape(256, EMBED + TAIL + WIDTH)
    texts = text_got[:, :EMBED]
    text_tail = text_got[:, EMBED : EMBED + TAIL]
    weight_t = text_got[:, EMBED + TAIL :]
    pair_of, tgroup_of = label_of(text_tail, 0), label_of(text_tail, 1)

    spot = jnp.arange(EMBED)
    column = (
        (spot % 128) // 16 * 128
        + spot // 256 * 32
        + (spot // 8) % 2 * 16
        + ((spot // 128) % 2 + c) % 2 * 8
        + spot % 8
    )
    order = (jnp.arange(EMBED)[:, None] == column[None, :]).astype(BF16)
    texts_turned = jnp.dot(texts, order, preferred_element_type=F32).astype(BF16)

    shaped = (257, 10, HEAD_DIM)
    queries, key_heads, value_heads = (
        t.reshape(shaped) for t in (query_tokens, key_tokens, value_tokens)
    )
    raw_scores = (
        jnp.einsum("ihd,jhd->hij", queries, key_heads, preferred_element_type=F32) * INV_ROOT
    )
    attn_probs = jax.nn.softmax(raw_scores, axis=-1)
    probs_low = attn_probs.astype(BF16)
    column_mass = jnp.sum(probs_low, axis=1, dtype=F32)
    pooled = jnp.sum(column_mass.T[:, :, None] * value_heads.astype(F32), axis=0) / 257.0
    pooled = pooled.reshape(1, WIDTH).astype(BF16)

    pooled_all = spread(pooled, "x", 4).reshape(4, WIDTH)
    partial_cols = contract(pooled_all, weight_t, ((1,), (1,)))
    cached, cached_norm = unit_rows(image_cache.astype(F32))
    image_message = jnp.concatenate(
        [
            cached.astype(BF16),
            label_tail(image_group),
            jnp.concatenate(halves(partial_cols), axis=0),
        ],
        axis=1,
    )
    image_got = spread(image_message, IMAGE_AXES, 16)
    images = image_got[:, :, :EMBED].reshape(128, EMBED)
    igroup_of = label_of(image_got[:, :, EMBED : EMBED + TAIL].reshape(128, TAIL), 0)
    fresh_got = image_got[:, :, EMBED + TAIL :].astype(F32)
    fresh_got = (fresh_got[:, :4] + fresh_got[:, 4:]).reshape(4, 4, 4, 256)
    fresh = jnp.sum(fresh_got, axis=1).transpose(1, 0, 2).reshape(4, EMBED)
    fresh_unit, fresh_norm = unit_rows(fresh)
    fresh_low = fresh_unit.astype(BF16)

    spots = jnp.arange(128)
    image_index = (z * 16 + spots // 32 * 4 + h * 2 + c) * 32 + spots % 32
    is_fresh = (spots % 32 == 0)[:, None]
    scores = contract(images, texts, ((1,), (1,)))
    fresh_scores = contract(fresh_low, texts_turned, ((1,), (1,)))
    scores = jnp.where(is_fresh, jnp.repeat(fresh_scores, 32, axis=0), scores)
    logits = temper * scores + logit_bias
    labels = (pair_of[None, :] == image_index[:, None]) | (igroup_of[:, None] == tgroup_of[None, :])
    signed = jnp.where(labels, 1.0, -1.0).astype(F32)
    margin = signed * logits
    losses = -jnp.sum(jax.nn.log_sigmoid(margin), axis=1, keepdims=True)
    coeffs = (temper * (-signed * jax.nn.sigmoid(-margin))).astype(BF16)
    image_part = jnp.dot(coeffs, texts, preferred_element_type=F32)
    fresh_part = jnp.dot(coeffs[::32], texts_turned, preferred_element_type=F32)
    dot_part = jnp.sum(fresh_part * fresh_unit, axis=1, keepdims=True)

    dot_high, dot_low = halves(dot_part)
    dots = jnp.pad(jnp.concatenate([dot_high, dot_low], axis=1), ((0, 4), (0, 0)))
    losses_high, losses_low = halves(losses)
    back = jnp.concatenate(
        [
            image_part.astype(BF16).reshape(16, 8, EMBED),
            losses_high.reshape(16, 8, 1),
            losses_low.reshape(16, 8, 1),
            jnp.broadcast_to(dots[None], (16, 8, 2)),
            jnp.zeros((16, 8, TAIL - 4), BF16),
            jnp.repeat(
                jnp.concatenate(halves(fresh_part), axis=0).reshape(8, 4, 256).transpose(1, 0, 2),
                4,
                axis=0,
            ),
        ],
        axis=2,
    )
    back_sum = jnp.sum(lax.all_to_all(back, IMAGE_AXES, 0, 0).astype(F32), axis=0)
    image_dir = back_sum[:, :EMBED]
    row_loss = back_sum[:, EMBED] + back_sum[:, EMBED + 1]
    dots = (back_sum[:, EMBED + 2] + back_sum[:, EMBED + 3])[:4, None]
    fresh_dir = back_sum[:4, EMBED + TAIL :] + back_sum[4:, EMBED + TAIL :]
    unit_cols = lax.dynamic_slice(fresh_unit, (0, x * 256), (4, 256))
    fresh_grad = ((fresh_dir - unit_cols * dots) * fresh_norm).astype(BF16)
    pooled_part = jnp.dot(fresh_grad, weight_t, preferred_element_type=F32)
    pooled_grad = jnp.sum(lax.all_to_all(pooled_part[:, None], "x", 0, 0), axis=0)

    fresh_plain = lax.dot_general(
        fresh_unit,
        order.astype(F32),
        (((1,), (1,)), ((), ())),
        precision=lax.Precision.HIGHEST,
        preferred_element_type=F32,
    )
    image_rows = jnp.where(is_fresh, jnp.repeat(fresh_plain.astype(BF16), 32, axis=0), images)
    text_part = contract(coeffs, image_rows, ((0,), (0,)))
    text_part = text_part[:128] + lax.ppermute(text_part[128:], "c", SWAP)
    text_part = text_part.astype(BF16).reshape(16, 8, EMBED)
    text_dir = jnp.sum(lax.all_to_all(text_part, TEXT_AXES, 0, 0).astype(F32), axis=0)

    own_fresh = ((jnp.arange(8) == 0) & (m == 0))[:, None]
    unit_image = jnp.where(own_fresh, lax.dynamic_slice(fresh_plain, (x, 0), (1, EMBED)), cached)
    image_norm = jnp.where(own_fresh, lax.dynamic_slice(fresh_norm, (x, 0), (1, 1)), cached_norm)
    image_grad = (
        image_dir - unit_image * jnp.sum(unit_image * image_dir, axis=1, keepdims=True)
    ) * image_norm
    text_grad = (
        text_dir - unit_text * jnp.sum(unit_text * text_dir, axis=1, keepdims=True)
    ) * text_norm

    cotangent = (pooled_grad * (LOSS_SCALE / 257)).astype(BF16).reshape(10, HEAD_DIM)
    prob_grad = jnp.einsum("hd,jhd->hj", cotangent, value_heads, preferred_element_type=F32)
    centre = jnp.sum(attn_probs * prob_grad[:, None, :], axis=-1, keepdims=True)
    score_grad = (attn_probs * (prob_grad[:, None, :] - centre)).astype(BF16)
    query_grad = (
        jnp.einsum("hij,jhd->ihd", score_grad, key_heads, preferred_element_type=F32) * INV_ROOT
    )
    key_grad = (
        jnp.einsum("hij,ihd->jhd", score_grad, queries, preferred_element_type=F32) * INV_ROOT
    )
    value_grad = jnp.einsum("hj,hd->jhd", column_mass, cotangent.astype(F32))
    out_shape = (1, 257, WIDTH)
    return (
        query_grad.reshape(out_shape).astype(BF16),
        key_grad.reshape(out_shape).astype(BF16),
        value_grad.reshape(out_shape).astype(BF16),
        image_grad,
        text_grad,
        row_loss,
    )


def solution(mesh):
    fine = Mesh(mesh.devices.reshape(8, 4, 2, 2, 4), ("z", "x", "h", "c", "m"))
    dp, pairs = ("z", "x", "h", "c"), ("z", "x", "h", "c", "m")
    tokens = P(dp, None, "m")
    return jax.shard_map(
        on_device,
        mesh=fine,
        in_specs=(
            tokens,
            tokens,
            tokens,
            P("m", dp),
            P(pairs, None),
            P(pairs, None),
            P(pairs),
            P(pairs),
            P(pairs),
            P(),
            P(),
        ),
        out_specs=(tokens, tokens, tokens, P(pairs, None), P(pairs, None), P(pairs)),
        check_vma=False,
    )
```

time: 196 us -> 146 us (0.74)
  the two profiles are of different devices: /device:TPU:16 before, /device:TPU:32 now
where the time goes in v2:
time: 146 us; the launch traced here: 145 us
  starting transfers between devices  47.9 us (33%)
  waiting for transfers between devices  33.3 us (23%)
  other arithmetic  24.5 us (17%)
  local copies, waits for them, and re-layouts  21.4 us (15%)
  matrix products  15.1 us (10%)
  between operations  2.55 us (2%)
    all_to_all x3, starting transfers between devices, spread(): return lax.all_to_all(sent, axes, 0, 0)  26.8 us
    all_to_all x3, waiting for transfers between devices, spread(): return lax.all_to_all(sent, axes, 0, 0)  20 us
    all_to_all x1, starting transfers between devices, on_device(): lax.all_to_all(text_part, TEXT_AXES, 0, 0).astype(F32)  9.7 us
    all_to_all x1, waiting for transfers between devices, on_device(): lax.all_to_all(back, IMAGE_AXES, 0, 0).astype(F32)  8.87 us
    all_to_all x1, waiting for transfers between devices, on_device(): lax.all_to_all(pooled_part[:, None], 'x', 0, 0)  4.44 us
    all_to_all x1, starting transfers between devices, on_device(): lax.all_to_all(back, IMAGE_AXES, 0, 0).astype(F32)  4.34 us
    unnamed x54, local copies, waits for them, and re-layouts  3.84 us
    dot_general x1, matrix products, on_device(): jnp.einsum('hij,jhd->ihd', score_grad, key_heads, preferred_element_type=...  3.75 us
  transfers between devices with their start and end apart: 8, of which 5 were waited for; matrix products, arithmetic and copies ran while one was open for 27% of the time, Pallas kernels for 0%

profile of v2, /device:TPU:32, one launch (start us, length us, event | category | flops | bytes accessed | tf_op | source)
XLA Modules:
  0.0 144.8 jit_solution(16755315341580262227)
XLA Ops:
  0.7 0.8 convert_bitcast_fusion.2
  1.4 0.7 convert_bitcast_fusion
  2.2 0.8 fusion.63
  3.1 0.8 fusion.50
  3.9 0.7 fusion.54
  4.6 0.9 broadcast_in_dim.67
  5.5 15.7 %all-to-all-start = ((bf16[16,8,2432]{2,1,0:T(8,128)(2,1)}), bf16[16,8,2432]{2,1,0:T(8,128)(2,1)}, u32[]{:S(2)}, u32[]{:S(2)}) async-start(bf16[16,8,2432]{2,1,0:T(8,128)(2,1)} %broadcast_in_dim.67), calls=%async_computation | async-start | bytes 1245184 | tf_op jit(solution)/shard_map/all_to_all | solution.py:24
  22.0 0.9 fusion.26
  23.0 3.0 %fusion.129 = (f32[10,257]{1,0:T(8,128)S(1)}, f32[10,257,257]{1,2,0:T(8,128)S(1)}) fusion(f32[10,257,257]{1,2,0:T(8,128)S(1)} %fusion.26), kind=kOutput, calls=%fused_computation.240 | output fusion | flops 2642216 | bytes 5294200 | tf_op jit(solution)/shard_map/sub | solution.py:100
  26.0 0.6 convert_reduce_fusion
  26.6 1.3 copy-done
  27.9 0.6 copy-done.14
  28.6 0.6 mul.248
  29.5 1.3 multiply_reduce_fusion.2
  31.4 0.7 reduce.13
  32.1 0.6 reshape.424
  32.8 6.9 %all-to-all-done = bf16[16,8,2432]{2,1,0:T(8,128)(2,1)} async-done(((bf16[16,8,2432]{2,1,0:T(8,128)(2,1)}), bf16[16,8,2432]{2,1,0:T(8,128)(2,1)}, u32[]{:S(2)}, u32[]{:S(2)}) %all-to-all-start) | async-done | bytes 622624 | tf_op jit(solution)/shard_map/all_to_all | solution.py:24
  39.8 4.3 %all-to-all-start.1 = ((bf16[4,2,640]{2,1,0:T(2,128)(2,1)}), bf16[4,2,640]{2,1,0:T(2,128)(2,1)S(1)}, u32[]{:S(2)}, u32[]{:S(2)}) async-start(bf16[4,2,640]{2,1,0:T(2,128)(2,1)} %reshape.424), calls=%async_computation.1 | async-start | bytes 20480 | tf_op jit(solution)/shard_map/all_to_all | solution.py:24
  44.1 1.9 %collective-permute-start = (bf16[16,8,2432]{2,1,0:T(8,128)(2,1)}, bf16[16,8,2432]{2,1,0:T(8,128)(2,1)S(1)}, u32[]{:S(2)}, u32[]{:S(2)}) collective-permute-start(bf16[16,8,2432]{2,1,0:T(8,128)(2,1)} %all-to-all-done), channel_id=1, source_target_pairs={{0,4},{4,0},{1,5},{5,1},{2,6},{6,2},{3,7},{7,3},{8,12},{12,8},{9,1... | collective-permute-start | bytes 1867784 | tf_op jit(solution)/shard_map/ppermute | solution.py:75
  48.1 1.3 all-to-all-done.1
  49.4 1.2 maximum_bitcast_fusion
  51.0 0.8 broadcast_in_dim.72
  51.7 6.8 %all-to-all-start.2 = ((bf16[16,8,1408]{2,1,0:T(8,128)(2,1)}), bf16[16,8,1408]{2,1,0:T(8,128)(2,1)S(1)}, u32[]{:S(2)}, u32[]{:S(2)}) async-start(bf16[16,8,1408]{2,1,0:T(8,128)(2,1)} %broadcast_in_dim.72), calls=%async_computation.2 | async-start | bytes 720896 | tf_op jit(solution)/shard_map/all_to_all | solution.py:24
  59.4 1.0 fusion.11
  60.4 11.8 %all-to-all-done.2 = bf16[16,8,1408]{2,1,0:T(8,128)(2,1)S(1)} async-done(((bf16[16,8,1408]{2,1,0:T(8,128)(2,1)}), bf16[16,8,1408]{2,1,0:T(8,128)(2,1)S(1)}, u32[]{:S(2)}, u32[]{:S(2)}) %all-to-all-start.2) | async-done | bytes 360480 | tf_op jit(solution)/shard_map/all_to_all | solution.py:24
  72.4 0.5 copy-done.21
  73.0 2.5 %fusion.130 = (bf16[4,1024]{1,0:T(4,128)(2,1)S(1)}, f32[4,1024]{1,0:T(4,128)}) fusion(f32[4,1024]{1,0:T(4,128)S(1)} %broadcast_multiply_fusion, s32[1024]{0:T(1024)S(1)} %fusion.91), kind=kOutput, calls=%fused_computation.241 | convolution fusion | flops 51384320 | bytes 45056 | tf_op jit(solution)/shard_map/dot_general | solution.py:170
  76.0 1.0 fusion.37
  77.0 0.9 subtract_convert_fusion
  77.9 0.9 fusion.14
  78.9 0.7 bitcast_select_fusion
  79.9 0.8 slice.124
  80.7 1.9 %collective-permute-start.1 = (f32[128,1024]{1,0:T(8,128)}, f32[128,1024]{1,0:T(8,128)}, u32[]{:S(2)}, u32[]{:S(2)}) collective-permute-start(f32[128,1024]{1,0:T(8,128)} %slice.124), channel_id=1, source_target_pairs={{0,4},{4,0},{1,5},{5,1},{2,6},{6,2},{3,7},{7,3},{8,12},{12,8},{9,1... | collective-permute-start | bytes 1572872 | tf_op jit(solution)/shard_map/ppermute | solution.py:179
  82.8 0.7 reduce_sum.147
  83.6 0.8 copy.80
  84.4 0.8 copy.81
  85.1 0.7 pad_maximum_fusion
  85.8 0.6 broadcast_in_dim.120
  86.5 0.6 broadcast_in_dim.121
  87.1 1.8 %concatenate.27 = bf16[16,8,1408]{2,1,0:T(8,128)(2,1)} concatenate(bf16[16,8,1024]{2,1,0:T(8,128)(2,1)} %fusion.14, bf16[16,8,1]{2,1,0:T(8,128)(2,1)} %copy.80, bf16[16,8,1]{2,1,0:T(8,128)(2,1)} %copy.81, bf16[16,8,2]{2,1,0:T(8,128)(2,1)} %broadcast_in_dim.120, bf16[16,8,124]{2,1,0:T(8,128)(2,1)} %broadcast_in_dim.121, bf16[16,8,256]{2,1,0:T(8,128)(2,1)S(1)} %bitcast.84), dimensions={2} | concatenate | bytes 720896 | tf_op jit(solution)/shard_map/concatenate | solution.py:145
  88.9 4.3 %all-to-all-start.3 = ((bf16[16,8,1408]{2,1,0:T(8,128)(2,1)}), bf16[16,8,1408]{2,1,0:T(8,128)(2,1)}, u32[]{:S(2)}, u32[]{:S(2)}) async-start(bf16[16,8,1408]{2,1,0:T(8,128)(2,1)} %concatenate.27), calls=%async_computation.3 | async-start | bytes 720896 | tf_op jit(solution)/shard_map/all_to_all | solution.py:160
  93.3 1.2 dynamic-slice.3
  94.5 0.7 constant_dynamic-slice_fusion
  95.2 1.3 broadcast_select_fusion
  96.5 1.8 %fusion.33 = bf16[16,8,1024]{2,1,0:T(8,128)(2,1)} fusion(f32[128,1024]{1,0:T(8,128)} %collective-permute-done.1, f32[256,1024]{1,0:T(8,128)S(1)} %fusion.131), kind=kLoop, calls=%fused_computation.50 | loop fusion | flops 262144 | bytes 1310720 | tf_op jit(solution)/shard_map/reshape | solution.py:180
  98.3 8.9 %all-to-all-done.3 = bf16[16,8,1408]{2,1,0:T(8,128)(2,1)} async-done(((bf16[16,8,1408]{2,1,0:T(8,128)(2,1)}), bf16[16,8,1408]{2,1,0:T(8,128)(2,1)}, u32[]{:S(2)}, u32[]{:S(2)}) %all-to-all-start.3) | async-done | bytes 360480 | tf_op jit(solution)/shard_map/all_to_all | solution.py:160
  107.2 1.0 convert_reduce_fusion.1
  108.2 0.7 fusion.105
  109.1 0.9 convolution_bitcast_fusion
  110.0 0.6 copy.82
  110.6 3.3 %all-to-all-start.4 = ((f32[4,1,1280]{2,1,0:T(1,128)}), f32[4,1,1280]{2,1,0:T(1,128)S(1)}, u32[]{:S(2)}, u32[]{:S(2)}) async-start(f32[4,1,1280]{2,1,0:T(1,128)} %copy.82), calls=%async_computation.4 | async-start | bytes 40960 | tf_op jit(solution)/shard_map/all_to_all | solution.py:168
  114.1 0.7 fusion.59
  114.8 4.4 %all-to-all-done.4 = f32[4,1,1280]{2,1,0:T(1,128)S(1)} async-done(((f32[4,1,1280]{2,1,0:T(1,128)}), f32[4,1,1280]{2,1,0:T(1,128)S(1)}, u32[]{:S(2)}, u32[]{:S(2)}) %all-to-all-start.4) | async-done | bytes 20512 | tf_op jit(solution)/shard_map/all_to_all | solution.py:168
  119.2 9.7 %all-to-all-start.5 = ((bf16[16,8,1024]{2,1,0:T(8,128)(2,1)}), bf16[16,8,1024]{2,1,0:T(8,128)(2,1)S(1)}, u32[]{:S(2)}, u32[]{:S(2)}) async-start(bf16[16,8,1024]{2,1,0:T(8,128)(2,1)} %fusion.33), calls=%async_computation.5 | async-start | bytes 524288 | tf_op jit(solution)/shard_map/all_to_all | solution.py:181
  129.0 0.6 bitcast_convert_fusion
  129.6 0.6 fusion.18
  130.2 1.2 convert_element_type.311
  131.4 1.0 fusion.19
  132.4 2.9 %multiply_reduce_fusion = f32[10,257]{1,0:T(8,128)S(1)} fusion(f32[10,257]{1,0:T(8,128)S(1)} %bitcast.88, f32[10,257,257]{1,2,0:T(8,128)} %copy-done, f32[10,257]{1,0:T(8,128)} %copy-done.12), kind=kLoop, calls=%fused_computation.5 | loop fusion | flops 1978900 | bytes 2672800 | tf_op jit(solution)/shard_map/reduce_sum | solution.py:195
  135.8 1.4 fusion.12
  137.4 1.2 convert_element_type.308
  138.7 3.7 %fusion.13 = bf16[257,10,128]{2,0,1:T(8,128)(2,1)S(1)} fusion(f32[10,257]{1,0:T(8,128)S(1)} %multiply_reduce_fusion, f32[10,257]{1,0:T(8,128)S(1)} %bitcast.90, bf16[257,10,128]{2,1,0:T(8,128)(2,1)S(1)} %copy-done.3, f32[10,257,257]{1,2,0:T(8,128)} %copy-done, f32[10,257]{1,0:T(8,128)S(1)} %copy-done.13), kind=kOutput, calls=%fused_computation.23 | convolution fusion | flops 172385312 | bytes 3988640 | tf_op jit(solution)/shard_map/hij,jhd->ihd/dot_general | solution.py:198
  142.6 1.2 convert_element_type.305
  144.1 0.7 fusion.62
  (103 shorter events, 6.5 us)
Async XLA Ops:
  0.6 20.5 %copy-start.7 = (bf16[1,257,1280]{2,1,0:T(8,128)(2,1)S(1)}, bf16[1,257,1280]{2,1,0:T(8,128)(2,1)}, u32[]{:S(2)}) copy-start(bf16[1,257,1280]{2,1,0:T(8,128)(2,1)} %param.11) | copy-start | bytes 1973764
  0.6 20.9 %copy-start.8 = (bf16[1,257,1280]{2,1,0:T(8,128)(2,1)S(1)}, bf16[1,257,1280]{2,1,0:T(8,128)(2,1)}, u32[]{:S(2)}) copy-start(bf16[1,257,1280]{2,1,0:T(8,128)(2,1)} %param.12) | copy-start | bytes 1973764
  3.1 0.8 copy-start.19
  5.5 34.3 %all-to-all-start = ((bf16[16,8,2432]{2,1,0:T(8,128)(2,1)}), bf16[16,8,2432]{2,1,0:T(8,128)(2,1)}, u32[]{:S(2)}, u32[]{:S(2)}) async-start(bf16[16,8,2432]{2,1,0:T(8,128)(2,1)} %broadcast_in_dim.67), calls=%async_computation | async-start | bytes 1245184 | tf_op jit(solution)/shard_map/all_to_all | solution.py:24
  21.6 1.3 copy-start.4
  22.0 1.0 copy-start.2
  26.0 1.9 %copy-start = (f32[10,257,257]{1,2,0:T(8,128)}, f32[10,257,257]{1,2,0:T(8,128)S(1)}, u32[]{:S(2)}) copy-start(f32[10,257,257]{1,2,0:T(8,128)S(1)} %get-tuple-element.28) | copy-start | bytes 7925884
  26.0 1.9 %copy-start.12 = (f32[10,257]{1,0:T(8,128)}, f32[10,257]{1,0:T(8,128)S(1)}, u32[]{:S(2)}) copy-start(f32[10,257]{1,0:T(8,128)S(1)} %get-tuple-element.27) | copy-start | bytes 30844
  27.9 0.6 copy-start.14
  29.2 3.5 %copy-start.10 = (bf16[8,1024]{1,0:T(8,128)(2,1)S(1)}, bf16[8,1024]{1,0:T(8,128)(2,1)}, u32[]{:S(2)}) copy-start(bf16[8,1024]{1,0:T(8,128)(2,1)} %param.15) | copy-start | bytes 49156
  29.5 16.7 %copy-start.15 = (f32[10,257]{1,0:T(8,128)S(1)}, f32[10,257]{1,0:T(8,128)}, u32[]{:S(2)}) copy-start(f32[10,257]{1,0:T(8,128)} %copy-done.14) | copy-start | bytes 30844
  29.5 16.8 %copy-start.6 = (bf16[1,257,1280]{2,1,0:T(8,128)(2,1)S(1)}, bf16[1,257,1280]{2,1,0:T(8,128)(2,1)}, u32[]{:S(2)}) copy-start(bf16[1,257,1280]{2,1,0:T(8,128)(2,1)} %param.13) | copy-start | bytes 1973764
  32.8 13.2 %copy-start.22 = (f32[8]{0:T(128)}, f32[8]{0:T(128)S(1)}, u32[]{:S(2)}) copy-start(f32[8]{0:T(128)S(1)} %fusion.64) | copy-start | bytes 100
  39.8 9.6 %all-to-all-start.1 = ((bf16[4,2,640]{2,1,0:T(2,128)(2,1)}), bf16[4,2,640]{2,1,0:T(2,128)(2,1)S(1)}, u32[]{:S(2)}, u32[]{:S(2)}) async-start(bf16[4,2,640]{2,1,0:T(2,128)(2,1)} %reshape.424), calls=%async_computation.1 | async-start | bytes 20480 | tf_op jit(solution)/shard_map/all_to_all | solution.py:24
  44.1 5.3 %collective-permute-start = (bf16[16,8,2432]{2,1,0:T(8,128)(2,1)}, bf16[16,8,2432]{2,1,0:T(8,128)(2,1)S(1)}, u32[]{:S(2)}, u32[]{:S(2)}) collective-permute-start(bf16[16,8,2432]{2,1,0:T(8,128)(2,1)} %all-to-all-done), channel_id=1, source_target_pairs={{0,4},{4,0},{1,5},{5,1},{2,6},{6,2},{3,7},{7,3},{8,12},{12,8},{9,1... | collective-permute-start | bytes 1867784 | tf_op jit(solution)/shard_map/ppermute | solution.py:75
  46.0 30.0 %copy-start.23 = (pred[128]{0:T(512)(128)(4,1)}, pred[128]{0:T(512)(128)(4,1)S(1)}, u32[]{:S(2)}) copy-start(pred[128]{0:T(512)(128)(4,1)S(1)} %broadcast_compare_fusion) | copy-start | bytes 388
  46.0 2.1 %copy-start.17 = (f32[8]{0:T(128)}, f32[8]{0:T(128)S(1)}, u32[]{:S(2)}) copy-start(f32[8]{0:T(128)S(1)} %add_rsqrt_fusion.1) | copy-start | bytes 100
  51.7 20.4 %all-to-all-start.2 = ((bf16[16,8,1408]{2,1,0:T(8,128)(2,1)}), bf16[16,8,1408]{2,1,0:T(8,128)(2,1)S(1)}, u32[]{:S(2)}, u32[]{:S(2)}) async-start(bf16[16,8,1408]{2,1,0:T(8,128)(2,1)} %broadcast_in_dim.72), calls=%async_computation.2 | async-start | bytes 720896 | tf_op jit(solution)/shard_map/all_to_all | solution.py:24
  72.2 3.8 %copy-start.24 = (s32[128]{0:T(128)S(1)}, s32[128]{0:T(128)}, u32[]{:S(2)}) copy-start(s32[128]{0:T(128)} %fusion.119) | copy-start | bytes 1540
  72.4 0.5 copy-start.21
  73.0 4.1 %copy-start.16 = (f32[4,1024]{1,0:T(4,128)}, f32[4,1024]{1,0:T(4,128)S(1)}, u32[]{:S(2)}) copy-start(f32[4,1024]{1,0:T(4,128)S(1)} %broadcast_multiply_fusion) | copy-start | bytes 49156
  80.7 15.8 %collective-permute-start.1 = (f32[128,1024]{1,0:T(8,128)}, f32[128,1024]{1,0:T(8,128)}, u32[]{:S(2)}, u32[]{:S(2)}) collective-permute-start(f32[128,1024]{1,0:T(8,128)} %slice.124), channel_id=1, source_target_pairs={{0,4},{4,0},{1,5},{5,1},{2,6},{6,2},{3,7},{7,3},{8,12},{12,8},{9,1... | collective-permute-start | bytes 1572872 | tf_op jit(solution)/shard_map/ppermute | solution.py:179
  87.1 26.8 %copy-start.18 = (f32[8]{0:T(128)S(1)}, f32[8]{0:T(128)}, u32[]{:S(2)}) copy-start(f32[8]{0:T(128)} %copy-done.17) | copy-start | bytes 100
  88.9 25.0 %copy-start.11 = (bf16[8,1024]{1,0:T(8,128)(2,1)S(1)}, bf16[8,1024]{1,0:T(8,128)(2,1)}, u32[]{:S(2)}) copy-start(bf16[8,1024]{1,0:T(8,128)(2,1)} %param.15) | copy-start | bytes 49156
  88.9 18.3 %all-to-all-start.3 = ((bf16[16,8,1408]{2,1,0:T(8,128)(2,1)}), bf16[16,8,1408]{2,1,0:T(8,128)(2,1)}, u32[]{:S(2)}, u32[]{:S(2)}) async-start(bf16[16,8,1408]{2,1,0:T(8,128)(2,1)} %concatenate.27), calls=%async_computation.3 | async-start | bytes 720896 | tf_op jit(solution)/shard_map/all_to_all | solution.py:160
  110.6 8.6 %all-to-all-start.4 = ((f32[4,1,1280]{2,1,0:T(1,128)}), f32[4,1,1280]{2,1,0:T(1,128)S(1)}, u32[]{:S(2)}, u32[]{:S(2)}) async-start(f32[4,1,1280]{2,1,0:T(1,128)} %copy.82), calls=%async_computation.4 | async-start | bytes 40960 | tf_op jit(solution)/shard_map/all_to_all | solution.py:168
  119.2 24.6 %all-to-all-start.5 = ((bf16[16,8,1024]{2,1,0:T(8,128)(2,1)}), bf16[16,8,1024]{2,1,0:T(8,128)(2,1)S(1)}, u32[]{:S(2)}, u32[]{:S(2)}) async-start(bf16[16,8,1024]{2,1,0:T(8,128)(2,1)} %fusion.33), calls=%async_computation.5 | async-start | bytes 524288 | tf_op jit(solution)/shard_map/all_to_all | solution.py:181
  130.2 5.2 %copy-start.5 = (bf16[257,10,128]{2,1,0:T(8,128)(2,1)S(1)}, bf16[257,10,128]{2,1,0:T(8,128)(2,1)}, u32[]{:S(2)}) copy-start(bf16[257,10,128]{2,1,0:T(8,128)(2,1)} %copy-done.4) | copy-start | bytes 1973764
  132.4 3.4 %copy-start.1 = (f32[10,257,257]{1,2,0:T(8,128)S(1)}, f32[10,257,257]{1,2,0:T(8,128)}, u32[]{:S(2)}) copy-start(f32[10,257,257]{1,2,0:T(8,128)} %copy-done) | copy-start | bytes 7925884
  132.4 3.4 %copy-start.13 = (f32[10,257]{1,0:T(8,128)S(1)}, f32[10,257]{1,0:T(8,128)}, u32[]{:S(2)}) copy-start(f32[10,257]{1,0:T(8,128)} %copy-done.12) | copy-start | bytes 30844
  137.2 1.4 copy-start.3
  142.4 1.5 %copy-start.9 = (bf16[8,1024]{1,0:T(8,128)(2,1)S(1)}, bf16[8,1024]{1,0:T(8,128)(2,1)}, u32[]{:S(2)}) copy-start(bf16[8,1024]{1,0:T(8,128)(2,1)} %param.16) | copy-start | bytes 49156
  142.4 1.5 %copy-start.20 = (f32[8]{0:T(128)S(1)}, f32[8]{0:T(128)}, u32[]{:S(2)}) copy-start(f32[8]{0:T(128)} %copy-done.19) | copy-start | bytes 100

commit v3 on v2

v3 whole, which is shorter than its diff:
```python
import math

import jax
import jax.numpy as jnp
from jax import lax
from jax.experimental import pallas as pl
from jax.experimental.pallas import tpu as pltpu
from jax.sharding import Mesh
from jax.sharding import PartitionSpec as P

SEQ = 257
HEADS = 10
HEAD_DIM = 128
LOSS_SCALE = 8192.0
EMBED = 1024
WIDTH = 1280
TAIL = 128
STEM = EMBED + TAIL
INV_ROOT = 1.0 / math.sqrt(HEAD_DIM)
PAIRED = 2

TEXT_AXES = ("z", "h")
IMAGE_AXES = ("x", "m")
SWAP = [(0, 1), (1, 0)]
BF16, F32 = jnp.bfloat16, jnp.float32

VMEM = pl.BlockSpec(memory_space=pltpu.VMEM)
SMEM = pl.BlockSpec(memory_space=pltpu.SMEM)
PARAMS = pltpu.CompilerParams(vmem_limit_bytes=24 * 2**20)


def spread(block, axes, count):
    sent = jnp.broadcast_to(block[None], (count,) + block.shape)
    return lax.all_to_all(sent, axes, 0, 0)


def halves(value):
    high = value.astype(BF16)
    return high, (value - high.astype(F32)).astype(BF16)


def unit_rows(raw_rows):
    row_norm = lax.rsqrt(jnp.sum(raw_rows * raw_rows, axis=1, keepdims=True) + 1e-06)
    return raw_rows * row_norm, row_norm


def contract(left, right, dims):
    return lax.dot_general(left, right, (dims, ((), ())), preferred_element_type=F32)


def lanes(shape):
    return lax.broadcasted_iota(jnp.int32, shape, 1)


def rows(shape):
    return lax.broadcasted_iota(jnp.int32, shape, 0)


def both(value):
    return value + pltpu.roll(value, 4, 0)


def block_sum(value):
    value = value.astype(F32)
    total = value[0:8]
    for i in range(1, 16):
        total += value[i * 8 : i * 8 + 8]
    return total


def attend_kernel(q_ref, k_ref, v_ref, probs_ref, mass_ref, pooled_ref):
    ones = jnp.ones((SEQ, HEAD_DIM), BF16)
    for one in range(PAIRED):
        at = slice(one * HEAD_DIM, (one + 1) * HEAD_DIM)
        scores = contract(q_ref[0, :, at], k_ref[0, :, at], ((1,), (1,))) * INV_ROOT
        raised = jnp.exp(scores - jnp.max(scores, axis=1, keepdims=True))
        probs = raised / jnp.sum(raised, axis=1, keepdims=True)
        probs_ref[one] = probs
        mass = contract(probs.astype(BF16), ones, ((0,), (0,)))
        mass_ref[:, at] = mass
        pooled = jnp.sum(mass * v_ref[0, :, at].astype(F32), axis=0, keepdims=True)
        pooled_ref[:, at] = (pooled * (1.0 / SEQ)).astype(BF16)


def attend(query_tokens, key_tokens, value_tokens):
    wide = PAIRED * HEAD_DIM
    tokens = pl.BlockSpec((1, SEQ, wide), lambda i: (0, 0, i))
    return pl.pallas_call(
        attend_kernel,
        grid=(HEADS // PAIRED,),
        in_specs=[tokens] * 3,
        out_specs=[
            pl.BlockSpec((PAIRED, SEQ, SEQ), lambda i: (i, 0, 0)),
            pl.BlockSpec((SEQ, wide), lambda i: (0, i)),
            pl.BlockSpec((1, wide), lambda i: (0, i)),
        ],
        out_shape=[
            jax.ShapeDtypeStruct((HEADS, SEQ, SEQ), F32),
            jax.ShapeDtypeStruct((SEQ, WIDTH), F32),
            jax.ShapeDtypeStruct((1, WIDTH), BF16),
        ],
        compiler_params=PARAMS,
        name="attend",
    )(query_tokens, key_tokens, value_tokens)


def attend_back_kernel(z_ref, q_ref, k_ref, v_ref, probs_ref, mass_ref, dq_ref, dk_ref, dv_ref):
    cot = (jnp.sum(z_ref[...], axis=0) * (LOSS_SCALE / SEQ)).astype(BF16)
    for one in range(PAIRED):
        at = slice(one * HEAD_DIM, (one + 1) * HEAD_DIM)
        cot_row = cot[:, at]
        probs = probs_ref[one]
        cot_rows = jnp.broadcast_to(cot_row, (8, HEAD_DIM))
        prob_grad = contract(cot_rows, v_ref[0, :, at], ((1,), (1,)))[:1]
        centre = jnp.sum(probs * prob_grad, axis=1, keepdims=True)
        score_grad = (probs * (prob_grad - centre)).astype(BF16)
        dq_ref[0, :, at] = (contract(score_grad, k_ref[0, :, at], ((1,), (0,))) * INV_ROOT).astype(
            BF16
        )
        dk_ref[0, :, at] = (contract(score_grad, q_ref[0, :, at], ((0,), (0,))) * INV_ROOT).astype(
            BF16
        )
        dv_ref[0, :, at] = (mass_ref[:, at] * cot_row.astype(F32)).astype(BF16)


def attend_back(parts, query_tokens, key_tokens, value_tokens, probs, mass):
    wide = PAIRED * HEAD_DIM
    tokens = pl.BlockSpec((1, SEQ, wide), lambda i: (0, 0, i))
    return pl.pallas_call(
        attend_back_kernel,
        grid=(HEADS // PAIRED,),
        in_specs=[
            pl.BlockSpec((4, 1, wide), lambda i: (0, 0, i)),
            tokens,
            tokens,
            tokens,
            pl.BlockSpec((PAIRED, SEQ, SEQ), lambda i: (i, 0, 0)),
            pl.BlockSpec((SEQ, wide), lambda i: (0, i)),
        ],
        out_specs=[tokens] * 3,
        out_shape=[jax.ShapeDtypeStruct((1, SEQ, WIDTH), BF16)] * 3,
        compiler_params=PARAMS,
        name="attend_back",
    )(parts, query_tokens, key_tokens, value_tokens, probs, mass)


def pair_kernel(
    place_ref,
    scalar_ref,
    got_ref,
    near_ref,
    far_ref,
    turned_ref,
    back_ref,
    coeff_ref,
    unit_ref,
    norm_ref,
):
    z, h, c = place_ref[0], place_ref[2], place_ref[3]
    temper = jnp.exp(jnp.full((1, 128), scalar_ref[0], F32))
    offset = scalar_ref[1]

    columns = got_ref[:, STEM:].astype(F32)
    fresh = []
    for x in range(4):
        total = columns[x * 32 : x * 32 + 8]
        for m in range(1, 4):
            total += columns[x * 32 + m * 8 : x * 32 + m * 8 + 8]
        fresh.append(both(total))
    fresh = jnp.concatenate(fresh, axis=1)
    fresh_unit, fresh_norm = unit_rows(fresh)
    fresh_low = fresh_unit.astype(BF16)
    unit_ref[...] = fresh_unit
    norm_ref[...] = jnp.broadcast_to(fresh_norm, (8, 128))

    images = got_ref[:, :EMBED]
    image_tail = got_ref[:, EMBED:STEM].astype(F32)
    image_group = image_tail[:, 0:1] * 64.0 + image_tail[:, 1:2]
    spot = rows((128, 1))
    image_index = ((z * 16 + spot // 32 * 4 + h * 2 + c) * 32 + spot % 32).astype(F32)
    square = (128, 128)
    is_fresh = rows(square) % 32 == 0
    chosen = (lanes((8, 128)) == 32 * (rows((8, 128)) % 4)).astype(BF16)

    image_part = jnp.zeros((128, EMBED), F32)
    fresh_part = jnp.zeros((8, EMBED), F32)
    losses = jnp.zeros((128, 1), F32)
    for half, text_ref in enumerate((near_ref, far_ref)):
        texts = text_ref[:, :EMBED]
        turned = turned_ref[half * 128 : half * 128 + 128, :]
        text_tail = jnp.transpose(text_ref[:, EMBED:STEM].astype(F32))
        pair_of = text_tail[0:1] * 64.0 + text_tail[1:2]
        text_group = text_tail[2:3] * 64.0 + text_tail[3:4]
        scores = contract(images, texts, ((1,), (1,)))
        fresh_scores = contract(fresh_low, turned, ((1,), (1,)))
        repeated = jnp.concatenate(
            [jnp.broadcast_to(fresh_scores[i : i + 1], (32, 128)) for i in range(4)], axis=0
        )
        logits = temper * jnp.where(is_fresh, repeated, scores) + offset
        positive = (pair_of == image_index) | (image_group == text_group)
        signed = jnp.where(positive, 1.0, -1.0).astype(F32)
        margin = signed * logits
        small = jnp.exp(-jnp.abs(margin))
        losses += jnp.sum(jnp.maximum(-margin, 0.0) + jnp.log1p(small), axis=1, keepdims=True)
        share = jnp.where(margin >= 0, small, 1.0) / (1.0 + small)
        coeffs = (temper * (-signed * share)).astype(BF16)
        coeff_ref[:, half * 128 : half * 128 + 128] = coeffs
        image_part += contract(coeffs, texts, ((1,), (0,)))
        fresh_coeffs = contract(chosen, coeffs, ((1,), (0,))).astype(BF16)
        fresh_part += contract(fresh_coeffs, turned, ((1,), (0,)))

    back_ref[:, :EMBED] = image_part.astype(BF16)
    dots = jnp.sum(fresh_part * fresh_unit, axis=1, keepdims=True)
    dots = jnp.concatenate([jnp.broadcast_to(dots, (8, 128))] * 16, axis=0)
    tail = jnp.where(lanes(square) < 2, losses, dots)
    tail_high = tail.astype(BF16).astype(F32)
    back_ref[:, EMBED:STEM] = jnp.where(
        lanes(square) % 2 == 0, tail_high, tail - tail_high
    ).astype(BF16)
    part_high = fresh_part.astype(BF16).astype(F32)
    packed = jnp.where(rows((8, EMBED)) < 4, part_high, fresh_part - part_high)
    back_ref[:, STEM:] = jnp.concatenate(
        [packed[:, x * 256 : x * 256 + 256] for x in range(4) for _ in range(4)], axis=0
    ).astype(BF16)


def pair_tile(place, scalars, got, near, far, turned):
    return pl.pallas_call(
        pair_kernel,
        in_specs=[SMEM, SMEM, VMEM, VMEM, VMEM, VMEM],
        out_specs=[VMEM] * 4,
        out_shape=[
            jax.ShapeDtypeStruct((128, STEM + 256), BF16),
            jax.ShapeDtypeStruct((128, 256), BF16),
            jax.ShapeDtypeStruct((8, EMBED), F32),
            jax.ShapeDtypeStruct((8, 128), F32),
        ],
        compiler_params=PARAMS,
        name="pair_tile",
    )(place, scalars, got, near, far, turned)


def fresh_grad_kernel(place_ref, got_ref, near_ref, far_ref, unit_ref, norm_ref, out_ref):
    x = place_ref[1]
    total = block_sum(got_ref[:, EMBED:])
    dots = total[:, 2:3] + total[:, 3:4]
    fresh_dir = both(total[:, TAIL:])
    unit_cols = unit_ref[:, pl.ds(pl.multiple_of(x * 256, 256), 256)]
    grad = ((fresh_dir - unit_cols * dots) * norm_ref[:, 0:1]).astype(BF16)
    out = contract(grad[:, :128], near_ref[:, STEM:], ((1,), (0,)))
    out += contract(grad[:, 128:], far_ref[:, STEM:], ((1,), (0,)))
    for i in range(4):
        out_ref[i] = out[i : i + 1]


def fresh_back(place, got, near, far, unit, norm):
    return pl.pallas_call(
        fresh_grad_kernel,
        in_specs=[SMEM] + [VMEM] * 5,
        out_specs=VMEM,
        out_shape=jax.ShapeDtypeStruct((4, 1, WIDTH), F32),
        compiler_params=PARAMS,
        name="fresh_back",
    )(place, got, near, far, unit, norm)


def text_kernel(got_ref, coeff_ref, unit_ref, order_ref, near_ref, far_ref, plain_ref):
    unit = unit_ref[...]
    first = unit.astype(BF16)
    rest = unit - first.astype(F32)
    second = rest.astype(BF16)
    third = (rest - second.astype(F32)).astype(BF16)
    order = order_ref[...]
    plain = contract(first, order, ((1,), (1,))) + (
        contract(second, order, ((1,), (1,))) + contract(third, order, ((1,), (1,)))
    )
    plain_ref[...] = plain
    fresh_low = plain.astype(BF16).astype(F32)
    repeated = jnp.concatenate(
        [jnp.broadcast_to(fresh_low[i : i + 1], (32, EMBED)) for i in range(4)], axis=0
    )
    image_rows = jnp.where(
        rows((128, EMBED)) % 32 == 0, repeated, got_ref[:, :EMBED].astype(F32)
    ).astype(BF16)
    near_ref[...] = contract(coeff_ref[:, :128], image_rows, ((0,), (0,)))
    far_ref[...] = contract(coeff_ref[:, 128:], image_rows, ((0,), (0,)))


def text_tile(got, coeffs, unit, order):
    return pl.pallas_call(
        text_kernel,
        in_specs=[VMEM] * 4,
        out_specs=[VMEM] * 3,
        out_shape=[
            jax.ShapeDtypeStruct((128, EMBED), F32),
            jax.ShapeDtypeStruct((128, EMBED), F32),
            jax.ShapeDtypeStruct((8, EMBED), F32),
        ],
        compiler_params=PARAMS,
        name="text_tile",
    )(got, coeffs, unit, order)


def image_grad_kernel(place_ref, got_ref, cache_ref, plain_ref, norm_ref, grad_ref, loss_ref):
    x, m = place_ref[1], place_ref[4]
    total = block_sum(got_ref[:, :STEM])
    cached, cached_norm = unit_rows(cache_ref[...].astype(F32))
    own = (rows((8, 1)) == 0) & (m == 0)
    plain = jnp.zeros((1, EMBED), F32)
    plain_norm = jnp.zeros((1, 1), F32)
    for i in range(4):
        plain = jnp.where(x == i, plain_ref[i : i + 1], plain)
        plain_norm = jnp.where(x == i, norm_ref[i : i + 1, 0:1], plain_norm)
    unit = jnp.where(own, plain, cached)
    norm = jnp.where(own, plain_norm, cached_norm)
    direction = total[:, :EMBED]
    grad_ref[...] = (
        direction - unit * jnp.sum(unit * direction, axis=1, keepdims=True)
    ) * norm
    loss_ref[...] = total[:, EMBED : EMBED + 1] + total[:, EMBED + 1 : EMBED + 2]


def image_end(place, got, cache, plain, norm):
    return pl.pallas_call(
        image_grad_kernel,
        in_specs=[SMEM] + [VMEM] * 4,
        out_specs=[VMEM] * 2,
        out_shape=[
            jax.ShapeDtypeStruct((8, EMBED), F32),
            jax.ShapeDtypeStruct((8, 1), F32),
        ],
        compiler_params=PARAMS,
        name="image_end",
    )(place, got, cache, plain, norm)


def text_grad_kernel(got_ref, embed_ref, grad_ref):
    total = block_sum(got_ref[...])
    unit, norm = unit_rows(embed_ref[...].astype(F32))
    grad_ref[...] = (total - unit * jnp.sum(unit * total, axis=1, keepdims=True)) * norm


def text_end(got, embed):
    return pl.pallas_call(
        text_grad_kernel,
        in_specs=[VMEM] * 2,
        out_specs=VMEM,
        out_shape=jax.ShapeDtypeStruct((8, EMBED), F32),
        compiler_params=PARAMS,
        name="text_end",
    )(got, embed)


def label_tail(*labels):
    parts = []
    for label in labels:
        parts += [label // 64, label % 64]
    tail = jnp.stack(parts, axis=1).astype(BF16)
    return jnp.pad(tail, ((0, 0), (0, TAIL - tail.shape[1])))


def on_device(
    query_tokens,
    key_tokens,
    value_tokens,
    head_weight,
    image_cache,
    text_embed,
    text_pair,
    image_group,
    text_group,
    logit_scale,
    logit_bias,
):
    z, x, h, c, m = (lax.axis_index(a) for a in ("z", "x", "h", "c", "m"))
    place = jnp.stack([z, x, h, c, m]).astype(jnp.int32)
    scalars = jnp.stack([logit_scale, logit_bias])

    unit_text, _ = unit_rows(text_embed.astype(F32))
    text_message = jnp.concatenate(
        [unit_text.astype(BF16), label_tail(text_pair, text_group), head_weight.T], axis=1
    )
    near = spread(text_message, TEXT_AXES, 16).reshape(128, STEM + WIDTH)
    far = lax.ppermute(near, "c", SWAP)

    spot = jnp.arange(EMBED)
    column = (
        (spot % 128) // 16 * 128
        + spot // 256 * 32
        + (spot // 8) % 2 * 16
        + ((spot // 128) % 2 + c) % 2 * 8
        + spot % 8
    )
    order = (jnp.arange(EMBED)[:, None] == column[None, :]).astype(BF16)
    texts = jnp.concatenate([near[:, :EMBED], far[:, :EMBED]], axis=0)
    turned = jnp.dot(texts, order, preferred_element_type=F32).astype(BF16)

    probs, mass, pooled = attend(query_tokens, key_tokens, value_tokens)

    pooled_all = spread(pooled, "x", 4).reshape(4, WIDTH)
    partial_cols = jnp.concatenate(
        [contract(pooled_all, side[:, STEM:], ((1,), (1,))) for side in (near, far)], axis=1
    )
    cached, _ = unit_rows(image_cache.astype(F32))
    image_message = jnp.concatenate(
        [
            cached.astype(BF16),
            label_tail(image_group),
            jnp.concatenate(halves(partial_cols), axis=0),
        ],
        axis=1,
    )
    image_got = spread(image_message, IMAGE_AXES, 16).reshape(128, STEM + 256)

    back, coeffs, unit, norm = pair_tile(place, scalars, image_got, near, far, turned)
    back = lax.all_to_all(back.reshape(16, 8, STEM + 256), IMAGE_AXES, 0, 0)
    back = back.reshape(128, STEM + 256)
    pooled_part = fresh_back(place, back, near, far, unit, norm)
    pooled_part = lax.all_to_all(pooled_part, "x", 0, 0)

    text_near, text_far, plain = text_tile(image_got, coeffs, unit, order)
    text_part = (text_near + lax.ppermute(text_far, "c", SWAP)).astype(BF16)
    text_part = lax.all_to_all(text_part.reshape(16, 8, EMBED), TEXT_AXES, 0, 0)

    query_grad, key_grad, value_grad = attend_back(
        pooled_part, query_tokens, key_tokens, value_tokens, probs, mass
    )
    image_grad, row_loss = image_end(place, back, image_cache, plain, norm)
    text_grad = text_end(text_part.reshape(128, EMBED), text_embed)
    return query_grad, key_grad, value_grad, image_grad, text_grad, row_loss.reshape(8)


def solution(mesh):
    fine = Mesh(mesh.devices.reshape(8, 4, 2, 2, 4), ("z", "x", "h", "c", "m"))
    dp, pairs = ("z", "x", "h", "c"), ("z", "x", "h", "c", "m")
    tokens = P(dp, None, "m")
    return jax.shard_map(
        on_device,
        mesh=fine,
        in_specs=(
            tokens,
            tokens,
            tokens,
            P("m", dp),
            P(pairs, None),
            P(pairs, None),
            P(pairs),
            P(pairs),
            P(pairs),
            P(),
            P(),
        ),
        out_specs=(tokens, tokens, tokens, P(pairs, None), P(pairs, None), P(pairs)),
        check_vma=False,
    )
```

time: 146 us -> 122 us (0.84)
  the two profiles are of different devices: /device:TPU:32 before, /device:TPU:2 now
where the time goes in v3:
time: 122 us; the launch traced here: 121 us
  starting transfers between devices  53.6 us (44%)
  Pallas kernels  21.5 us (18%)
  waiting for transfers between devices  20 us (16%)
  local copies, waits for them, and re-layouts  14.8 us (12%)
  other arithmetic  7.69 us (6%)
  between operations  2.13 us (2%)
  matrix products  1.37 us (1%)
    all_to_all x3, starting transfers between devices, spread(): return lax.all_to_all(sent, axes, 0, 0)  32.5 us
    all_to_all x3, waiting for transfers between devices, spread(): return lax.all_to_all(sent, axes, 0, 0)  13.4 us
    unnamed x32, local copies, waits for them, and re-layouts  12.5 us
    pallas_call x1, Pallas kernels, attend(): pl.pallas_call(attend_kernel, grid=(HEADS // PAIRED,), in_specs=[tokens]...  6.74 us
    all_to_all x1, starting transfers between devices, on_device(): back = lax.all_to_all(back.reshape(16, 8, STEM + 256), IMAGE_AXES, 0, 0)  6.03 us
    all_to_all x1, starting transfers between devices, on_device(): pooled_part = lax.all_to_all(pooled_part, 'x', 0, 0)  5.9 us
    pallas_call x1, Pallas kernels, attend_back(): pl.pallas_call(attend_back_kernel, grid=(HEADS // PAIRED,), in_specs=[pl....  5.86 us
    all_to_all x1, starting transfers between devices, on_device(): text_part = lax.all_to_all(text_part.reshape(16, 8, EMBED), TEXT_AXES, 0, 0)  5.35 us
  transfers between devices with their start and end apart: 8, of which 6 were waited for; matrix products, arithmetic and copies ran while one was open for 6% of the time, Pallas kernels for 15%

profile of v3, /device:TPU:2, one launch (start us, length us, event | category | flops | bytes accessed | tf_op | source)
XLA Modules:
  0.0 121.1 jit_solution(2189760434523222065)
XLA Ops:
  0.6 0.0 copy-start.11
  0.6 0.0 copy-start.13
  0.7 0.7 convert_bitcast_fusion
  1.4 0.1 copy.25
  1.5 0.8 fusion.20
  2.3 0.8 fusion.21
  3.1 0.7 fusion.17
  3.8 0.9 broadcast_in_dim.10
  4.7 15.7 %all-to-all-start.1 = ((bf16[16,8,2432]{2,1,0:T(8,128)(2,1)}), bf16[16,8,2432]{2,1,0:T(8,128)(2,1)S(1)}, u32[]{:S(2)}, u32[]{:S(2)}) async-start(bf16[16,8,2432]{2,1,0:T(8,128)(2,1)} %broadcast_in_dim.10), calls=%async_computation.1 | async-start | bytes 1245184 | tf_op jit(solution)/shard_map/all_to_all | solution.py:34
  20.4 0.0 copy-start.2
  20.4 1.1 copy-done.2
  21.5 1.1 copy-done.4
  22.6 1.1 copy-done.6
  23.7 6.7 %attend.1 = (f32[10,257,257]{2,1,0:T(8,128)S(1)}, f32[257,1280]{1,0:T(8,128)S(1)}, bf16[1,1280]{1,0:T(2,128)(2,1)S(1)}) custom-call(bf16[1,257,1280]{2,1,0:T(8,128)(2,1)S(1)} %copy-done.2, bf16[1,257,1280]{2,1,0:T(8,128)(2,1)S(1)} %copy-done.4, bf16[1,257,1280]{2,1,0:T(8,128)(2,1)S(1)} %copy-done.6), custom_call_target="tpu_custom_call" | custom-call | tf_op jit(solution)/shard_map/attend/pallas_call | solution.py:88
  30.4 0.0 copy-start
  30.4 1.9 %copy-done = f32[10,257,257]{2,1,0:T(8,128)} copy-done((f32[10,257,257]{2,1,0:T(8,128)}, f32[10,257,257]{2,1,0:T(8,128)S(1)}, u32[]{:S(2)}) %copy-start) | copy-done | bytes 2641984
  32.3 1.1 copy-done.8
  33.5 0.5 broadcast.347
  34.0 0.7 reduce.2
  34.7 0.6 reshape.163
  35.3 0.0 copy-done.11
  35.3 0.1 fusion.18
  35.4 0.0 copy-done.13
  35.5 3.5 %all-to-all-done.1 = bf16[16,8,2432]{2,1,0:T(8,128)(2,1)S(1)} async-done(((bf16[16,8,2432]{2,1,0:T(8,128)(2,1)}), bf16[16,8,2432]{2,1,0:T(8,128)(2,1)S(1)}, u32[]{:S(2)}, u32[]{:S(2)}) %all-to-all-start.1) | async-done | bytes 622624 | tf_op jit(solution)/shard_map/all_to_all | solution.py:34
  39.0 4.8 %all-to-all-start = ((bf16[4,2,640]{2,1,0:T(2,128)(2,1)}), bf16[4,2,640]{2,1,0:T(2,128)(2,1)S(1)}, u32[]{:S(2)}, u32[]{:S(2)}) async-start(bf16[4,2,640]{2,1,0:T(2,128)(2,1)} %reshape.163), calls=%async_computation | async-start | bytes 20480 | tf_op jit(solution)/shard_map/all_to_all | solution.py:34
  43.8 1.9 %collective-permute-start = (bf16[128,2432]{1,0:T(8,128)(2,1)S(1)}, bf16[128,2432]{1,0:T(8,128)(2,1)S(1)}, u32[]{:S(2)}, u32[]{:S(2)}) collective-permute-start(bf16[128,2432]{1,0:T(8,128)(2,1)S(1)} %bitcast.34), channel_id=1, source_target_pairs={{0,4},{4,0},{1,5},{5,1},{2,6},{6,2},{3,7},{7,3},{8,12},{12,8},{9,1... | collective-permute-start | bytes 1867784 | tf_op jit(solution)/shard_map/ppermute | solution.py:384
  45.7 0.1 fusion.19
  45.8 0.1 copy.24
  45.9 1.8 %all-to-all-done = bf16[4,2,640]{2,1,0:T(2,128)(2,1)S(1)} async-done(((bf16[4,2,640]{2,1,0:T(2,128)(2,1)}), bf16[4,2,640]{2,1,0:T(2,128)(2,1)S(1)}, u32[]{:S(2)}, u32[]{:S(2)}) %all-to-all-start) | async-done | bytes 10272 | tf_op jit(solution)/shard_map/all_to_all | solution.py:34
  47.7 0.2 fusion.9
  47.9 0.0 collective-permute-done.far_ref
  47.9 0.2 fusion.7
  48.1 0.1 fusion.60
  48.2 0.8 broadcast_in_dim.11
  48.9 12.0 %all-to-all-start.2 = ((bf16[16,8,1408]{2,1,0:T(8,128)(2,1)}), bf16[16,8,1408]{2,1,0:T(8,128)(2,1)S(1)}, u32[]{:S(2)}, u32[]{:S(2)}) async-start(bf16[16,8,1408]{2,1,0:T(8,128)(2,1)} %broadcast_in_dim.11), calls=%async_computation.2 | async-start | bytes 720896 | tf_op jit(solution)/shard_map/all_to_all | solution.py:34
  62.3 0.1 stack.64.place_ref
  62.4 0.1 pad_maximum_fusion.2.scalar_ref
  62.5 1.0 fusion.3.turned_ref
  63.5 8.2 %all-to-all-done.2 = bf16[16,8,1408]{2,1,0:T(8,128)(2,1)S(1)} async-done(((bf16[16,8,1408]{2,1,0:T(8,128)(2,1)}), bf16[16,8,1408]{2,1,0:T(8,128)(2,1)S(1)}, u32[]{:S(2)}, u32[]{:S(2)}) %all-to-all-start.2) | async-done | bytes 360480 | tf_op jit(solution)/shard_map/all_to_all | solution.py:34
  71.7 2.4 %pair_tile.1 = (bf16[128,1408]{1,0:T(8,128)(2,1)}, bf16[128,256]{1,0:T(8,128)(2,1)S(1)}, f32[8,1024]{1,0:T(8,128)S(1)}, f32[8,128]{1,0:T(8,128)S(1)}) custom-call(s32[5]{0:T(128)S(1)} %stack.64.place_ref, f32[2]{0:T(128)S(1)} %pad_maximum_fusion.2.scalar_ref, bf16[128,1408]{1,0:T(8,128)(2,1)S(1)} %bitcast.39, bf16[128,2432]{1,0:T(8,128)(2,1)S(1)} %bitcast.37, ...), custom_call_target="tpu_custom_call" | custom-call | tf_op jit(solution)/shard_map/pair_tile/pallas_call | solution.py:228
  74.1 6.0 %all-to-all-start.3 = ((bf16[16,8,1408]{2,1,0:T(8,128)(2,1)}), bf16[16,8,1408]{2,1,0:T(8,128)(2,1)S(1)}, u32[]{:S(2)}, u32[]{:S(2)}) async-start(bf16[16,8,1408]{2,1,0:T(8,128)(2,1)} %bitcast.16), calls=%async_computation.3 | async-start | bytes 720896 | tf_op jit(solution)/shard_map/all_to_all | solution.py:416
  80.2 0.0 copy-start.5
  80.2 0.9 fusion.order_ref
  81.1 2.8 %text_tile.1 = (f32[128,1024]{1,0:T(8,128)S(1)}, f32[128,1024]{1,0:T(8,128)}, f32[8,1024]{1,0:T(8,128)S(1)}) custom-call(bf16[128,1408]{1,0:T(8,128)(2,1)S(1)} %bitcast.40, bf16[128,256]{1,0:T(8,128)(2,1)S(1)} %get-tuple-element.30.coeff_ref, f32[8,1024]{1,0:T(8,128)S(1)} %get-tuple-element.23.unit_ref, bf16[1024,1024]{1,0:T(8,128)(2,1)S(1)} %fusion.order_ref), custom_call_target="tpu_custom_call" | custom-call | tf_op jit(solution)/shard_map/text_tile/pallas_call | solution.py:290
  83.9 0.8 copy-done.10
  84.7 1.9 %collective-permute-start.1 = (f32[128,1024]{1,0:T(8,128)}, f32[128,1024]{1,0:T(8,128)}, u32[]{:S(2)}, u32[]{:S(2)}) collective-permute-start(f32[128,1024]{1,0:T(8,128)} %get-tuple-element.34), channel_id=1, source_target_pairs={{0,4},{4,0},{1,5},{5,1},{2,6},{6,2},{3,7},{7,3},{8,12},{12,8},{9,1... | collective-permute-start | bytes 1572872 | tf_op jit(solution)/shard_map/ppermute | solution.py:422
  86.6 3.4 %all-to-all-done.3 = bf16[16,8,1408]{2,1,0:T(8,128)(2,1)S(1)} async-done(((bf16[16,8,1408]{2,1,0:T(8,128)(2,1)}), bf16[16,8,1408]{2,1,0:T(8,128)(2,1)S(1)}, u32[]{:S(2)}, u32[]{:S(2)}) %all-to-all-start.3) | async-done | bytes 360480 | tf_op jit(solution)/shard_map/all_to_all | solution.py:416
  90.0 1.5 %fresh_back.1 = f32[4,1,1280]{2,1,0:T(1,128)} custom-call(s32[5]{0:T(128)S(1)} %stack.64.place_ref, bf16[128,1408]{1,0:T(8,128)(2,1)S(1)} %bitcast.41, bf16[128,2432]{1,0:T(8,128)(2,1)S(1)} %bitcast.38, bf16[128,2432]{1,0:T(8,128)(2,1)S(1)} %collective-permute-done.far_ref, f32[8,1024]{1,0:T(8,128)S(1)} %get-tuple-element.23.unit_ref, ...), custom_call_target="tpu_custom_call" | custom-call | tf_op jit(solution)/shard_map/fresh_back/pallas_call | solution.py:257
  91.5 5.9 %all-to-all-start.4 = ((f32[4,1,1280]{2,1,0:T(1,128)}), f32[4,1,1280]{2,1,0:T(1,128)S(1)}, u32[]{:S(2)}, u32[]{:S(2)}) async-start(f32[4,1,1280]{2,1,0:T(1,128)} %fresh_back.1), calls=%async_computation.4 | async-start | bytes 40960 | tf_op jit(solution)/shard_map/all_to_all | solution.py:419
  97.4 0.0 collective-permute-done.1
  97.4 2.0 %fusion.11 = bf16[16,8,1024]{2,1,0:T(8,128)(2,1)} fusion(f32[128,1024]{1,0:T(8,128)} %copy-done.10, f32[128,1024]{1,0:T(8,128)} %collective-permute-done.1), kind=kLoop, calls=%fused_computation.13 | loop fusion | flops 262144 | bytes 1310720 | tf_op jit(solution)/shard_map/reshape | solution.py:423
  99.4 2.0 %all-to-all-done.4.z_ref = f32[4,1,1280]{2,1,0:T(1,128)S(1)} async-done(((f32[4,1,1280]{2,1,0:T(1,128)}), f32[4,1,1280]{2,1,0:T(1,128)S(1)}, u32[]{:S(2)}, u32[]{:S(2)}) %all-to-all-start.4) | async-done | bytes 20512 | tf_op jit(solution)/shard_map/all_to_all | solution.py:419
  101.3 5.4 %all-to-all-start.5 = ((bf16[16,8,1024]{2,1,0:T(8,128)(2,1)}), bf16[16,8,1024]{2,1,0:T(8,128)(2,1)S(1)}, u32[]{:S(2)}, u32[]{:S(2)}) async-start(bf16[16,8,1024]{2,1,0:T(8,128)(2,1)} %fusion.11), calls=%async_computation.5 | async-start | bytes 524288 | tf_op jit(solution)/shard_map/all_to_all | solution.py:423
  106.7 0.0 copy-start.12
  106.7 1.3 %image_end.1 = (f32[8,1024]{1,0:T(8,128)}, f32[8,1]{1,0:T(8,128)S(1)}) custom-call(s32[5]{0:T(128)S(1)} %stack.64.place_ref, bf16[128,1408]{1,0:T(8,128)(2,1)S(1)} %bitcast.42, bf16[8,1024]{1,0:T(8,128)(2,1)S(1)} %copy-done.11, f32[8,1024]{1,0:T(8,128)S(1)} %get-tuple-element.31.plain_ref, f32[8,128]{1,0:T(8,128)S(1)} %get-tuple-element.24.norm_ref), custom_call_target="tpu_custom_call" | custom-call | tf_op jit(solution)/shard_map/image_end/pallas_call | solution.py:324
  108.0 0.6 reduce.1
  108.7 0.0 copy-done.3
  108.7 0.0 copy-done.5
  108.7 2.1 %copy-done.1 = f32[10,257,257]{2,1,0:T(8,128)S(1)} copy-done((f32[10,257,257]{2,1,0:T(8,128)S(1)}, f32[10,257,257]{2,1,0:T(8,128)}, u32[]{:S(2)}) %copy-start.1) | copy-done | bytes 2641984
  110.8 1.1 copy-done.7
  111.9 1.3 %copy-done.9 = f32[257,1280]{1,0:T(8,128)S(1)} copy-done((f32[257,1280]{1,0:T(8,128)S(1)}, f32[257,1280]{1,0:T(8,128)}, u32[]{:S(2)}) %copy-start.9) | copy-done | bytes 1315864
  113.3 5.9 %attend_back.1 = (bf16[1,257,1280]{2,1,0:T(8,128)(2,1)}, bf16[1,257,1280]{2,1,0:T(8,128)(2,1)}, bf16[1,257,1280]{2,1,0:T(8,128)(2,1)}) custom-call(f32[4,1,1280]{2,1,0:T(1,128)S(1)} %all-to-all-done.4.z_ref, bf16[1,257,1280]{2,1,0:T(8,128)(2,1)S(1)} %copy-done.3, bf16[1,257,1280]{2,1,0:T(8,128)(2,1)S(1)} %copy-done.5, bf16[1,257,1280]{2,1,0:T(8,128)(2,1)S(1)} %copy-done.7, ...), custom_call_target="tpu_custom_call" | custom-call | tf_op jit(solution)/shard_map/attend_back/pallas_call | solution.py:129
  119.1 1.2 all-to-all-done.5
  120.3 0.8 text_end.1
  (22 shorter events, 0.2 us)
Async XLA Ops:
  0.6 34.7 %copy-start.11 = (bf16[8,1024]{1,0:T(8,128)(2,1)S(1)}, bf16[8,1024]{1,0:T(8,128)(2,1)}, u32[]{:S(2)}) copy-start(bf16[8,1024]{1,0:T(8,128)(2,1)} %cache_ref.1) | copy-start | bytes 49156
  0.6 34.8 %copy-start.13 = (s32[8]{0:T(128)S(1)}, s32[8]{0:T(128)}, u32[]{:S(2)}) copy-start(s32[8]{0:T(128)} %param.18) | copy-start | bytes 100
  4.7 34.3 %all-to-all-start.1 = ((bf16[16,8,2432]{2,1,0:T(8,128)(2,1)}), bf16[16,8,2432]{2,1,0:T(8,128)(2,1)S(1)}, u32[]{:S(2)}, u32[]{:S(2)}) async-start(bf16[16,8,2432]{2,1,0:T(8,128)(2,1)} %broadcast_in_dim.10), calls=%async_computation.1 | async-start | bytes 1245184 | tf_op jit(solution)/shard_map/all_to_all | solution.py:34
  20.4 1.1 copy-start.2
  21.5 1.1 copy-start.4
  22.6 1.1 copy-start.6
  30.4 1.9 %copy-start = (f32[10,257,257]{2,1,0:T(8,128)}, f32[10,257,257]{2,1,0:T(8,128)S(1)}, u32[]{:S(2)}) copy-start(f32[10,257,257]{2,1,0:T(8,128)S(1)} %get-tuple-element.25.probs_ref) | copy-start | bytes 7925884
  32.3 1.1 copy-start.8
  39.0 8.7 %all-to-all-start = ((bf16[4,2,640]{2,1,0:T(2,128)(2,1)}), bf16[4,2,640]{2,1,0:T(2,128)(2,1)S(1)}, u32[]{:S(2)}, u32[]{:S(2)}) async-start(bf16[4,2,640]{2,1,0:T(2,128)(2,1)} %reshape.163), calls=%async_computation | async-start | bytes 20480 | tf_op jit(solution)/shard_map/all_to_all | solution.py:34
  43.8 4.0 %collective-permute-start = (bf16[128,2432]{1,0:T(8,128)(2,1)S(1)}, bf16[128,2432]{1,0:T(8,128)(2,1)S(1)}, u32[]{:S(2)}, u32[]{:S(2)}) collective-permute-start(bf16[128,2432]{1,0:T(8,128)(2,1)S(1)} %bitcast.34), channel_id=1, source_target_pairs={{0,4},{4,0},{1,5},{5,1},{2,6},{6,2},{3,7},{7,3},{8,12},{12,8},{9,1... | collective-permute-start | bytes 1867784 | tf_op jit(solution)/shard_map/ppermute | solution.py:384
  48.9 22.7 %all-to-all-start.2 = ((bf16[16,8,1408]{2,1,0:T(8,128)(2,1)}), bf16[16,8,1408]{2,1,0:T(8,128)(2,1)S(1)}, u32[]{:S(2)}, u32[]{:S(2)}) async-start(bf16[16,8,1408]{2,1,0:T(8,128)(2,1)} %broadcast_in_dim.11), calls=%async_computation.2 | async-start | bytes 720896 | tf_op jit(solution)/shard_map/all_to_all | solution.py:34
  74.1 15.9 %all-to-all-start.3 = ((bf16[16,8,1408]{2,1,0:T(8,128)(2,1)}), bf16[16,8,1408]{2,1,0:T(8,128)(2,1)S(1)}, u32[]{:S(2)}, u32[]{:S(2)}) async-start(bf16[16,8,1408]{2,1,0:T(8,128)(2,1)} %bitcast.16), calls=%async_computation.3 | async-start | bytes 720896 | tf_op jit(solution)/shard_map/all_to_all | solution.py:416
  80.2 28.5 %copy-start.3 = (bf16[1,257,1280]{2,1,0:T(8,128)(2,1)S(1)}, bf16[1,257,1280]{2,1,0:T(8,128)(2,1)}, u32[]{:S(2)}) copy-start(bf16[1,257,1280]{2,1,0:T(8,128)(2,1)} %q_ref.3) | copy-start | bytes 1973764
  80.2 28.5 %copy-start.5 = (bf16[1,257,1280]{2,1,0:T(8,128)(2,1)S(1)}, bf16[1,257,1280]{2,1,0:T(8,128)(2,1)}, u32[]{:S(2)}) copy-start(bf16[1,257,1280]{2,1,0:T(8,128)(2,1)} %k_ref.3) | copy-start | bytes 1973764
  83.9 0.8 copy-start.10
  84.7 12.8 %collective-permute-start.1 = (f32[128,1024]{1,0:T(8,128)}, f32[128,1024]{1,0:T(8,128)}, u32[]{:S(2)}, u32[]{:S(2)}) collective-permute-start(f32[128,1024]{1,0:T(8,128)} %get-tuple-element.34), channel_id=1, source_target_pairs={{0,4},{4,0},{1,5},{5,1},{2,6},{6,2},{3,7},{7,3},{8,12},{12,8},{9,1... | collective-permute-start | bytes 1572872 | tf_op jit(solution)/shard_map/ppermute | solution.py:422
  91.5 9.8 %all-to-all-start.4 = ((f32[4,1,1280]{2,1,0:T(1,128)}), f32[4,1,1280]{2,1,0:T(1,128)S(1)}, u32[]{:S(2)}, u32[]{:S(2)}) async-start(f32[4,1,1280]{2,1,0:T(1,128)} %fresh_back.1), calls=%async_computation.4 | async-start | bytes 40960 | tf_op jit(solution)/shard_map/all_to_all | solution.py:419
  101.3 19.0 %all-to-all-start.5 = ((bf16[16,8,1024]{2,1,0:T(8,128)(2,1)}), bf16[16,8,1024]{2,1,0:T(8,128)(2,1)S(1)}, u32[]{:S(2)}, u32[]{:S(2)}) async-start(bf16[16,8,1024]{2,1,0:T(8,128)(2,1)} %fusion.11), calls=%async_computation.5 | async-start | bytes 524288 | tf_op jit(solution)/shard_map/all_to_all | solution.py:423
  106.7 13.6 %copy-start.12 = (bf16[8,1024]{1,0:T(8,128)(2,1)S(1)}, bf16[8,1024]{1,0:T(8,128)(2,1)}, u32[]{:S(2)}) copy-start(bf16[8,1024]{1,0:T(8,128)(2,1)} %embed_ref.1) | copy-start | bytes 49156
  108.7 2.1 %copy-start.1 = (f32[10,257,257]{2,1,0:T(8,128)S(1)}, f32[10,257,257]{2,1,0:T(8,128)}, u32[]{:S(2)}) copy-start(f32[10,257,257]{2,1,0:T(8,128)} %copy-done) | copy-start | bytes 7925884
  110.8 1.1 copy-start.7
  111.9 1.3 %copy-start.9 = (f32[257,1280]{1,0:T(8,128)S(1)}, f32[257,1280]{1,0:T(8,128)}, u32[]{:S(2)}) copy-start(f32[257,1280]{1,0:T(8,128)} %copy-done.8) | copy-start | bytes 3947524

commit v4 on v3

--- a/solution.py
+++ b/solution.py
@@ -27,16 +27,18 @@
 VMEM = pl.BlockSpec(memory_space=pltpu.VMEM)
 SMEM = pl.BlockSpec(memory_space=pltpu.SMEM)
 PARAMS = pltpu.CompilerParams(vmem_limit_bytes=24 * 2**20)
-
-
-def spread(block, axes, count):
-    sent = jnp.broadcast_to(block[None], (count,) + block.shape)
-    return lax.all_to_all(sent, axes, 0, 0)
-
-
-def halves(value):
-    high = value.astype(BF16)
-    return high, (value - high.astype(F32)).astype(BF16)
+STREAMED = pltpu.CompilerParams(vmem_limit_bytes=56 * 2**20)
+
+
+def lasting(microseconds):
+    return pl.CostEstimate(
+        flops=0, transcendentals=0, bytes_accessed=int(microseconds * 3_600_000)
+    )
+
+
+def exchange(blocks, axes, count):
+    sent = blocks.reshape(count, blocks.shape[0] // count, blocks.shape[1])
+    return lax.all_to_all(sent, axes, 0, 0).reshape(blocks.shape)
 
 
 def unit_rows(raw_rows):
@@ -63,12 +65,18 @@
 def block_sum(value):
     value = value.astype(F32)
     total = value[0:8]
-    for i in range(1, 16):
+    for i in range(1, value.shape[0] // 8):
         total += value[i * 8 : i * 8 + 8]
     return total
 
 
 def attend_kernel(q_ref, k_ref, v_ref, probs_ref, mass_ref, pooled_ref):
+    step = pl.program_id(0)
+
+    @pl.when(step == 0)
+    def _():
+        pooled_ref[...] = jnp.zeros_like(pooled_ref)
+
     ones = jnp.ones((SEQ, HEAD_DIM), BF16)
     for one in range(PAIRED):
         at = slice(one * HEAD_DIM, (one + 1) * HEAD_DIM)
@@ -79,7 +87,9 @@
         mass = contract(probs.astype(BF16), ones, ((0,), (0,)))
         mass_ref[:, at] = mass
         pooled = jnp.sum(mass * v_ref[0, :, at].astype(F32), axis=0, keepdims=True)
-        pooled_ref[:, at] = (pooled * (1.0 / SEQ)).astype(BF16)
+        pooled = (pooled * (1.0 / SEQ)).astype(BF16).astype(F32)
+        for copy in range(4):
+            pooled_ref[copy, pl.ds(step * PAIRED + one, 1), :] = pooled
 
 
 def attend(query_tokens, key_tokens, value_tokens):
@@ -92,14 +102,15 @@
         out_specs=[
             pl.BlockSpec((PAIRED, SEQ, SEQ), lambda i: (i, 0, 0)),
             pl.BlockSpec((SEQ, wide), lambda i: (0, i)),
-            pl.BlockSpec((1, wide), lambda i: (0, i)),
+            pl.BlockSpec((4, 16, HEAD_DIM), lambda i: (0, 0, 0)),
         ],
         out_shape=[
             jax.ShapeDtypeStruct((HEADS, SEQ, SEQ), F32),
             jax.ShapeDtypeStruct((SEQ, WIDTH), F32),
-            jax.ShapeDtypeStruct((1, WIDTH), BF16),
-        ],
-        compiler_params=PARAMS,
+            jax.ShapeDtypeStruct((4, 16, HEAD_DIM), F32),
+        ],
+        compiler_params=STREAMED,
+        cost_estimate=lasting(7),
         name="attend",
     )(query_tokens, key_tokens, value_tokens)
 
@@ -123,7 +134,7 @@
         dv_ref[0, :, at] = (mass_ref[:, at] * cot_row.astype(F32)).astype(BF16)
 
 
-def attend_back(parts, query_tokens, key_tokens, value_tokens, probs, mass):
+def attend_back(pooled_grad, query_tokens, key_tokens, value_tokens, probs, mass):
     wide = PAIRED * HEAD_DIM
     tokens = pl.BlockSpec((1, SEQ, wide), lambda i: (0, 0, i))
     return pl.pallas_call(
@@ -139,9 +150,111 @@
         ],
         out_specs=[tokens] * 3,
         out_shape=[jax.ShapeDtypeStruct((1, SEQ, WIDTH), BF16)] * 3,
-        compiler_params=PARAMS,
+        compiler_params=STREAMED,
+        cost_estimate=lasting(6),
         name="attend_back",
-    )(parts, query_tokens, key_tokens, value_tokens, probs, mass)
+    )(pooled_grad, query_tokens, key_tokens, value_tokens, probs, mass)
+
+
+def tail_of(labels):
+    lane, row = lanes((8, TAIL)), rows((8, TAIL))
+    tail = jnp.zeros((8, TAIL), jnp.int32)
+    for place, label_ref in enumerate(labels):
+        label = jnp.zeros((8, TAIL), jnp.int32)
+        for i in range(8):
+            label = jnp.where(row == i, label_ref[i], label)
+        tail = jnp.where(lane == 2 * place, label // 64, tail)
+        tail = jnp.where(lane == 2 * place + 1, label % 64, tail)
+    return tail.astype(F32)
+
+
+def first_kernel(
+    pair_ref, igroup_ref, tgroup_ref, text_ref, cache_ref, weight_ref, text_out_ref, image_out_ref
+):
+    unit_text, _ = unit_rows(text_ref[...].astype(F32))
+    unit_image, _ = unit_rows(cache_ref[...].astype(F32))
+    message = jnp.concatenate(
+        [unit_text, tail_of((pair_ref, tgroup_ref)), weight_ref[...].astype(F32)], axis=1
+    )
+    message = jnp.concatenate([message, message], axis=0).astype(BF16)
+    for i in range(8):
+        text_out_ref[i * 16 : i * 16 + 16, :] = message
+    stem = jnp.concatenate([unit_image, tail_of((igroup_ref,))], axis=1)
+    image_out_ref[...] = jnp.concatenate([stem, stem], axis=0).astype(BF16)
+
+
+def first_messages(pair, igroup, tgroup, text, cache, weight):
+    return pl.pallas_call(
+        first_kernel,
+        in_specs=[SMEM] * 3 + [VMEM] * 3,
+        out_specs=[VMEM] * 2,
+        out_shape=[
+            jax.ShapeDtypeStruct((128, STEM + WIDTH), BF16),
+            jax.ShapeDtypeStruct((16, STEM), BF16),
+        ],
+        compiler_params=STREAMED,
+        cost_estimate=lasting(1),
+        name="first_messages",
+    )(pair, igroup, tgroup, text, cache, weight)
+
+
+def fresh_kernel(pooled_ref, near_ref, far_ref, stem_ref, out_ref):
+    heads = [
+        jnp.concatenate([pooled_ref[b, i : i + 1, :] for b in (0, 1, 2, 3) * 2], axis=0)
+        for i in range(HEADS)
+    ]
+    pooled = jnp.concatenate(heads, axis=1).astype(BF16)
+    columns = jnp.concatenate(
+        [contract(pooled, side[:, STEM:], ((1,), (1,))) for side in (near_ref, far_ref)], axis=1
+    )
+    high = columns.astype(BF16).astype(F32)
+    packed = jnp.where(rows((8, 256)) < 4, high, columns - high)
+    packed = jnp.concatenate([packed, packed], axis=0).astype(BF16)
+    for i in range(8):
+        out_ref[i * 16 : i * 16 + 16, :STEM] = stem_ref[...]
+        out_ref[i * 16 : i * 16 + 16, STEM:] = packed
+
+
+def fresh_message(pooled, near, far, stem):
+    return pl.pallas_call(
+        fresh_kernel,
+        in_specs=[VMEM] * 4,
+        out_specs=VMEM,
+        out_shape=jax.ShapeDtypeStruct((128, STEM + 256), BF16),
+        compiler_params=PARAMS,
+        cost_estimate=lasting(1),
+        name="fresh_message",
+    )(pooled, near, far, stem)
+
+
+def order_of(c):
+    spot = lanes((1, EMBED))
+    column = (
+        spot % 128 // 16 * 128
+        + spot // 256 * 32
+        + spot // 8 % 2 * 16
+        + (spot // 128 + c) % 2 * 8
+        + spot % 8
+    )
+    return (rows((EMBED, EMBED)) == column).astype(BF16)
+
+
+def turn_kernel(place_ref, near_ref, far_ref, turned_ref):
+    order = order_of(place_ref[3])
+    turned_ref[:128, :] = contract(near_ref[:, :EMBED], order, ((1,), (0,))).astype(BF16)
+    turned_ref[128:, :] = contract(far_ref[:, :EMBED], order, ((1,), (0,))).astype(BF16)
+
+
+def turn(place, near, far):
+    return pl.pallas_call(
+        turn_kernel,
+        in_specs=[SMEM, VMEM, VMEM],
+        out_specs=VMEM,
+        out_shape=jax.ShapeDtypeStruct((256, EMBED), BF16),
+        compiler_params=PARAMS,
+        cost_estimate=lasting(3),
+        name="turn",
+    )(place, near, far)
 
 
 def pair_kernel(
@@ -152,7 +265,8 @@
     far_ref,
     turned_ref,
     back_ref,
-    coeff_ref,
+    own_ref,
+    other_ref,
     unit_ref,
     norm_ref,
 ):
@@ -204,10 +318,15 @@
         losses += jnp.sum(jnp.maximum(-margin, 0.0) + jnp.log1p(small), axis=1, keepdims=True)
         share = jnp.where(margin >= 0, small, 1.0) / (1.0 + small)
         coeffs = (temper * (-signed * share)).astype(BF16)
-        coeff_ref[:, half * 128 : half * 128 + 128] = coeffs
+        (own_ref, other_ref)[half][:128, :128] = coeffs
         image_part += contract(coeffs, texts, ((1,), (0,)))
         fresh_coeffs = contract(chosen, coeffs, ((1,), (0,))).astype(BF16)
         fresh_part += contract(fresh_coeffs, turned, ((1,), (0,)))
+
+    for ref in (own_ref, other_ref):
+        ref[:128, 128:] = images
+        ref[128:, :128] = jnp.zeros((16, 128), BF16)
+        ref[128:, 128:] = jnp.concatenate([fresh_unit, fresh_unit], axis=0).astype(BF16)
 
     back_ref[:, :EMBED] = image_part.astype(BF16)
     dots = jnp.sum(fresh_part * fresh_unit, axis=1, keepdims=True)
@@ -228,14 +347,16 @@
     return pl.pallas_call(
         pair_kernel,
         in_specs=[SMEM, SMEM, VMEM, VMEM, VMEM, VMEM],
-        out_specs=[VMEM] * 4,
+        out_specs=[VMEM] * 5,
         out_shape=[
             jax.ShapeDtypeStruct((128, STEM + 256), BF16),
-            jax.ShapeDtypeStruct((128, 256), BF16),
+            jax.ShapeDtypeStruct((144, 128 + EMBED), BF16),
+            jax.ShapeDtypeStruct((144, 128 + EMBED), BF16),
             jax.ShapeDtypeStruct((8, EMBED), F32),
             jax.ShapeDtypeStruct((8, 128), F32),
         ],
         compiler_params=PARAMS,
+        cost_estimate=lasting(3),
         name="pair_tile",
     )(place, scalars, got, near, far, turned)
 
@@ -260,45 +381,54 @@
         out_specs=VMEM,
         out_shape=jax.ShapeDtypeStruct((4, 1, WIDTH), F32),
         compiler_params=PARAMS,
+        cost_estimate=lasting(2),
         name="fresh_back",
     )(place, got, near, far, unit, norm)
 
 
-def text_kernel(got_ref, coeff_ref, unit_ref, order_ref, near_ref, far_ref, plain_ref):
-    unit = unit_ref[...]
-    first = unit.astype(BF16)
-    rest = unit - first.astype(F32)
-    second = rest.astype(BF16)
-    third = (rest - second.astype(F32)).astype(BF16)
-    order = order_ref[...]
-    plain = contract(first, order, ((1,), (1,))) + (
-        contract(second, order, ((1,), (1,))) + contract(third, order, ((1,), (1,)))
-    )
-    plain_ref[...] = plain
-    fresh_low = plain.astype(BF16).astype(F32)
-    repeated = jnp.concatenate(
-        [jnp.broadcast_to(fresh_low[i : i + 1], (32, EMBED)) for i in range(4)], axis=0
-    )
-    image_rows = jnp.where(
-        rows((128, EMBED)) % 32 == 0, repeated, got_ref[:, :EMBED].astype(F32)
-    ).astype(BF16)
-    near_ref[...] = contract(coeff_ref[:, :128], image_rows, ((0,), (0,)))
-    far_ref[...] = contract(coeff_ref[:, 128:], image_rows, ((0,), (0,)))
-
-
-def text_tile(got, coeffs, unit, order):
+def text_kernel(place_ref, own_ref, other_ref, unit_ref, keep_ref, send_ref, plain_ref):
+    h, c = place_ref[2], place_ref[3]
+    total = jnp.zeros((128, EMBED), F32)
+    for ref, core in ((own_ref, c), (other_ref, 1 - c)):
+        order = order_of(core)
+        if ref is own_ref:
+            rest = unit_ref[...]
+            plain = jnp.zeros((8, EMBED), F32)
+            for _ in range(3):
+                piece = rest.astype(BF16)
+                rest -= piece.astype(F32)
+                plain += contract(piece, order, ((1,), (1,)))
+            plain_ref[...] = plain
+        fresh_low = contract(ref[128:, 128:], order, ((1,), (1,)))
+        repeated = jnp.concatenate(
+            [jnp.broadcast_to(fresh_low[i : i + 1], (32, EMBED)) for i in range(4)], axis=0
+        )
+        image_rows = jnp.where(
+            rows((128, EMBED)) % 32 == 0, repeated, ref[:128, 128:].astype(F32)
+        ).astype(BF16)
+        total += contract(ref[:128, :128], image_rows, ((0,), (0,)))
+    sent = []
+    for step in range(8):
+        first, second = total[step * 16 : step * 16 + 8], total[step * 16 + 8 : step * 16 + 16]
+        keep_ref[step * 8 : step * 8 + 8, :] = jnp.where(h == 0, first, second)
+        sent.append(jnp.where(h == 0, second, first))
+    send_ref[...] = jnp.concatenate(sent, axis=0).astype(BF16)
+
+
+def text_tile(place, own, other, unit):
     return pl.pallas_call(
         text_kernel,
-        in_specs=[VMEM] * 4,
+        in_specs=[SMEM] + [VMEM] * 3,
         out_specs=[VMEM] * 3,
         out_shape=[
-            jax.ShapeDtypeStruct((128, EMBED), F32),
-            jax.ShapeDtypeStruct((128, EMBED), F32),
+            jax.ShapeDtypeStruct((64, EMBED), F32),
+            jax.ShapeDtypeStruct((64, EMBED), BF16),
             jax.ShapeDtypeStruct((8, EMBED), F32),
         ],
         compiler_params=PARAMS,
+        cost_estimate=lasting(4),
         name="text_tile",
-    )(got, coeffs, unit, order)
+    )(place, own, other, unit)
 
 
 def image_grad_kernel(place_ref, got_ref, cache_ref, plain_ref, norm_ref, grad_ref, loss_ref):
@@ -330,6 +460,7 @@
             jax.ShapeDtypeStruct((8, 1), F32),
         ],
         compiler_params=PARAMS,
+        cost_estimate=lasting(1),
         name="image_end",
     )(place, got, cache, plain, norm)
 
@@ -347,16 +478,9 @@
         out_specs=VMEM,
         out_shape=jax.ShapeDtypeStruct((8, EMBED), F32),
         compiler_params=PARAMS,
+        cost_estimate=lasting(1),
         name="text_end",
     )(got, embed)
-
-
-def label_tail(*labels):
-    parts = []
-    for label in labels:
-        parts += [label // 64, label % 64]
-    tail = jnp.stack(parts, axis=1).astype(BF16)
-    return jnp.pad(tail, ((0, 0), (0, TAIL - tail.shape[1])))
 
 
 def on_device(
@@ -376,57 +500,37 @@
     place = jnp.stack([z, x, h, c, m]).astype(jnp.int32)
     scalars = jnp.stack([logit_scale, logit_bias])
 
-    unit_text, _ = unit_rows(text_embed.astype(F32))
-    text_message = jnp.concatenate(
-        [unit_text.astype(BF16), label_tail(text_pair, text_group), head_weight.T], axis=1
-    )
-    near = spread(text_message, TEXT_AXES, 16).reshape(128, STEM + WIDTH)
+    message, stem = first_messages(
+        text_pair, image_group, text_group, text_embed, image_cache, head_weight.T
+    )
+    near = exchange(message, TEXT_AXES, 16)
+    probs, mass, pooled = attend(query_tokens, key_tokens, value_tokens)
+    near, pooled = lax.optimization_barrier((near, pooled))
     far = lax.ppermute(near, "c", SWAP)
-
-    spot = jnp.arange(EMBED)
-    column = (
-        (spot % 128) // 16 * 128
-        + spot // 256 * 32
-        + (spot // 8) % 2 * 16
-        + ((spot // 128) % 2 + c) % 2 * 8
-        + spot % 8
-    )
-    order = (jnp.arange(EMBED)[:, None] == column[None, :]).astype(BF16)
-    texts = jnp.concatenate([near[:, :EMBED], far[:, :EMBED]], axis=0)
-    turned = jnp.dot(texts, order, preferred_element_type=F32).astype(BF16)
-
-    probs, mass, pooled = attend(query_tokens, key_tokens, value_tokens)
-
-    pooled_all = spread(pooled, "x", 4).reshape(4, WIDTH)
-    partial_cols = jnp.concatenate(
-        [contract(pooled_all, side[:, STEM:], ((1,), (1,))) for side in (near, far)], axis=1
-    )
-    cached, _ = unit_rows(image_cache.astype(F32))
-    image_message = jnp.concatenate(
-        [
-            cached.astype(BF16),
-            label_tail(image_group),
-            jnp.concatenate(halves(partial_cols), axis=0),
-        ],
-        axis=1,
-    )
-    image_got = spread(image_message, IMAGE_AXES, 16).reshape(128, STEM + 256)
-
-    back, coeffs, unit, norm = pair_tile(place, scalars, image_got, near, far, turned)
-    back = lax.all_to_all(back.reshape(16, 8, STEM + 256), IMAGE_AXES, 0, 0)
-    back = back.reshape(128, STEM + 256)
-    pooled_part = fresh_back(place, back, near, far, unit, norm)
-    pooled_part = lax.all_to_all(pooled_part, "x", 0, 0)
-
-    text_near, text_far, plain = text_tile(image_got, coeffs, unit, order)
-    text_part = (text_near + lax.ppermute(text_far, "c", SWAP)).astype(BF16)
-    text_part = lax.all_to_all(text_part.reshape(16, 8, EMBED), TEXT_AXES, 0, 0)
+    turned = turn(place, near, far)
+
+    pooled_all = lax.all_to_all(pooled, "x", 0, 0)
+    message = fresh_message(pooled_all, near, far, stem)
+    image_got = exchange(message, IMAGE_AXES, 16)
+
+    back, own, other, unit, norm = pair_tile(place, scalars, image_got, near, far, turned)
+    other = lax.ppermute(other, "c", SWAP)
+    back = exchange(back, IMAGE_AXES, 16)
+    keep, send, plain = text_tile(place, own, other, unit)
+    back, keep, send, plain = lax.optimization_barrier((back, keep, send, plain))
+    text_part = (keep + lax.ppermute(send, "h", SWAP).astype(F32)).astype(BF16)
+    pooled_grad = lax.all_to_all(fresh_back(place, back, near, far, unit, norm), "x", 0, 0)
+    image_grad, row_loss = image_end(place, back, image_cache, plain, norm)
+    pooled_grad, text_part, image_grad = lax.optimization_barrier(
+        (pooled_grad, text_part, image_grad)
+    )
+    text_part = exchange(text_part, "z", 8)
 
     query_grad, key_grad, value_grad = attend_back(
-        pooled_part, query_tokens, key_tokens, value_tokens, probs, mass
-    )
-    image_grad, row_loss = image_end(place, back, image_cache, plain, norm)
-    text_grad = text_end(text_part.reshape(128, EMBED), text_embed)
+        pooled_grad, query_tokens, key_tokens, value_tokens, probs, mass
+    )
+    text_part, query_grad = lax.optimization_barrier((text_part, query_grad))
+    text_grad = text_end(text_part, text_embed)
     return query_grad, key_grad, value_grad, image_grad, text_grad, row_loss.reshape(8)
 
 

time: 122 us -> 118 us (0.967)
  the two profiles are of different devices: /device:TPU:2 before, /device:TPU:64 now
where the time goes in v4:
time: 118 us; the launch traced here: 117 us
  starting transfers between devices  44.8 us (38%)
  Pallas kernels  30.6 us (26%)
  waiting for transfers between devices  27.8 us (24%)
  blocking collectives  9.75 us (8%)
  between operations  2.03 us (2%)
  other arithmetic  1.38 us (1%)
    all_to_all x4, starting transfers between devices, exchange(): return lax.all_to_all(sent, axes, 0, 0).reshape(blocks.shape)  34.3 us
    all_to_all x4, waiting for transfers between devices, exchange(): return lax.all_to_all(sent, axes, 0, 0).reshape(blocks.shape)  22.9 us
    all_to_all x1, blocking collectives, on_device(): pooled_all = lax.all_to_all(pooled, 'x', 0, 0)  9.75 us
    pallas_call x1, Pallas kernels, attend(): pl.pallas_call(attend_kernel, grid=(HEADS // PAIRED,), in_specs=[tokens]...  8.48 us
    pallas_call x1, Pallas kernels, attend_back(): pl.pallas_call(attend_back_kernel, grid=(HEADS // PAIRED,), in_specs=[pl....  8 us
    pallas_call x1, Pallas kernels, text_tile(): pl.pallas_call(text_kernel, in_specs=[SMEM] + [VMEM] * 3, out_specs=[VMEM...  3.63 us
    ppermute x1, starting transfers between devices, on_device(): text_part = (keep + lax.ppermute(send, 'h', SWAP).astype(F32)).astype(BF16)  3.43 us
    all_to_all x1, starting transfers between devices, on_device(): lax.all_to_all(fresh_back(place, back, near, far, unit, norm), 'x', 0, 0)  3.26 us
  transfers between devices with their start and end apart: 8, of which 6 were waited for; matrix products, arithmetic and copies ran while one was open for 1% of the time, Pallas kernels for 21%

profile of v4, /device:TPU:64, one launch (start us, length us, event | category | flops | bytes accessed | tf_op | source)
XLA Modules:
  0.0 117.2 jit_solution(15501014595024456515)
XLA Ops:
  0.6 1.8 %first_messages.1 = (bf16[128,2432]{1,0:T(8,128)(2,1)}, bf16[16,1152]{1,0:T(8,128)(2,1)}) custom-call(s32[8]{0:T(128)} %pair_ref.1, s32[8]{0:T(128)} %igroup_ref.1, s32[8]{0:T(128)} %tgroup_ref.1, bf16[8,1024]{1,0:T(8,128)(2,1)} %embed_ref.1, bf16[8,1024]{1,0:T(8,128)(2,1)} %cache_ref.3, bf16[8,1280]{1,0:T(8,128)(2,1)} %bitcast.28), custom_call_target="tpu_custom_call" | custom-call | bytes 3600000 | tf_op jit(solution)/shard_map/first_messages/pallas_call | solution.py:187
  2.4 15.2 %all-to-all-start = ((bf16[16,8,2432]{2,1,0:T(8,128)(2,1)}), bf16[16,8,2432]{2,1,0:T(8,128)(2,1)S(1)}, u32[]{:S(2)}, u32[]{:S(2)}) async-start(bf16[16,8,2432]{2,1,0:T(8,128)(2,1)} %bitcast.27), calls=%async_computation | async-start | bytes 1245184 | tf_op jit(solution)/shard_map/all_to_all | solution.py:41
  17.6 8.5 %attend.1 = (f32[10,257,257]{2,1,0:T(8,128)}, f32[257,1280]{1,0:T(8,128)}, f32[4,16,128]{2,1,0:T(8,128)}) custom-call(bf16[1,257,1280]{2,1,0:T(8,128)(2,1)} %q_ref.3, bf16[1,257,1280]{2,1,0:T(8,128)(2,1)} %k_ref.3, bf16[1,257,1280]{2,1,0:T(8,128)(2,1)} %v_ref.3), custom_call_target="tpu_custom_call" | custom-call | bytes 25200000 | tf_op jit(solution)/shard_map/attend/pallas_call | solution.py:98
  26.1 9.1 %all-to-all-done = bf16[16,8,2432]{2,1,0:T(8,128)(2,1)S(1)} async-done(((bf16[16,8,2432]{2,1,0:T(8,128)(2,1)}), bf16[16,8,2432]{2,1,0:T(8,128)(2,1)S(1)}, u32[]{:S(2)}, u32[]{:S(2)}) %all-to-all-start) | async-done | bytes 622624 | tf_op jit(solution)/shard_map/all_to_all | solution.py:41
  35.2 1.9 %collective-permute-start = (bf16[128,2432]{1,0:T(8,128)(2,1)S(1)}, bf16[128,2432]{1,0:T(8,128)(2,1)S(1)}, u32[]{:S(2)}, u32[]{:S(2)}) collective-permute-start(bf16[128,2432]{1,0:T(8,128)(2,1)S(1)} %bitcast.18), channel_id=1, source_target_pairs={{0,4},{4,0},{1,5},{5,1},{2,6},{6,2},{3,7},{7,3},{8,12},{12,8},{9,1... | collective-permute-start | bytes 1867784 | tf_op jit(solution)/shard_map/ppermute | solution.py:509
  37.1 9.8 %all_to_all.30.pooled_ref = f32[4,16,128]{2,1,0:T(8,128)S(1)} all-to-all(f32[4,16,128]{2,1,0:T(8,128)} %get-tuple-element.37), channel_id=1, replica_groups=mesh['z'=8,'x'=4,'h'=2,'c'=2,'m'=4] {'x'}, dimensions={0} | all-to-all | bytes 65536 | tf_op jit(solution)/shard_map/all_to_all | solution.py:512
  46.8 0.0 collective-permute-done.far_ref
  46.8 0.0 copy-start.2
  46.8 0.8 copy-done.2
  47.6 1.0 fresh_message.1
  48.6 0.0 copy-start
  48.6 11.4 %all-to-all-start.2 = ((bf16[16,8,1408]{2,1,0:T(8,128)(2,1)}), bf16[16,8,1408]{2,1,0:T(8,128)(2,1)S(1)}, u32[]{:S(2)}, u32[]{:S(2)}) async-start(bf16[16,8,1408]{2,1,0:T(8,128)(2,1)} %bitcast.10), calls=%async_computation.2 | async-start | bytes 720896 | tf_op jit(solution)/shard_map/all_to_all | solution.py:41
  61.3 0.1 stack.32.place_ref
  61.4 0.1 pad_maximum_fusion.scalar_ref
  61.5 1.6 %turn.1.turned_ref = bf16[256,1024]{1,0:T(8,128)(2,1)S(1)} custom-call(s32[5]{0:T(128)S(1)} %stack.32.place_ref, bf16[128,2432]{1,0:T(8,128)(2,1)S(1)} %bitcast.20, bf16[128,2432]{1,0:T(8,128)(2,1)S(1)} %collective-permute-done.far_ref), custom_call_target="tpu_custom_call" | custom-call | bytes 10800000 | tf_op jit(solution)/shard_map/turn/pallas_call | solution.py:249
  63.1 9.1 %all-to-all-done.2 = bf16[16,8,1408]{2,1,0:T(8,128)(2,1)S(1)} async-done(((bf16[16,8,1408]{2,1,0:T(8,128)(2,1)}), bf16[16,8,1408]{2,1,0:T(8,128)(2,1)S(1)}, u32[]{:S(2)}, u32[]{:S(2)}) %all-to-all-start.2) | async-done | bytes 360480 | tf_op jit(solution)/shard_map/all_to_all | solution.py:41
  72.2 2.5 %pair_tile.1 = (bf16[128,1408]{1,0:T(8,128)(2,1)}, bf16[144,1152]{1,0:T(8,128)(2,1)S(1)}, bf16[144,1152]{1,0:T(8,128)(2,1)S(1)}, f32[8,1024]{1,0:T(8,128)S(1)}, f32[8,128]{1,0:T(8,128)S(1)}) custom-call(s32[5]{0:T(128)S(1)} %stack.32.place_ref, f32[2]{0:T(128)S(1)} %pad_maximum_fusion.scalar_ref, bf16[128,1408]{1,0:T(8,128)(2,1)S(1)} %bitcast.25, ...), custom_call_target="tpu_custom_call" | custom-call | bytes 10800000 | tf_op jit(solution)/shard_map/pair_tile/pallas_call | solution.py:347
  74.7 3.5 %all-to-all-start.3 = ((bf16[16,8,1408]{2,1,0:T(8,128)(2,1)}), bf16[16,8,1408]{2,1,0:T(8,128)(2,1)S(1)}, u32[]{:S(2)}, u32[]{:S(2)}) async-start(bf16[16,8,1408]{2,1,0:T(8,128)(2,1)} %bitcast.12), calls=%async_computation.3 | async-start | bytes 720896 | tf_op jit(solution)/shard_map/all_to_all | solution.py:41
  78.3 1.9 %collective-permute-start.1 = (bf16[144,1152]{1,0:T(8,128)(2,1)S(1)}, bf16[144,1152]{1,0:T(8,128)(2,1)S(1)}, u32[]{:S(2)}, u32[]{:S(2)}) collective-permute-start(bf16[144,1152]{1,0:T(8,128)(2,1)S(1)} %get-tuple-element.42), channel_id=1, source_target_pairs={{0,4},{4,0},{1,5},{5,1},{2,6},{6,2},{3,7},{7,3},{8,12},{12,8},{9,1... | collective-permute-start | bytes 995336 | tf_op jit(solution)/shard_map/ppermute | solution.py:517
  80.2 1.6 %collective-permute-done.1.other_ref = bf16[144,1152]{1,0:T(8,128)(2,1)S(1)} collective-permute-done((bf16[144,1152]{1,0:T(8,128)(2,1)S(1)}, bf16[144,1152]{1,0:T(8,128)(2,1)S(1)}, u32[]{:S(2)}, u32[]{:S(2)}) %collective-permute-start.1) | collective-permute-done | bytes 331808 | tf_op jit(solution)/shard_map/ppermute | solution.py:517
  81.8 3.6 %text_tile.1 = (f32[64,1024]{1,0:T(8,128)S(1)}, bf16[64,1024]{1,0:T(8,128)(2,1)S(1)}, f32[8,1024]{1,0:T(8,128)S(1)}) custom-call(s32[5]{0:T(128)S(1)} %stack.32.place_ref, bf16[144,1152]{1,0:T(8,128)(2,1)S(1)} %get-tuple-element.41.own_ref, bf16[144,1152]{1,0:T(8,128)(2,1)S(1)} %collective-permute-done.1.other_ref, f32[8,1024]{1,0:T(8,128)S(1)} %get-tuple-element.43.unit_ref), custom_call_target="tpu_custom_call" | custom-call | bytes 14400000 | tf_op jit(solution)/shard_map/text_tile/pallas_call | solution.py:419
  85.4 4.7 %all-to-all-done.3 = bf16[16,8,1408]{2,1,0:T(8,128)(2,1)S(1)} async-done(((bf16[16,8,1408]{2,1,0:T(8,128)(2,1)}), bf16[16,8,1408]{2,1,0:T(8,128)(2,1)S(1)}, u32[]{:S(2)}, u32[]{:S(2)}) %all-to-all-start.3) | async-done | bytes 360480 | tf_op jit(solution)/shard_map/all_to_all | solution.py:41
  90.1 3.4 %collective-permute-start.2 = (bf16[64,1024]{1,0:T(8,128)(2,1)S(1)}, bf16[64,1024]{1,0:T(8,128)(2,1)S(1)}, u32[]{:S(2)}, u32[]{:S(2)}) collective-permute-start(bf16[64,1024]{1,0:T(8,128)(2,1)S(1)} %get-tuple-element.50), channel_id=1, source_target_pairs={{0,8},{8,0},{1,9},{9,1},{2,10},{10,2},{3,11},{11,3},{4,12},{12,4},... | collective-permute-start | bytes 393224 | tf_op jit(solution)/shard_map/ppermute | solution.py:521
  93.6 1.5 %fresh_back.1 = f32[4,1,1280]{2,1,0:T(1,128)} custom-call(s32[5]{0:T(128)S(1)} %stack.32.place_ref, bf16[128,1408]{1,0:T(8,128)(2,1)S(1)} %bitcast.23, bf16[128,2432]{1,0:T(8,128)(2,1)S(1)} %bitcast.22, bf16[128,2432]{1,0:T(8,128)(2,1)S(1)} %collective-permute-done.far_ref, f32[8,1024]{1,0:T(8,128)S(1)} %get-tuple-element.43.unit_ref, ...), custom_call_target="tpu_custom_call" | custom-call | bytes 7200000 | tf_op jit(solution)/shard_map/fresh_back/pallas_call | solution.py:378
  95.0 3.3 %all-to-all-start.4 = ((f32[4,1,1280]{2,1,0:T(1,128)}), f32[4,1,1280]{2,1,0:T(1,128)S(1)}, u32[]{:S(2)}, u32[]{:S(2)}) async-start(f32[4,1,1280]{2,1,0:T(1,128)} %fresh_back.1), calls=%async_computation.4 | async-start | bytes 40960 | tf_op jit(solution)/shard_map/all_to_all | solution.py:522
  98.3 0.0 copy-done
  98.3 1.3 %image_end.1 = (f32[8,1024]{1,0:T(8,128)}, f32[8,1]{1,0:T(8,128)S(1)}) custom-call(s32[5]{0:T(128)S(1)} %stack.32.place_ref, bf16[128,1408]{1,0:T(8,128)(2,1)S(1)} %bitcast.24, bf16[8,1024]{1,0:T(8,128)(2,1)S(1)} %copy-done, f32[8,1024]{1,0:T(8,128)S(1)} %get-tuple-element.51.plain_ref, f32[8,128]{1,0:T(8,128)S(1)} %get-tuple-element.48.norm_ref), custom_call_target="tpu_custom_call" | custom-call | bytes 3600000 | tf_op jit(solution)/shard_map/image_end/pallas_call | solution.py:454
  99.7 0.0 copy-start.1
  99.7 2.0 %collective-permute-done.2 = bf16[64,1024]{1,0:T(8,128)(2,1)S(1)} collective-permute-done((bf16[64,1024]{1,0:T(8,128)(2,1)S(1)}, bf16[64,1024]{1,0:T(8,128)(2,1)S(1)}, u32[]{:S(2)}, u32[]{:S(2)}) %collective-permute-start.2) | collective-permute-done | bytes 131104 | tf_op jit(solution)/shard_map/ppermute | solution.py:521
  101.6 0.7 add_convert_fusion
  102.3 1.3 %all-to-all-done.4.z_ref = f32[4,1,1280]{2,1,0:T(1,128)S(1)} async-done(((f32[4,1,1280]{2,1,0:T(1,128)}), f32[4,1,1280]{2,1,0:T(1,128)S(1)}, u32[]{:S(2)}, u32[]{:S(2)}) %all-to-all-start.4) | async-done | bytes 20512 | tf_op jit(solution)/shard_map/all_to_all | solution.py:522
  103.7 0.0 copy-start.3
  103.7 4.1 %all-to-all-start.5 = ((bf16[8,8,1024]{2,1,0:T(8,128)(2,1)}), bf16[8,8,1024]{2,1,0:T(8,128)(2,1)S(1)}, u32[]{:S(2)}, u32[]{:S(2)}) async-start(bf16[8,8,1024]{2,1,0:T(8,128)(2,1)} %bitcast.14), calls=%async_computation.5 | async-start | bytes 262144 | tf_op jit(solution)/shard_map/all_to_all | solution.py:41
  107.8 0.6 reduce
  108.4 0.0 copy-done.3
  108.4 8.0 %attend_back.1 = (bf16[1,257,1280]{2,1,0:T(8,128)(2,1)}, bf16[1,257,1280]{2,1,0:T(8,128)(2,1)}, bf16[1,257,1280]{2,1,0:T(8,128)(2,1)}) custom-call(f32[4,1,1280]{2,1,0:T(1,128)} %copy-done.3, bf16[1,257,1280]{2,1,0:T(8,128)(2,1)} %q_ref.3, bf16[1,257,1280]{2,1,0:T(8,128)(2,1)} %k_ref.3, bf16[1,257,1280]{2,1,0:T(8,128)(2,1)} %v_ref.3, ...), custom_call_target="tpu_custom_call" | custom-call | bytes 21600000 | tf_op jit(solution)/shard_map/attend_back/pallas_call | solution.py:140
  116.4 0.0 all-to-all-done.5
  116.4 0.0 copy-done.1
  116.4 0.8 text_end.1
Async XLA Ops:
  2.4 32.8 %all-to-all-start = ((bf16[16,8,2432]{2,1,0:T(8,128)(2,1)}), bf16[16,8,2432]{2,1,0:T(8,128)(2,1)S(1)}, u32[]{:S(2)}, u32[]{:S(2)}) async-start(bf16[16,8,2432]{2,1,0:T(8,128)(2,1)} %bitcast.27), calls=%async_computation | async-start | bytes 1245184 | tf_op jit(solution)/shard_map/all_to_all | solution.py:41
  35.2 11.7 %collective-permute-start = (bf16[128,2432]{1,0:T(8,128)(2,1)S(1)}, bf16[128,2432]{1,0:T(8,128)(2,1)S(1)}, u32[]{:S(2)}, u32[]{:S(2)}) collective-permute-start(bf16[128,2432]{1,0:T(8,128)(2,1)S(1)} %bitcast.18), channel_id=1, source_target_pairs={{0,4},{4,0},{1,5},{5,1},{2,6},{6,2},{3,7},{7,3},{8,12},{12,8},{9,1... | collective-permute-start | bytes 1867784 | tf_op jit(solution)/shard_map/ppermute | solution.py:509
  46.8 0.8 copy-start.2
  48.6 49.7 %copy-start = (bf16[8,1024]{1,0:T(8,128)(2,1)S(1)}, bf16[8,1024]{1,0:T(8,128)(2,1)}, u32[]{:S(2)}) copy-start(bf16[8,1024]{1,0:T(8,128)(2,1)} %cache_ref.3) | copy-start | bytes 49156
  48.6 23.6 %all-to-all-start.2 = ((bf16[16,8,1408]{2,1,0:T(8,128)(2,1)}), bf16[16,8,1408]{2,1,0:T(8,128)(2,1)S(1)}, u32[]{:S(2)}, u32[]{:S(2)}) async-start(bf16[16,8,1408]{2,1,0:T(8,128)(2,1)} %bitcast.10), calls=%async_computation.2 | async-start | bytes 720896 | tf_op jit(solution)/shard_map/all_to_all | solution.py:41
  74.7 15.4 %all-to-all-start.3 = ((bf16[16,8,1408]{2,1,0:T(8,128)(2,1)}), bf16[16,8,1408]{2,1,0:T(8,128)(2,1)S(1)}, u32[]{:S(2)}, u32[]{:S(2)}) async-start(bf16[16,8,1408]{2,1,0:T(8,128)(2,1)} %bitcast.12), calls=%async_computation.3 | async-start | bytes 720896 | tf_op jit(solution)/shard_map/all_to_all | solution.py:41
  78.3 3.5 %collective-permute-start.1 = (bf16[144,1152]{1,0:T(8,128)(2,1)S(1)}, bf16[144,1152]{1,0:T(8,128)(2,1)S(1)}, u32[]{:S(2)}, u32[]{:S(2)}) collective-permute-start(bf16[144,1152]{1,0:T(8,128)(2,1)S(1)} %get-tuple-element.42), channel_id=1, source_target_pairs={{0,4},{4,0},{1,5},{5,1},{2,6},{6,2},{3,7},{7,3},{8,12},{12,8},{9,1... | collective-permute-start | bytes 995336 | tf_op jit(solution)/shard_map/ppermute | solution.py:517
  90.1 11.5 %collective-permute-start.2 = (bf16[64,1024]{1,0:T(8,128)(2,1)S(1)}, bf16[64,1024]{1,0:T(8,128)(2,1)S(1)}, u32[]{:S(2)}, u32[]{:S(2)}) collective-permute-start(bf16[64,1024]{1,0:T(8,128)(2,1)S(1)} %get-tuple-element.50), channel_id=1, source_target_pairs={{0,8},{8,0},{1,9},{9,1},{2,10},{10,2},{3,11},{11,3},{4,12},{12,4},... | collective-permute-start | bytes 393224 | tf_op jit(solution)/shard_map/ppermute | solution.py:521
  95.0 8.6 %all-to-all-start.4 = ((f32[4,1,1280]{2,1,0:T(1,128)}), f32[4,1,1280]{2,1,0:T(1,128)S(1)}, u32[]{:S(2)}, u32[]{:S(2)}) async-start(f32[4,1,1280]{2,1,0:T(1,128)} %fresh_back.1), calls=%async_computation.4 | async-start | bytes 40960 | tf_op jit(solution)/shard_map/all_to_all | solution.py:522
  99.7 16.8 %copy-start.1 = (bf16[8,1024]{1,0:T(8,128)(2,1)S(1)}, bf16[8,1024]{1,0:T(8,128)(2,1)}, u32[]{:S(2)}) copy-start(bf16[8,1024]{1,0:T(8,128)(2,1)} %embed_ref.1) | copy-start | bytes 49156
  103.7 4.8 %copy-start.3 = (f32[4,1,1280]{2,1,0:T(1,128)}, f32[4,1,1280]{2,1,0:T(1,128)S(1)}, u32[]{:S(2)}) copy-start(f32[4,1,1280]{2,1,0:T(1,128)S(1)} %all-to-all-done.4.z_ref) | copy-start | bytes 61444
  103.7 12.8 %all-to-all-start.5 = ((bf16[8,8,1024]{2,1,0:T(8,128)(2,1)}), bf16[8,8,1024]{2,1,0:T(8,128)(2,1)S(1)}, u32[]{:S(2)}, u32[]{:S(2)}) async-start(bf16[8,8,1024]{2,1,0:T(8,128)(2,1)} %bitcast.14), calls=%async_computation.5 | async-start | bytes 262144 | tf_op jit(solution)/shard_map/all_to_all | solution.py:41

commit v5 on v4

--- a/solution.py
+++ b/solution.py
@@ -77,19 +77,27 @@
     def _():
         pooled_ref[...] = jnp.zeros_like(pooled_ref)
 
-    ones = jnp.ones((SEQ, HEAD_DIM), BF16)
+    row = rows((8, SEQ))
     for one in range(PAIRED):
         at = slice(one * HEAD_DIM, (one + 1) * HEAD_DIM)
-        scores = contract(q_ref[0, :, at], k_ref[0, :, at], ((1,), (1,))) * INV_ROOT
-        raised = jnp.exp(scores - jnp.max(scores, axis=1, keepdims=True))
-        probs = raised / jnp.sum(raised, axis=1, keepdims=True)
+        scores = contract(q_ref[0, :, at], k_ref[0, :, at], ((1,), (1,)))
+        scores = scores - jnp.max(scores, axis=1, keepdims=True)
+        raised = jnp.exp2(scores * (INV_ROOT * math.log2(math.e)))
+        probs = raised * (1.0 / jnp.sum(raised, axis=1, keepdims=True))
         probs_ref[one] = probs
-        mass = contract(probs.astype(BF16), ones, ((0,), (0,)))
-        mass_ref[:, at] = mass
-        pooled = jnp.sum(mass * v_ref[0, :, at].astype(F32), axis=0, keepdims=True)
+        rest = jnp.sum(probs.astype(BF16).astype(F32), axis=0, keepdims=True)
+        mass = jnp.zeros((8, SEQ), F32)
+        for place in range(3):
+            piece = rest.astype(BF16).astype(F32)
+            mass = jnp.where(row == place, piece, mass)
+            rest = rest - piece
+        mass = mass.astype(BF16)
+        mass_ref[one] = mass
+        pooled = jnp.sum(
+            contract(mass, v_ref[0, :, at], ((1,), (0,))), axis=0, keepdims=True
+        )
         pooled = (pooled * (1.0 / SEQ)).astype(BF16).astype(F32)
-        for copy in range(4):
-            pooled_ref[copy, pl.ds(step * PAIRED + one, 1), :] = pooled
+        pooled_ref[pl.ds(step * PAIRED + one, 1), :] = pooled
 
 
 def attend(query_tokens, key_tokens, value_tokens):
@@ -101,13 +109,13 @@
         in_specs=[tokens] * 3,
         out_specs=[
             pl.BlockSpec((PAIRED, SEQ, SEQ), lambda i: (i, 0, 0)),
-            pl.BlockSpec((SEQ, wide), lambda i: (0, i)),
-            pl.BlockSpec((4, 16, HEAD_DIM), lambda i: (0, 0, 0)),
+            pl.BlockSpec((PAIRED, 8, SEQ), lambda i: (i, 0, 0)),
+            pl.BlockSpec((16, HEAD_DIM), lambda i: (0, 0)),
         ],
         out_shape=[
             jax.ShapeDtypeStruct((HEADS, SEQ, SEQ), F32),
-            jax.ShapeDtypeStruct((SEQ, WIDTH), F32),
-            jax.ShapeDtypeStruct((4, 16, HEAD_DIM), F32),
+            jax.ShapeDtypeStruct((HEADS, 8, SEQ), BF16),
+            jax.ShapeDtypeStruct((16, HEAD_DIM), F32),
         ],
         compiler_params=STREAMED,
         cost_estimate=lasting(7),
@@ -121,7 +129,7 @@
         at = slice(one * HEAD_DIM, (one + 1) * HEAD_DIM)
         cot_row = cot[:, at]
         probs = probs_ref[one]
-        cot_rows = jnp.broadcast_to(cot_row, (8, HEAD_DIM))
+        cot_rows = jnp.broadcast_to(cot_row.astype(F32), (8, HEAD_DIM)).astype(BF16)
         prob_grad = contract(cot_rows, v_ref[0, :, at], ((1,), (1,)))[:1]
         centre = jnp.sum(probs * prob_grad, axis=1, keepdims=True)
         score_grad = (probs * (prob_grad - centre)).astype(BF16)
@@ -131,7 +139,7 @@
         dk_ref[0, :, at] = (contract(score_grad, q_ref[0, :, at], ((0,), (0,))) * INV_ROOT).astype(
             BF16
         )
-        dv_ref[0, :, at] = (mass_ref[:, at] * cot_row.astype(F32)).astype(BF16)
+        dv_ref[0, :, at] = contract(mass_ref[one], cot_rows, ((0,), (0,))).astype(BF16)
 
 
 def attend_back(pooled_grad, query_tokens, key_tokens, value_tokens, probs, mass):
@@ -146,7 +154,7 @@
             tokens,
             tokens,
             pl.BlockSpec((PAIRED, SEQ, SEQ), lambda i: (i, 0, 0)),
-            pl.BlockSpec((SEQ, wide), lambda i: (0, i)),
+            pl.BlockSpec((PAIRED, 8, SEQ), lambda i: (i, 0, 0)),
         ],
         out_specs=[tokens] * 3,
         out_shape=[jax.ShapeDtypeStruct((1, SEQ, WIDTH), BF16)] * 3,
@@ -198,9 +206,17 @@
     )(pair, igroup, tgroup, text, cache, weight)
 
 
-def fresh_kernel(pooled_ref, near_ref, far_ref, stem_ref, out_ref):
+def fresh_kernel(place_ref, p0_ref, p1_ref, p2_ref, p3_ref, near_ref, far_ref, stem_ref, out_ref):
+    x = place_ref[1]
+    shifted = [ref[...] for ref in (p0_ref, p1_ref, p2_ref, p3_ref)]
+    images = []
+    for image in range(4):
+        chosen = shifted[0]
+        for shift in range(1, 4):
+            chosen = jnp.where((x + shift) % 4 == image, shifted[shift], chosen)
+        images.append(chosen)
     heads = [
-        jnp.concatenate([pooled_ref[b, i : i + 1, :] for b in (0, 1, 2, 3) * 2], axis=0)
+        jnp.concatenate([images[b][i : i + 1, :] for b in (0, 1, 2, 3) * 2], axis=0)
         for i in range(HEADS)
     ]
     pooled = jnp.concatenate(heads, axis=1).astype(BF16)
@@ -215,16 +231,16 @@
         out_ref[i * 16 : i * 16 + 16, STEM:] = packed
 
 
-def fresh_message(pooled, near, far, stem):
+def fresh_message(place, pooled, near, far, stem):
     return pl.pallas_call(
         fresh_kernel,
-        in_specs=[VMEM] * 4,
+        in_specs=[SMEM] + [VMEM] * 7,
         out_specs=VMEM,
         out_shape=jax.ShapeDtypeStruct((128, STEM + 256), BF16),
         compiler_params=PARAMS,
         cost_estimate=lasting(1),
         name="fresh_message",
-    )(pooled, near, far, stem)
+    )(place, *pooled, near, far, stem)
 
 
 def order_of(c):
@@ -388,18 +404,19 @@
 
 def text_kernel(place_ref, own_ref, other_ref, unit_ref, keep_ref, send_ref, plain_ref):
     h, c = place_ref[2], place_ref[3]
+    theirs = other_ref[128:, 128:].astype(F32)[:8]
+    theirs = jnp.concatenate(
+        [theirs[:, (i ^ 1) * 128 : (i ^ 1) * 128 + 128] for i in range(8)], axis=1
+    )
+    pieces, rest = [], unit_ref[...]
+    for _ in range(3):
+        pieces.append(rest.astype(BF16).astype(F32))
+        rest = rest - pieces[-1]
+    turned = jnp.concatenate(pieces + [theirs], axis=0).astype(BF16)
+    plain = contract(turned, order_of(c), ((1,), (1,)))
+    plain_ref[...] = plain[:8] + (plain[8:16] + plain[16:24])
     total = jnp.zeros((128, EMBED), F32)
-    for ref, core in ((own_ref, c), (other_ref, 1 - c)):
-        order = order_of(core)
-        if ref is own_ref:
-            rest = unit_ref[...]
-            plain = jnp.zeros((8, EMBED), F32)
-            for _ in range(3):
-                piece = rest.astype(BF16)
-                rest -= piece.astype(F32)
-                plain += contract(piece, order, ((1,), (1,)))
-            plain_ref[...] = plain
-        fresh_low = contract(ref[128:, 128:], order, ((1,), (1,)))
+    for ref, fresh_low in ((own_ref, plain[:8]), (other_ref, plain[24:])):
         repeated = jnp.concatenate(
             [jnp.broadcast_to(fresh_low[i : i + 1], (32, EMBED)) for i in range(4)], axis=0
         )
@@ -447,7 +464,9 @@
     grad_ref[...] = (
         direction - unit * jnp.sum(unit * direction, axis=1, keepdims=True)
     ) * norm
-    loss_ref[...] = total[:, EMBED : EMBED + 1] + total[:, EMBED + 1 : EMBED + 2]
+    loss = total[:, EMBED : EMBED + 1] + total[:, EMBED + 1 : EMBED + 2]
+    here = rows((8, 8)) == lanes((8, 8))
+    loss_ref[...] = jnp.sum(jnp.where(here, loss, 0.0), axis=0, keepdims=True)
 
 
 def image_end(place, got, cache, plain, norm):
@@ -457,7 +476,7 @@
         out_specs=[VMEM] * 2,
         out_shape=[
             jax.ShapeDtypeStruct((8, EMBED), F32),
-            jax.ShapeDtypeStruct((8, 1), F32),
+            jax.ShapeDtypeStruct((1, 8), F32),
         ],
         compiler_params=PARAMS,
         cost_estimate=lasting(1),
@@ -505,12 +524,14 @@
     )
     near = exchange(message, TEXT_AXES, 16)
     probs, mass, pooled = attend(query_tokens, key_tokens, value_tokens)
+    pooled = [pooled] + [
+        lax.ppermute(pooled, "x", [((i + s) % 4, i) for i in range(4)]) for s in range(1, 4)
+    ]
     near, pooled = lax.optimization_barrier((near, pooled))
     far = lax.ppermute(near, "c", SWAP)
     turned = turn(place, near, far)
 
-    pooled_all = lax.all_to_all(pooled, "x", 0, 0)
-    message = fresh_message(pooled_all, near, far, stem)
+    message = fresh_message(place, pooled, near, far, stem)
     image_got = exchange(message, IMAGE_AXES, 16)
 
     back, own, other, unit, norm = pair_tile(place, scalars, image_got, near, far, turned)

time: 118 us -> 117 us (level)
  the two profiles are of different devices: /device:TPU:64 before, /device:TPU:2 now
where the time goes in v5:
time: 117 us; the launch traced here: 116 us
  starting transfers between devices  63 us (54%)
  Pallas kernels  27.8 us (24%)
  waiting for transfers between devices  20.4 us (17%)
  between operations  2.04 us (2%)
  local copies, waits for them, and re-layouts  1.56 us (1%)
    all_to_all x4, starting transfers between devices, exchange(): return lax.all_to_all(sent, axes, 0, 0).reshape(blocks.shape)  39.3 us
    all_to_all x4, waiting for transfers between devices, exchange(): return lax.all_to_all(sent, axes, 0, 0).reshape(blocks.shape)  13.3 us
    ppermute x3, starting transfers between devices, on_device(): lax.ppermute(pooled, 'x', [((i + s) % 4, i) for i in range(4)])  10.5 us
    pallas_call x1, Pallas kernels, attend_back(): pl.pallas_call(attend_back_kernel, grid=(HEADS // PAIRED,), in_specs=[pl....  8.23 us
    pallas_call x1, Pallas kernels, attend(): pl.pallas_call(attend_kernel, grid=(HEADS // PAIRED,), in_specs=[tokens]...  6.97 us
    all_to_all x1, starting transfers between devices, on_device(): lax.all_to_all(fresh_back(place, back, near, far, unit, norm), 'x', 0, 0)  6.03 us
    ppermute x1, starting transfers between devices, on_device(): text_part = (keep + lax.ppermute(send, 'h', SWAP).astype(F32)).astype(BF16)  3.4 us
    pallas_call x1, Pallas kernels, pair_tile(): pl.pallas_call(pair_kernel, in_specs=[SMEM, SMEM, VMEM, VMEM, VMEM, VMEM]...  2.45 us
  transfers between devices with their start and end apart: 11, of which 9 were waited for; matrix products, arithmetic and copies ran while one was open for 1% of the time, Pallas kernels for 18%

profile of v5, /device:TPU:2, one launch (start us, length us, event | category | flops | bytes accessed | tf_op | source)
XLA Modules:
  0.0 115.5 jit_solution(1064186873973288694)
XLA Ops:
  0.6 1.8 %first_messages.1 = (bf16[128,2432]{1,0:T(8,128)(2,1)}, bf16[16,1152]{1,0:T(8,128)(2,1)}) custom-call(s32[8]{0:T(128)} %pair_ref.1, s32[8]{0:T(128)} %igroup_ref.1, s32[8]{0:T(128)} %tgroup_ref.1, bf16[8,1024]{1,0:T(8,128)(2,1)} %embed_ref.1, bf16[8,1024]{1,0:T(8,128)(2,1)} %cache_ref.3, bf16[8,1280]{1,0:T(8,128)(2,1)} %bitcast.29), custom_call_target="tpu_custom_call" | custom-call | bytes 3600000 | tf_op jit(solution)/shard_map/first_messages/pallas_call | solution.py:195
  2.4 15.7 %all-to-all-start = ((bf16[16,8,2432]{2,1,0:T(8,128)(2,1)}), bf16[16,8,2432]{2,1,0:T(8,128)(2,1)S(1)}, u32[]{:S(2)}, u32[]{:S(2)}) async-start(bf16[16,8,2432]{2,1,0:T(8,128)(2,1)} %bitcast.28), calls=%async_computation | async-start | bytes 1245184 | tf_op jit(solution)/shard_map/all_to_all | solution.py:41
  18.1 7.0 %attend.1 = (f32[10,257,257]{2,1,0:T(8,128)}, bf16[10,8,257]{2,1,0:T(8,128)(2,1)}, f32[16,128]{1,0:T(8,128)}) custom-call(bf16[1,257,1280]{2,1,0:T(8,128)(2,1)} %q_ref.3, bf16[1,257,1280]{2,1,0:T(8,128)(2,1)} %k_ref.3, bf16[1,257,1280]{2,1,0:T(8,128)(2,1)} %v_ref.3), custom_call_target="tpu_custom_call" | custom-call | bytes 25200000 | tf_op jit(solution)/shard_map/attend/pallas_call | solution.py:106
  25.1 3.4 %collective-permute-start.2 = (f32[16,128]{1,0:T(8,128)}, f32[16,128]{1,0:T(8,128)S(1)}, u32[]{:S(2)}, u32[]{:S(2)}) collective-permute-start(f32[16,128]{1,0:T(8,128)} %get-tuple-element.40.p0_ref), channel_id=1, source_target_pairs={{48,0},{0,16},{16,32},{32,48},{49,1},{1,17},{17,33},{33,49},{50,2}... | collective-permute-start | bytes 24584 | tf_op jit(solution)/shard_map/ppermute | solution.py:528
  28.5 3.0 %collective-permute-start.1 = (f32[16,128]{1,0:T(8,128)}, f32[16,128]{1,0:T(8,128)S(1)}, u32[]{:S(2)}, u32[]{:S(2)}) collective-permute-start(f32[16,128]{1,0:T(8,128)} %get-tuple-element.40.p0_ref), channel_id=1, source_target_pairs={{32,0},{48,16},{0,32},{16,48},{33,1},{49,17},{1,33},{17,49},{34,2}... | collective-permute-start | bytes 24584 | tf_op jit(solution)/shard_map/ppermute | solution.py:528
  31.5 4.1 %collective-permute-start = (f32[16,128]{1,0:T(8,128)}, f32[16,128]{1,0:T(8,128)S(1)}, u32[]{:S(2)}, u32[]{:S(2)}) collective-permute-start(f32[16,128]{1,0:T(8,128)} %get-tuple-element.40.p0_ref), channel_id=1, source_target_pairs={{16,0},{32,16},{48,32},{0,48},{17,1},{33,17},{49,33},{1,49},{18,2}... | collective-permute-start | bytes 24584 | tf_op jit(solution)/shard_map/ppermute | solution.py:528
  35.5 0.0 collective-permute-done.2.p3_ref
  35.6 0.2 collective-permute-done.1.p2_ref
  35.7 1.5 %collective-permute-done.p1_ref = f32[16,128]{1,0:T(8,128)S(1)} collective-permute-done((f32[16,128]{1,0:T(8,128)}, f32[16,128]{1,0:T(8,128)S(1)}, u32[]{:S(2)}, u32[]{:S(2)}) %collective-permute-start) | collective-permute-done | bytes 8224 | tf_op jit(solution)/shard_map/ppermute | solution.py:528
  37.2 0.0 all-to-all-done
  37.2 1.9 %collective-permute-start.3 = (bf16[128,2432]{1,0:T(8,128)(2,1)S(1)}, bf16[128,2432]{1,0:T(8,128)(2,1)S(1)}, u32[]{:S(2)}, u32[]{:S(2)}) collective-permute-start(bf16[128,2432]{1,0:T(8,128)(2,1)S(1)} %bitcast.19), channel_id=1, source_target_pairs={{0,4},{4,0},{1,5},{5,1},{2,6},{6,2},{3,7},{7,3},{8,12},{12,8},{9,1... | collective-permute-start | bytes 1867784 | tf_op jit(solution)/shard_map/ppermute | solution.py:531
  39.2 0.1 stack.32.place_ref
  39.2 1.9 %collective-permute-done.3.far_ref = bf16[128,2432]{1,0:T(8,128)(2,1)S(1)} collective-permute-done((bf16[128,2432]{1,0:T(8,128)(2,1)S(1)}, bf16[128,2432]{1,0:T(8,128)(2,1)S(1)}, u32[]{:S(2)}, u32[]{:S(2)}) %collective-permute-start.3) | collective-permute-done | bytes 622624 | tf_op jit(solution)/shard_map/ppermute | solution.py:531
  41.2 0.0 copy-start.2
  41.2 0.8 copy-done.2
  41.9 0.0 copy-start.3
  41.9 0.7 copy-done.3
  42.6 1.6 %fresh_message.1 = bf16[128,1408]{1,0:T(8,128)(2,1)} custom-call(s32[5]{0:T(128)S(1)} %stack.32.place_ref, f32[16,128]{1,0:T(8,128)S(1)} %copy-done.3, f32[16,128]{1,0:T(8,128)S(1)} %collective-permute-done.p1_ref, f32[16,128]{1,0:T(8,128)S(1)} %collective-permute-done.1.p2_ref, f32[16,128]{1,0:T(8,128)S(1)} %collective-permute-done.2.p3_ref, ...), custom_call_target="tpu_custom_call" | custom-call | bytes 3600000 | tf_op jit(solution)/shard_map/fresh_message/pallas_call | solution.py:235
  44.2 0.0 copy-start
  44.2 11.8 %all-to-all-start.1 = ((bf16[16,8,1408]{2,1,0:T(8,128)(2,1)}), bf16[16,8,1408]{2,1,0:T(8,128)(2,1)S(1)}, u32[]{:S(2)}, u32[]{:S(2)}) async-start(bf16[16,8,1408]{2,1,0:T(8,128)(2,1)} %bitcast.10), calls=%async_computation.1 | async-start | bytes 720896 | tf_op jit(solution)/shard_map/all_to_all | solution.py:41
  57.3 0.1 pad_maximum_fusion.scalar_ref
  57.4 1.6 %turn.1.turned_ref = bf16[256,1024]{1,0:T(8,128)(2,1)S(1)} custom-call(s32[5]{0:T(128)S(1)} %stack.32.place_ref, bf16[128,2432]{1,0:T(8,128)(2,1)S(1)} %bitcast.21, bf16[128,2432]{1,0:T(8,128)(2,1)S(1)} %collective-permute-done.3.far_ref), custom_call_target="tpu_custom_call" | custom-call | bytes 10800000 | tf_op jit(solution)/shard_map/turn/pallas_call | solution.py:265
  59.0 7.7 %all-to-all-done.1 = bf16[16,8,1408]{2,1,0:T(8,128)(2,1)S(1)} async-done(((bf16[16,8,1408]{2,1,0:T(8,128)(2,1)}), bf16[16,8,1408]{2,1,0:T(8,128)(2,1)S(1)}, u32[]{:S(2)}, u32[]{:S(2)}) %all-to-all-start.1) | async-done | bytes 360480 | tf_op jit(solution)/shard_map/all_to_all | solution.py:41
  66.7 2.5 %pair_tile.1 = (bf16[128,1408]{1,0:T(8,128)(2,1)}, bf16[144,1152]{1,0:T(8,128)(2,1)S(1)}, bf16[144,1152]{1,0:T(8,128)(2,1)S(1)}, f32[8,1024]{1,0:T(8,128)S(1)}, f32[8,128]{1,0:T(8,128)S(1)}) custom-call(s32[5]{0:T(128)S(1)} %stack.32.place_ref, f32[2]{0:T(128)S(1)} %pad_maximum_fusion.scalar_ref, bf16[128,1408]{1,0:T(8,128)(2,1)S(1)} %bitcast.26, ...), custom_call_target="tpu_custom_call" | custom-call | bytes 10800000 | tf_op jit(solution)/shard_map/pair_tile/pallas_call | solution.py:363
  69.2 6.0 %all-to-all-start.2 = ((bf16[16,8,1408]{2,1,0:T(8,128)(2,1)}), bf16[16,8,1408]{2,1,0:T(8,128)(2,1)S(1)}, u32[]{:S(2)}, u32[]{:S(2)}) async-start(bf16[16,8,1408]{2,1,0:T(8,128)(2,1)} %bitcast.12), calls=%async_computation.2 | async-start | bytes 720896 | tf_op jit(solution)/shard_map/all_to_all | solution.py:41
  75.2 1.9 %collective-permute-start.4 = (bf16[144,1152]{1,0:T(8,128)(2,1)S(1)}, bf16[144,1152]{1,0:T(8,128)(2,1)S(1)}, u32[]{:S(2)}, u32[]{:S(2)}) collective-permute-start(bf16[144,1152]{1,0:T(8,128)(2,1)S(1)} %get-tuple-element.48), channel_id=1, source_target_pairs={{0,4},{4,0},{1,5},{5,1},{2,6},{6,2},{3,7},{7,3},{8,12},{12,8},{9,1... | collective-permute-start | bytes 995336 | tf_op jit(solution)/shard_map/ppermute | solution.py:538
  77.1 1.6 %collective-permute-done.4.other_ref = bf16[144,1152]{1,0:T(8,128)(2,1)S(1)} collective-permute-done((bf16[144,1152]{1,0:T(8,128)(2,1)S(1)}, bf16[144,1152]{1,0:T(8,128)(2,1)S(1)}, u32[]{:S(2)}, u32[]{:S(2)}) %collective-permute-start.4) | collective-permute-done | bytes 331808 | tf_op jit(solution)/shard_map/ppermute | solution.py:538
  78.7 1.5 %text_tile.1 = (f32[64,1024]{1,0:T(8,128)S(1)}, bf16[64,1024]{1,0:T(8,128)(2,1)S(1)}, f32[8,1024]{1,0:T(8,128)S(1)}) custom-call(s32[5]{0:T(128)S(1)} %stack.32.place_ref, bf16[144,1152]{1,0:T(8,128)(2,1)S(1)} %get-tuple-element.47.own_ref, bf16[144,1152]{1,0:T(8,128)(2,1)S(1)} %collective-permute-done.4.other_ref, f32[8,1024]{1,0:T(8,128)S(1)} %get-tuple-element.49.unit_ref), custom_call_target="tpu_custom_call" | custom-call | bytes 14400000 | tf_op jit(solution)/shard_map/text_tile/pallas_call | solution.py:436
  80.3 4.8 %all-to-all-done.2 = bf16[16,8,1408]{2,1,0:T(8,128)(2,1)S(1)} async-done(((bf16[16,8,1408]{2,1,0:T(8,128)(2,1)}), bf16[16,8,1408]{2,1,0:T(8,128)(2,1)S(1)}, u32[]{:S(2)}, u32[]{:S(2)}) %all-to-all-start.2) | async-done | bytes 360480 | tf_op jit(solution)/shard_map/all_to_all | solution.py:41
  85.1 3.4 %collective-permute-start.5 = (bf16[64,1024]{1,0:T(8,128)(2,1)S(1)}, bf16[64,1024]{1,0:T(8,128)(2,1)S(1)}, u32[]{:S(2)}, u32[]{:S(2)}) collective-permute-start(bf16[64,1024]{1,0:T(8,128)(2,1)S(1)} %get-tuple-element.56), channel_id=1, source_target_pairs={{0,8},{8,0},{1,9},{9,1},{2,10},{10,2},{3,11},{11,3},{4,12},{12,4},... | collective-permute-start | bytes 393224 | tf_op jit(solution)/shard_map/ppermute | solution.py:542
  88.5 1.5 %fresh_back.1 = f32[4,1,1280]{2,1,0:T(1,128)} custom-call(s32[5]{0:T(128)S(1)} %stack.32.place_ref, bf16[128,1408]{1,0:T(8,128)(2,1)S(1)} %bitcast.24, bf16[128,2432]{1,0:T(8,128)(2,1)S(1)} %bitcast.23, bf16[128,2432]{1,0:T(8,128)(2,1)S(1)} %collective-permute-done.3.far_ref, f32[8,1024]{1,0:T(8,128)S(1)} %get-tuple-element.49.unit_ref, ...), custom_call_target="tpu_custom_call" | custom-call | bytes 7200000 | tf_op jit(solution)/shard_map/fresh_back/pallas_call | solution.py:394
  90.0 0.0 copy-start.1
  90.0 6.0 %all-to-all-start.3 = ((f32[4,1,1280]{2,1,0:T(1,128)}), f32[4,1,1280]{2,1,0:T(1,128)S(1)}, u32[]{:S(2)}, u32[]{:S(2)}) async-start(f32[4,1,1280]{2,1,0:T(1,128)} %fresh_back.1), calls=%async_computation.3 | async-start | bytes 40960 | tf_op jit(solution)/shard_map/all_to_all | solution.py:543
  96.0 0.0 copy-done
  96.0 1.4 %image_end.1 = (f32[8,1024]{1,0:T(8,128)}, f32[1,8]{1,0:T(1,128)}) custom-call(s32[5]{0:T(128)S(1)} %stack.32.place_ref, bf16[128,1408]{1,0:T(8,128)(2,1)S(1)} %bitcast.25, bf16[8,1024]{1,0:T(8,128)(2,1)S(1)} %copy-done, f32[8,1024]{1,0:T(8,128)S(1)} %get-tuple-element.57.plain_ref, f32[8,128]{1,0:T(8,128)S(1)} %get-tuple-element.54.norm_ref), custom_call_target="tpu_custom_call" | custom-call | bytes 3600000 | tf_op jit(solution)/shard_map/image_end/pallas_call | solution.py:473
  97.4 0.5 collective-permute-done.5
  97.9 0.7 add_convert_fusion
  98.5 1.4 %all-to-all-done.3.z_ref = f32[4,1,1280]{2,1,0:T(1,128)S(1)} async-done(((f32[4,1,1280]{2,1,0:T(1,128)}), f32[4,1,1280]{2,1,0:T(1,128)S(1)}, u32[]{:S(2)}, u32[]{:S(2)}) %all-to-all-start.3) | async-done | bytes 20512 | tf_op jit(solution)/shard_map/all_to_all | solution.py:543
  99.9 0.0 copy-start.4
  99.9 5.7 %all-to-all-start.4 = ((bf16[8,8,1024]{2,1,0:T(8,128)(2,1)}), bf16[8,8,1024]{2,1,0:T(8,128)(2,1)S(1)}, u32[]{:S(2)}, u32[]{:S(2)}) async-start(bf16[8,8,1024]{2,1,0:T(8,128)(2,1)} %bitcast.14), calls=%async_computation.4 | async-start | bytes 262144 | tf_op jit(solution)/shard_map/all_to_all | solution.py:41
  105.7 0.0 copy-done.4
  105.7 8.2 %attend_back.1 = (bf16[1,257,1280]{2,1,0:T(8,128)(2,1)}, bf16[1,257,1280]{2,1,0:T(8,128)(2,1)}, bf16[1,257,1280]{2,1,0:T(8,128)(2,1)}) custom-call(f32[4,1,1280]{2,1,0:T(1,128)} %copy-done.4, bf16[1,257,1280]{2,1,0:T(8,128)(2,1)} %q_ref.3, bf16[1,257,1280]{2,1,0:T(8,128)(2,1)} %k_ref.3, bf16[1,257,1280]{2,1,0:T(8,128)(2,1)} %v_ref.3, ...), custom_call_target="tpu_custom_call" | custom-call | bytes 21600000 | tf_op jit(solution)/shard_map/attend_back/pallas_call | solution.py:148
  113.9 0.8 all-to-all-done.4
  114.7 0.0 copy-done.1
  114.7 0.8 text_end.1
Async XLA Ops:
  2.4 34.8 %all-to-all-start = ((bf16[16,8,2432]{2,1,0:T(8,128)(2,1)}), bf16[16,8,2432]{2,1,0:T(8,128)(2,1)S(1)}, u32[]{:S(2)}, u32[]{:S(2)}) async-start(bf16[16,8,2432]{2,1,0:T(8,128)(2,1)} %bitcast.28), calls=%async_computation | async-start | bytes 1245184 | tf_op jit(solution)/shard_map/all_to_all | solution.py:41
  25.1 10.5 %collective-permute-start.2 = (f32[16,128]{1,0:T(8,128)}, f32[16,128]{1,0:T(8,128)S(1)}, u32[]{:S(2)}, u32[]{:S(2)}) collective-permute-start(f32[16,128]{1,0:T(8,128)} %get-tuple-element.40.p0_ref), channel_id=1, source_target_pairs={{48,0},{0,16},{16,32},{32,48},{49,1},{1,17},{17,33},{33,49},{50,2}... | collective-permute-start | bytes 24584 | tf_op jit(solution)/shard_map/ppermute | solution.py:528
  28.5 7.3 %collective-permute-start.1 = (f32[16,128]{1,0:T(8,128)}, f32[16,128]{1,0:T(8,128)S(1)}, u32[]{:S(2)}, u32[]{:S(2)}) collective-permute-start(f32[16,128]{1,0:T(8,128)} %get-tuple-element.40.p0_ref), channel_id=1, source_target_pairs={{32,0},{48,16},{0,32},{16,48},{33,1},{49,17},{1,33},{17,49},{34,2}... | collective-permute-start | bytes 24584 | tf_op jit(solution)/shard_map/ppermute | solution.py:528
  31.5 5.8 %collective-permute-start = (f32[16,128]{1,0:T(8,128)}, f32[16,128]{1,0:T(8,128)S(1)}, u32[]{:S(2)}, u32[]{:S(2)}) collective-permute-start(f32[16,128]{1,0:T(8,128)} %get-tuple-element.40.p0_ref), channel_id=1, source_target_pairs={{16,0},{32,16},{48,32},{0,48},{17,1},{33,17},{49,33},{1,49},{18,2}... | collective-permute-start | bytes 24584 | tf_op jit(solution)/shard_map/ppermute | solution.py:528
  37.2 3.9 %collective-permute-start.3 = (bf16[128,2432]{1,0:T(8,128)(2,1)S(1)}, bf16[128,2432]{1,0:T(8,128)(2,1)S(1)}, u32[]{:S(2)}, u32[]{:S(2)}) collective-permute-start(bf16[128,2432]{1,0:T(8,128)(2,1)S(1)} %bitcast.19), channel_id=1, source_target_pairs={{0,4},{4,0},{1,5},{5,1},{2,6},{6,2},{3,7},{7,3},{8,12},{12,8},{9,1... | collective-permute-start | bytes 1867784 | tf_op jit(solution)/shard_map/ppermute | solution.py:531
  41.2 0.8 copy-start.2
  41.9 0.7 copy-start.3
  44.2 51.8 %copy-start = (bf16[8,1024]{1,0:T(8,128)(2,1)S(1)}, bf16[8,1024]{1,0:T(8,128)(2,1)}, u32[]{:S(2)}) copy-start(bf16[8,1024]{1,0:T(8,128)(2,1)} %cache_ref.3) | copy-start | bytes 49156
  44.2 22.5 %all-to-all-start.1 = ((bf16[16,8,1408]{2,1,0:T(8,128)(2,1)}), bf16[16,8,1408]{2,1,0:T(8,128)(2,1)S(1)}, u32[]{:S(2)}, u32[]{:S(2)}) async-start(bf16[16,8,1408]{2,1,0:T(8,128)(2,1)} %bitcast.10), calls=%async_computation.1 | async-start | bytes 720896 | tf_op jit(solution)/shard_map/all_to_all | solution.py:41
  69.2 15.9 %all-to-all-start.2 = ((bf16[16,8,1408]{2,1,0:T(8,128)(2,1)}), bf16[16,8,1408]{2,1,0:T(8,128)(2,1)S(1)}, u32[]{:S(2)}, u32[]{:S(2)}) async-start(bf16[16,8,1408]{2,1,0:T(8,128)(2,1)} %bitcast.12), calls=%async_computation.2 | async-start | bytes 720896 | tf_op jit(solution)/shard_map/all_to_all | solution.py:41
  75.2 3.5 %collective-permute-start.4 = (bf16[144,1152]{1,0:T(8,128)(2,1)S(1)}, bf16[144,1152]{1,0:T(8,128)(2,1)S(1)}, u32[]{:S(2)}, u32[]{:S(2)}) collective-permute-start(bf16[144,1152]{1,0:T(8,128)(2,1)S(1)} %get-tuple-element.48), channel_id=1, source_target_pairs={{0,4},{4,0},{1,5},{5,1},{2,6},{6,2},{3,7},{7,3},{8,12},{12,8},{9,1... | collective-permute-start | bytes 995336 | tf_op jit(solution)/shard_map/ppermute | solution.py:538
  85.1 12.8 %collective-permute-start.5 = (bf16[64,1024]{1,0:T(8,128)(2,1)S(1)}, bf16[64,1024]{1,0:T(8,128)(2,1)S(1)}, u32[]{:S(2)}, u32[]{:S(2)}) collective-permute-start(bf16[64,1024]{1,0:T(8,128)(2,1)S(1)} %get-tuple-element.56), channel_id=1, source_target_pairs={{0,8},{8,0},{1,9},{9,1},{2,10},{10,2},{3,11},{11,3},{4,12},{12,4},... | collective-permute-start | bytes 393224 | tf_op jit(solution)/shard_map/ppermute | solution.py:542
  90.0 24.8 %copy-start.1 = (bf16[8,1024]{1,0:T(8,128)(2,1)S(1)}, bf16[8,1024]{1,0:T(8,128)(2,1)}, u32[]{:S(2)}) copy-start(bf16[8,1024]{1,0:T(8,128)(2,1)} %embed_ref.1) | copy-start | bytes 49156
  90.0 10.0 %all-to-all-start.3 = ((f32[4,1,1280]{2,1,0:T(1,128)}), f32[4,1,1280]{2,1,0:T(1,128)S(1)}, u32[]{:S(2)}, u32[]{:S(2)}) async-start(f32[4,1,1280]{2,1,0:T(1,128)} %fresh_back.1), calls=%async_computation.3 | async-start | bytes 40960 | tf_op jit(solution)/shard_map/all_to_all | solution.py:543
  99.9 5.7 %copy-start.4 = (f32[4,1,1280]{2,1,0:T(1,128)}, f32[4,1,1280]{2,1,0:T(1,128)S(1)}, u32[]{:S(2)}) copy-start(f32[4,1,1280]{2,1,0:T(1,128)S(1)} %all-to-all-done.3.z_ref) | copy-start | bytes 61444
  99.9 14.8 %all-to-all-start.4 = ((bf16[8,8,1024]{2,1,0:T(8,128)(2,1)}), bf16[8,8,1024]{2,1,0:T(8,128)(2,1)S(1)}, u32[]{:S(2)}, u32[]{:S(2)}) async-start(bf16[8,8,1024]{2,1,0:T(8,128)(2,1)} %bitcast.14), calls=%async_computation.4 | async-start | bytes 262144 | tf_op jit(solution)/shard_map/all_to_all | solution.py:41

commit v6 on v5

--- a/solution.py
+++ b/solution.py
@@ -538,7 +538,7 @@
     other = lax.ppermute(other, "c", SWAP)
     back = exchange(back, IMAGE_AXES, 16)
     keep, send, plain = text_tile(place, own, other, unit)
-    back, keep, send, plain = lax.optimization_barrier((back, keep, send, plain))
+    back, keep, plain = lax.optimization_barrier((back, keep, plain))
     text_part = (keep + lax.ppermute(send, "h", SWAP).astype(F32)).astype(BF16)
     pooled_grad = lax.all_to_all(fresh_back(place, back, near, far, unit, norm), "x", 0, 0)
     image_grad, row_loss = image_end(place, back, image_cache, plain, norm)

time: 117 us -> 112 us (0.957)
  waiting for transfers between devices: 20.4 us -> 17 us
  starting transfers between devices: 63 us -> 61.3 us
    all_to_all x4, waiting for transfers between devices: 13.3 us -> 9.9 us  [exchange(): return lax.all_to_all(sent, axes, 0, 0).reshape(blocks.shape)]
    all_to_all x4, starting transfers between devices: 39.3 us -> 37.6 us  [exchange(): return lax.all_to_all(sent, axes, 0, 0).reshape(blocks.shape)]
  transfers between devices with their start and end apart: 11 -> 11, of which waited for: 9 -> 8; matrix products, arithmetic and copies ran while one was open for 1% -> 1% of each run, Pallas kernels for 18% -> 19%
where the time goes in v6:
time: 112 us; the launch traced here: 110 us
  starting transfers between devices  61.3 us (55%)
  Pallas kernels  27.8 us (25%)
  waiting for transfers between devices  17 us (15%)
  between operations  2.04 us (2%)
  local copies, waits for them, and re-layouts  1.56 us (1%)
    all_to_all x4, starting transfers between devices, exchange(): return lax.all_to_all(sent, axes, 0, 0).reshape(blocks.shape)  37.6 us
    ppermute x3, starting transfers between devices, on_device(): lax.ppermute(pooled, 'x', [((i + s) % 4, i) for i in range(4)])  10.5 us
    all_to_all x4, waiting for transfers between devices, exchange(): return lax.all_to_all(sent, axes, 0, 0).reshape(blocks.shape)  9.9 us
    pallas_call x1, Pallas kernels, attend_back(): pl.pallas_call(attend_back_kernel, grid=(HEADS // PAIRED,), in_specs=[pl....  8.23 us
    pallas_call x1, Pallas kernels, attend(): pl.pallas_call(attend_kernel, grid=(HEADS // PAIRED,), in_specs=[tokens]...  6.97 us
    all_to_all x1, starting transfers between devices, on_device(): lax.all_to_all(fresh_back(place, back, near, far, unit, norm), 'x', 0, 0)  6.03 us
    ppermute x1, starting transfers between devices, on_device(): text_part = (keep + lax.ppermute(send, 'h', SWAP).astype(F32)).astype(BF16)  3.4 us
    pallas_call x1, Pallas kernels, pair_tile(): pl.pallas_call(pair_kernel, in_specs=[SMEM, SMEM, VMEM, VMEM, VMEM, VMEM]...  2.45 us
  transfers between devices with their start and end apart: 11, of which 8 were waited for; matrix products, arithmetic and copies ran while one was open for 1% of the time, Pallas kernels for 19%

profile of v6, /device:TPU:2, one launch (start us, length us, event | category | flops | bytes accessed | tf_op | source)
XLA Modules:
  0.0 110.4 jit_solution(14976806353129251141)
XLA Ops:
  0.6 1.8 %first_messages.1 = (bf16[128,2432]{1,0:T(8,128)(2,1)}, bf16[16,1152]{1,0:T(8,128)(2,1)}) custom-call(s32[8]{0:T(128)} %pair_ref.1, s32[8]{0:T(128)} %igroup_ref.1, s32[8]{0:T(128)} %tgroup_ref.1, bf16[8,1024]{1,0:T(8,128)(2,1)} %embed_ref.1, bf16[8,1024]{1,0:T(8,128)(2,1)} %cache_ref.3, bf16[8,1280]{1,0:T(8,128)(2,1)} %bitcast.29), custom_call_target="tpu_custom_call" | custom-call | bytes 3600000 | tf_op jit(solution)/shard_map/first_messages/pallas_call | solution.py:195
  2.4 15.7 %all-to-all-start = ((bf16[16,8,2432]{2,1,0:T(8,128)(2,1)}), bf16[16,8,2432]{2,1,0:T(8,128)(2,1)S(1)}, u32[]{:S(2)}, u32[]{:S(2)}) async-start(bf16[16,8,2432]{2,1,0:T(8,128)(2,1)} %bitcast.28), calls=%async_computation | async-start | bytes 1245184 | tf_op jit(solution)/shard_map/all_to_all | solution.py:41
  18.1 7.0 %attend.1 = (f32[10,257,257]{2,1,0:T(8,128)}, bf16[10,8,257]{2,1,0:T(8,128)(2,1)}, f32[16,128]{1,0:T(8,128)}) custom-call(bf16[1,257,1280]{2,1,0:T(8,128)(2,1)} %q_ref.3, bf16[1,257,1280]{2,1,0:T(8,128)(2,1)} %k_ref.3, bf16[1,257,1280]{2,1,0:T(8,128)(2,1)} %v_ref.3), custom_call_target="tpu_custom_call" | custom-call | bytes 25200000 | tf_op jit(solution)/shard_map/attend/pallas_call | solution.py:106
  25.1 3.4 %collective-permute-start.2 = (f32[16,128]{1,0:T(8,128)}, f32[16,128]{1,0:T(8,128)S(1)}, u32[]{:S(2)}, u32[]{:S(2)}) collective-permute-start(f32[16,128]{1,0:T(8,128)} %get-tuple-element.39.p0_ref), channel_id=1, source_target_pairs={{48,0},{0,16},{16,32},{32,48},{49,1},{1,17},{17,33},{33,49},{50,2}... | collective-permute-start | bytes 24584 | tf_op jit(solution)/shard_map/ppermute | solution.py:528
  28.5 3.0 %collective-permute-start.1 = (f32[16,128]{1,0:T(8,128)}, f32[16,128]{1,0:T(8,128)S(1)}, u32[]{:S(2)}, u32[]{:S(2)}) collective-permute-start(f32[16,128]{1,0:T(8,128)} %get-tuple-element.39.p0_ref), channel_id=1, source_target_pairs={{32,0},{48,16},{0,32},{16,48},{33,1},{49,17},{1,33},{17,49},{34,2}... | collective-permute-start | bytes 24584 | tf_op jit(solution)/shard_map/ppermute | solution.py:528
  31.5 4.1 %collective-permute-start = (f32[16,128]{1,0:T(8,128)}, f32[16,128]{1,0:T(8,128)S(1)}, u32[]{:S(2)}, u32[]{:S(2)}) collective-permute-start(f32[16,128]{1,0:T(8,128)} %get-tuple-element.39.p0_ref), channel_id=1, source_target_pairs={{16,0},{32,16},{48,32},{0,48},{17,1},{33,17},{49,33},{1,49},{18,2}... | collective-permute-start | bytes 24584 | tf_op jit(solution)/shard_map/ppermute | solution.py:528
  35.5 0.0 collective-permute-done.2.p3_ref
  35.6 0.2 collective-permute-done.1.p2_ref
  35.7 1.5 %collective-permute-done.p1_ref = f32[16,128]{1,0:T(8,128)S(1)} collective-permute-done((f32[16,128]{1,0:T(8,128)}, f32[16,128]{1,0:T(8,128)S(1)}, u32[]{:S(2)}, u32[]{:S(2)}) %collective-permute-start) | collective-permute-done | bytes 8224 | tf_op jit(solution)/shard_map/ppermute | solution.py:528
  37.2 0.0 all-to-all-done
  37.2 1.9 %collective-permute-start.3 = (bf16[128,2432]{1,0:T(8,128)(2,1)S(1)}, bf16[128,2432]{1,0:T(8,128)(2,1)S(1)}, u32[]{:S(2)}, u32[]{:S(2)}) collective-permute-start(bf16[128,2432]{1,0:T(8,128)(2,1)S(1)} %bitcast.19), channel_id=1, source_target_pairs={{0,4},{4,0},{1,5},{5,1},{2,6},{6,2},{3,7},{7,3},{8,12},{12,8},{9,1... | collective-permute-start | bytes 1867784 | tf_op jit(solution)/shard_map/ppermute | solution.py:531
  39.2 0.1 stack.32.place_ref
  39.2 1.9 %collective-permute-done.3.far_ref = bf16[128,2432]{1,0:T(8,128)(2,1)S(1)} collective-permute-done((bf16[128,2432]{1,0:T(8,128)(2,1)S(1)}, bf16[128,2432]{1,0:T(8,128)(2,1)S(1)}, u32[]{:S(2)}, u32[]{:S(2)}) %collective-permute-start.3) | collective-permute-done | bytes 622624 | tf_op jit(solution)/shard_map/ppermute | solution.py:531
  41.2 0.0 copy-start.2
  41.2 0.8 copy-done.2
  41.9 0.0 copy-start.3
  41.9 0.7 copy-done.3
  42.6 1.6 %fresh_message.1 = bf16[128,1408]{1,0:T(8,128)(2,1)} custom-call(s32[5]{0:T(128)S(1)} %stack.32.place_ref, f32[16,128]{1,0:T(8,128)S(1)} %copy-done.3, f32[16,128]{1,0:T(8,128)S(1)} %collective-permute-done.p1_ref, f32[16,128]{1,0:T(8,128)S(1)} %collective-permute-done.1.p2_ref, f32[16,128]{1,0:T(8,128)S(1)} %collective-permute-done.2.p3_ref, ...), custom_call_target="tpu_custom_call" | custom-call | bytes 3600000 | tf_op jit(solution)/shard_map/fresh_message/pallas_call | solution.py:235
  44.2 0.0 copy-start
  44.2 11.8 %all-to-all-start.1 = ((bf16[16,8,1408]{2,1,0:T(8,128)(2,1)}), bf16[16,8,1408]{2,1,0:T(8,128)(2,1)S(1)}, u32[]{:S(2)}, u32[]{:S(2)}) async-start(bf16[16,8,1408]{2,1,0:T(8,128)(2,1)} %bitcast.10), calls=%async_computation.1 | async-start | bytes 720896 | tf_op jit(solution)/shard_map/all_to_all | solution.py:41
  57.3 0.1 pad_maximum_fusion.scalar_ref
  57.4 1.6 %turn.1.turned_ref = bf16[256,1024]{1,0:T(8,128)(2,1)S(1)} custom-call(s32[5]{0:T(128)S(1)} %stack.32.place_ref, bf16[128,2432]{1,0:T(8,128)(2,1)S(1)} %bitcast.21, bf16[128,2432]{1,0:T(8,128)(2,1)S(1)} %collective-permute-done.3.far_ref), custom_call_target="tpu_custom_call" | custom-call | bytes 10800000 | tf_op jit(solution)/shard_map/turn/pallas_call | solution.py:265
  59.0 7.7 %all-to-all-done.1 = bf16[16,8,1408]{2,1,0:T(8,128)(2,1)S(1)} async-done(((bf16[16,8,1408]{2,1,0:T(8,128)(2,1)}), bf16[16,8,1408]{2,1,0:T(8,128)(2,1)S(1)}, u32[]{:S(2)}, u32[]{:S(2)}) %all-to-all-start.1) | async-done | bytes 360480 | tf_op jit(solution)/shard_map/all_to_all | solution.py:41
  66.7 2.5 %pair_tile.1 = (bf16[128,1408]{1,0:T(8,128)(2,1)}, bf16[144,1152]{1,0:T(8,128)(2,1)S(1)}, bf16[144,1152]{1,0:T(8,128)(2,1)S(1)}, f32[8,1024]{1,0:T(8,128)S(1)}, f32[8,128]{1,0:T(8,128)S(1)}) custom-call(s32[5]{0:T(128)S(1)} %stack.32.place_ref, f32[2]{0:T(128)S(1)} %pad_maximum_fusion.scalar_ref, bf16[128,1408]{1,0:T(8,128)(2,1)S(1)} %bitcast.26, ...), custom_call_target="tpu_custom_call" | custom-call | bytes 10800000 | tf_op jit(solution)/shard_map/pair_tile/pallas_call | solution.py:363
  69.2 6.0 %all-to-all-start.2 = ((bf16[16,8,1408]{2,1,0:T(8,128)(2,1)}), bf16[16,8,1408]{2,1,0:T(8,128)(2,1)S(1)}, u32[]{:S(2)}, u32[]{:S(2)}) async-start(bf16[16,8,1408]{2,1,0:T(8,128)(2,1)} %bitcast.12), calls=%async_computation.2 | async-start | bytes 720896 | tf_op jit(solution)/shard_map/all_to_all | solution.py:41
  75.2 1.9 %collective-permute-start.4 = (bf16[144,1152]{1,0:T(8,128)(2,1)S(1)}, bf16[144,1152]{1,0:T(8,128)(2,1)S(1)}, u32[]{:S(2)}, u32[]{:S(2)}) collective-permute-start(bf16[144,1152]{1,0:T(8,128)(2,1)S(1)} %get-tuple-element.47), channel_id=1, source_target_pairs={{0,4},{4,0},{1,5},{5,1},{2,6},{6,2},{3,7},{7,3},{8,12},{12,8},{9,1... | collective-permute-start | bytes 995336 | tf_op jit(solution)/shard_map/ppermute | solution.py:538
  77.1 1.6 %collective-permute-done.4.other_ref = bf16[144,1152]{1,0:T(8,128)(2,1)S(1)} collective-permute-done((bf16[144,1152]{1,0:T(8,128)(2,1)S(1)}, bf16[144,1152]{1,0:T(8,128)(2,1)S(1)}, u32[]{:S(2)}, u32[]{:S(2)}) %collective-permute-start.4) | collective-permute-done | bytes 331808 | tf_op jit(solution)/shard_map/ppermute | solution.py:538
  78.7 1.5 %text_tile.1 = (f32[64,1024]{1,0:T(8,128)S(1)}, bf16[64,1024]{1,0:T(8,128)(2,1)S(1)}, f32[8,1024]{1,0:T(8,128)S(1)}) custom-call(s32[5]{0:T(128)S(1)} %stack.32.place_ref, bf16[144,1152]{1,0:T(8,128)(2,1)S(1)} %get-tuple-element.46.own_ref, bf16[144,1152]{1,0:T(8,128)(2,1)S(1)} %collective-permute-done.4.other_ref, f32[8,1024]{1,0:T(8,128)S(1)} %get-tuple-element.48.unit_ref), custom_call_target="tpu_custom_call" | custom-call | bytes 14400000 | tf_op jit(solution)/shard_map/text_tile/pallas_call | solution.py:436
  80.3 3.4 %collective-permute-start.5 = (bf16[64,1024]{1,0:T(8,128)(2,1)S(1)}, bf16[64,1024]{1,0:T(8,128)(2,1)S(1)}, u32[]{:S(2)}, u32[]{:S(2)}) collective-permute-start(bf16[64,1024]{1,0:T(8,128)(2,1)S(1)} %get-tuple-element.54), channel_id=1, source_target_pairs={{0,8},{8,0},{1,9},{9,1},{2,10},{10,2},{3,11},{11,3},{4,12},{12,4},... | collective-permute-start | bytes 393224 | tf_op jit(solution)/shard_map/ppermute | solution.py:542
  83.7 1.4 %all-to-all-done.2 = bf16[16,8,1408]{2,1,0:T(8,128)(2,1)S(1)} async-done(((bf16[16,8,1408]{2,1,0:T(8,128)(2,1)}), bf16[16,8,1408]{2,1,0:T(8,128)(2,1)S(1)}, u32[]{:S(2)}, u32[]{:S(2)}) %all-to-all-start.2) | async-done | bytes 360480 | tf_op jit(solution)/shard_map/all_to_all | solution.py:41
  85.1 1.5 %fresh_back.1 = f32[4,1,1280]{2,1,0:T(1,128)} custom-call(s32[5]{0:T(128)S(1)} %stack.32.place_ref, bf16[128,1408]{1,0:T(8,128)(2,1)S(1)} %bitcast.24, bf16[128,2432]{1,0:T(8,128)(2,1)S(1)} %bitcast.23, bf16[128,2432]{1,0:T(8,128)(2,1)S(1)} %collective-permute-done.3.far_ref, f32[8,1024]{1,0:T(8,128)S(1)} %get-tuple-element.48.unit_ref, ...), custom_call_target="tpu_custom_call" | custom-call | bytes 7200000 | tf_op jit(solution)/shard_map/fresh_back/pallas_call | solution.py:394
  86.5 0.0 copy-start.1
  86.6 6.0 %all-to-all-start.3 = ((f32[4,1,1280]{2,1,0:T(1,128)}), f32[4,1,1280]{2,1,0:T(1,128)S(1)}, u32[]{:S(2)}, u32[]{:S(2)}) async-start(f32[4,1,1280]{2,1,0:T(1,128)} %fresh_back.1), calls=%async_computation.3 | async-start | bytes 40960 | tf_op jit(solution)/shard_map/all_to_all | solution.py:543
  92.6 0.0 collective-permute-done.5
  92.6 0.7 add_convert_fusion
  93.3 0.0 copy-done
  93.3 1.4 %image_end.1 = (f32[8,1024]{1,0:T(8,128)}, f32[1,8]{1,0:T(1,128)}) custom-call(s32[5]{0:T(128)S(1)} %stack.32.place_ref, bf16[128,1408]{1,0:T(8,128)(2,1)S(1)} %bitcast.25, bf16[8,1024]{1,0:T(8,128)(2,1)S(1)} %copy-done, f32[8,1024]{1,0:T(8,128)S(1)} %get-tuple-element.55.plain_ref, f32[8,128]{1,0:T(8,128)S(1)} %get-tuple-element.52.norm_ref), custom_call_target="tpu_custom_call" | custom-call | bytes 3600000 | tf_op jit(solution)/shard_map/image_end/pallas_call | solution.py:473
  94.6 1.9 %all-to-all-done.3.z_ref = f32[4,1,1280]{2,1,0:T(1,128)S(1)} async-done(((f32[4,1,1280]{2,1,0:T(1,128)}), f32[4,1,1280]{2,1,0:T(1,128)S(1)}, u32[]{:S(2)}, u32[]{:S(2)}) %all-to-all-start.3) | async-done | bytes 20512 | tf_op jit(solution)/shard_map/all_to_all | solution.py:543
  96.5 0.0 copy-start.4
  96.5 4.0 %all-to-all-start.4 = ((bf16[8,8,1024]{2,1,0:T(8,128)(2,1)}), bf16[8,8,1024]{2,1,0:T(8,128)(2,1)S(1)}, u32[]{:S(2)}, u32[]{:S(2)}) async-start(bf16[8,8,1024]{2,1,0:T(8,128)(2,1)} %bitcast.14), calls=%async_computation.4 | async-start | bytes 262144 | tf_op jit(solution)/shard_map/all_to_all | solution.py:41
  100.5 0.0 copy-done.4
  100.6 8.2 %attend_back.1 = (bf16[1,257,1280]{2,1,0:T(8,128)(2,1)}, bf16[1,257,1280]{2,1,0:T(8,128)(2,1)}, bf16[1,257,1280]{2,1,0:T(8,128)(2,1)}) custom-call(f32[4,1,1280]{2,1,0:T(1,128)} %copy-done.4, bf16[1,257,1280]{2,1,0:T(8,128)(2,1)} %q_ref.3, bf16[1,257,1280]{2,1,0:T(8,128)(2,1)} %k_ref.3, bf16[1,257,1280]{2,1,0:T(8,128)(2,1)} %v_ref.3, ...), custom_call_target="tpu_custom_call" | custom-call | bytes 21600000 | tf_op jit(solution)/shard_map/attend_back/pallas_call | solution.py:148
  108.8 0.8 all-to-all-done.4
  109.6 0.0 copy-done.1
  109.6 0.8 text_end.1
Async XLA Ops:
  2.4 34.8 %all-to-all-start = ((bf16[16,8,2432]{2,1,0:T(8,128)(2,1)}), bf16[16,8,2432]{2,1,0:T(8,128)(2,1)S(1)}, u32[]{:S(2)}, u32[]{:S(2)}) async-start(bf16[16,8,2432]{2,1,0:T(8,128)(2,1)} %bitcast.28), calls=%async_computation | async-start | bytes 1245184 | tf_op jit(solution)/shard_map/all_to_all | solution.py:41
  25.1 10.5 %collective-permute-start.2 = (f32[16,128]{1,0:T(8,128)}, f32[16,128]{1,0:T(8,128)S(1)}, u32[]{:S(2)}, u32[]{:S(2)}) collective-permute-start(f32[16,128]{1,0:T(8,128)} %get-tuple-element.39.p0_ref), channel_id=1, source_target_pairs={{48,0},{0,16},{16,32},{32,48},{49,1},{1,17},{17,33},{33,49},{50,2}... | collective-permute-start | bytes 24584 | tf_op jit(solution)/shard_map/ppermute | solution.py:528
  28.5 7.3 %collective-permute-start.1 = (f32[16,128]{1,0:T(8,128)}, f32[16,128]{1,0:T(8,128)S(1)}, u32[]{:S(2)}, u32[]{:S(2)}) collective-permute-start(f32[16,128]{1,0:T(8,128)} %get-tuple-element.39.p0_ref), channel_id=1, source_target_pairs={{32,0},{48,16},{0,32},{16,48},{33,1},{49,17},{1,33},{17,49},{34,2}... | collective-permute-start | bytes 24584 | tf_op jit(solution)/shard_map/ppermute | solution.py:528
  31.5 5.8 %collective-permute-start = (f32[16,128]{1,0:T(8,128)}, f32[16,128]{1,0:T(8,128)S(1)}, u32[]{:S(2)}, u32[]{:S(2)}) collective-permute-start(f32[16,128]{1,0:T(8,128)} %get-tuple-element.39.p0_ref), channel_id=1, source_target_pairs={{16,0},{32,16},{48,32},{0,48},{17,1},{33,17},{49,33},{1,49},{18,2}... | collective-permute-start | bytes 24584 | tf_op jit(solution)/shard_map/ppermute | solution.py:528
  37.2 3.9 %collective-permute-start.3 = (bf16[128,2432]{1,0:T(8,128)(2,1)S(1)}, bf16[128,2432]{1,0:T(8,128)(2,1)S(1)}, u32[]{:S(2)}, u32[]{:S(2)}) collective-permute-start(bf16[128,2432]{1,0:T(8,128)(2,1)S(1)} %bitcast.19), channel_id=1, source_target_pairs={{0,4},{4,0},{1,5},{5,1},{2,6},{6,2},{3,7},{7,3},{8,12},{12,8},{9,1... | collective-permute-start | bytes 1867784 | tf_op jit(solution)/shard_map/ppermute | solution.py:531
  41.2 0.8 copy-start.2
  41.9 0.7 copy-start.3
  44.2 49.1 %copy-start = (bf16[8,1024]{1,0:T(8,128)(2,1)S(1)}, bf16[8,1024]{1,0:T(8,128)(2,1)}, u32[]{:S(2)}) copy-start(bf16[8,1024]{1,0:T(8,128)(2,1)} %cache_ref.3) | copy-start | bytes 49156
  44.2 22.5 %all-to-all-start.1 = ((bf16[16,8,1408]{2,1,0:T(8,128)(2,1)}), bf16[16,8,1408]{2,1,0:T(8,128)(2,1)S(1)}, u32[]{:S(2)}, u32[]{:S(2)}) async-start(bf16[16,8,1408]{2,1,0:T(8,128)(2,1)} %bitcast.10), calls=%async_computation.1 | async-start | bytes 720896 | tf_op jit(solution)/shard_map/all_to_all | solution.py:41
  69.2 15.9 %all-to-all-start.2 = ((bf16[16,8,1408]{2,1,0:T(8,128)(2,1)}), bf16[16,8,1408]{2,1,0:T(8,128)(2,1)S(1)}, u32[]{:S(2)}, u32[]{:S(2)}) async-start(bf16[16,8,1408]{2,1,0:T(8,128)(2,1)} %bitcast.12), calls=%async_computation.2 | async-start | bytes 720896 | tf_op jit(solution)/shard_map/all_to_all | solution.py:41
  75.2 3.5 %collective-permute-start.4 = (bf16[144,1152]{1,0:T(8,128)(2,1)S(1)}, bf16[144,1152]{1,0:T(8,128)(2,1)S(1)}, u32[]{:S(2)}, u32[]{:S(2)}) collective-permute-start(bf16[144,1152]{1,0:T(8,128)(2,1)S(1)} %get-tuple-element.47), channel_id=1, source_target_pairs={{0,4},{4,0},{1,5},{5,1},{2,6},{6,2},{3,7},{7,3},{8,12},{12,8},{9,1... | collective-permute-start | bytes 995336 | tf_op jit(solution)/shard_map/ppermute | solution.py:538
  80.3 12.3 %collective-permute-start.5 = (bf16[64,1024]{1,0:T(8,128)(2,1)S(1)}, bf16[64,1024]{1,0:T(8,128)(2,1)S(1)}, u32[]{:S(2)}, u32[]{:S(2)}) collective-permute-start(bf16[64,1024]{1,0:T(8,128)(2,1)S(1)} %get-tuple-element.54), channel_id=1, source_target_pairs={{0,8},{8,0},{1,9},{9,1},{2,10},{10,2},{3,11},{11,3},{4,12},{12,4},... | collective-permute-start | bytes 393224 | tf_op jit(solution)/shard_map/ppermute | solution.py:542
  86.5 23.1 %copy-start.1 = (bf16[8,1024]{1,0:T(8,128)(2,1)S(1)}, bf16[8,1024]{1,0:T(8,128)(2,1)}, u32[]{:S(2)}) copy-start(bf16[8,1024]{1,0:T(8,128)(2,1)} %embed_ref.1) | copy-start | bytes 49156
  86.6 10.0 %all-to-all-start.3 = ((f32[4,1,1280]{2,1,0:T(1,128)}), f32[4,1,1280]{2,1,0:T(1,128)S(1)}, u32[]{:S(2)}, u32[]{:S(2)}) async-start(f32[4,1,1280]{2,1,0:T(1,128)} %fresh_back.1), calls=%async_computation.3 | async-start | bytes 40960 | tf_op jit(solution)/shard_map/all_to_all | solution.py:543
  96.5 4.0 %copy-start.4 = (f32[4,1,1280]{2,1,0:T(1,128)}, f32[4,1,1280]{2,1,0:T(1,128)S(1)}, u32[]{:S(2)}) copy-start(f32[4,1,1280]{2,1,0:T(1,128)S(1)} %all-to-all-done.3.z_ref) | copy-start | bytes 61444
  96.5 13.1 %all-to-all-start.4 = ((bf16[8,8,1024]{2,1,0:T(8,128)(2,1)}), bf16[8,8,1024]{2,1,0:T(8,128)(2,1)S(1)}, u32[]{:S(2)}, u32[]{:S(2)}) async-start(bf16[8,8,1024]{2,1,0:T(8,128)(2,1)} %bitcast.14), calls=%async_computation.4 | async-start | bytes 262144 | tf_op jit(solution)/shard_map/all_to_all | solution.py:41

commit v7 on v6

--- a/solution.py
+++ b/solution.py
@@ -17,7 +17,7 @@
 TAIL = 128
 STEM = EMBED + TAIL
 INV_ROOT = 1.0 / math.sqrt(HEAD_DIM)
-PAIRED = 2
+PAIRED = 5
 
 TEXT_AXES = ("z", "h")
 IMAGE_AXES = ("x", "m")
@@ -91,8 +91,8 @@
             piece = rest.astype(BF16).astype(F32)
             mass = jnp.where(row == place, piece, mass)
             rest = rest - piece
+        mass_ref[one] = mass
         mass = mass.astype(BF16)
-        mass_ref[one] = mass
         pooled = jnp.sum(
             contract(mass, v_ref[0, :, at], ((1,), (0,))), axis=0, keepdims=True
         )
@@ -114,7 +114,7 @@
         ],
         out_shape=[
             jax.ShapeDtypeStruct((HEADS, SEQ, SEQ), F32),
-            jax.ShapeDtypeStruct((HEADS, 8, SEQ), BF16),
+            jax.ShapeDtypeStruct((HEADS, 8, SEQ), F32),
             jax.ShapeDtypeStruct((16, HEAD_DIM), F32),
         ],
         compiler_params=STREAMED,
@@ -136,10 +136,9 @@
         dq_ref[0, :, at] = (contract(score_grad, k_ref[0, :, at], ((1,), (0,))) * INV_ROOT).astype(
             BF16
         )
-        dk_ref[0, :, at] = (contract(score_grad, q_ref[0, :, at], ((0,), (0,))) * INV_ROOT).astype(
-            BF16
-        )
-        dv_ref[0, :, at] = contract(mass_ref[one], cot_rows, ((0,), (0,))).astype(BF16)
+        key_grad = jnp.transpose(contract(q_ref[0, :, at], score_grad, ((0,), (0,))))
+        dk_ref[0, :, at] = (key_grad * INV_ROOT).astype(BF16)
+        dv_ref[0, :, at] = contract(mass_ref[one].astype(BF16), cot_rows, ((0,), (0,))).astype(BF16)
 
 
 def attend_back(pooled_grad, query_tokens, key_tokens, value_tokens, probs, mass):

time: 112 us -> 111 us (level)
  Pallas kernels: 27.8 us -> 26.3 us
  transfers between devices with their start and end apart: 11 -> 11, of which waited for: 8 -> 8; matrix products, arithmetic and copies ran while one was open for 1% -> 1% of each run, Pallas kernels for 19% -> 18%
where the time goes in v7:
time: 111 us; the launch traced here: 110 us
  starting transfers between devices  61.7 us (56%)
  Pallas kernels  26.3 us (24%)
  waiting for transfers between devices  18.1 us (16%)
  between operations  2.04 us (2%)
  local copies, waits for them, and re-layouts  1.56 us (1%)
    all_to_all x4, starting transfers between devices, exchange(): return lax.all_to_all(sent, axes, 0, 0).reshape(blocks.shape)  38 us
    all_to_all x4, waiting for transfers between devices, exchange(): return lax.all_to_all(sent, axes, 0, 0).reshape(blocks.shape)  11 us
    ppermute x3, starting transfers between devices, on_device(): lax.ppermute(pooled, 'x', [((i + s) % 4, i) for i in range(4)])  10.5 us
    pallas_call x1, Pallas kernels, attend_back(): pl.pallas_call(attend_back_kernel, grid=(HEADS // PAIRED,), in_specs=[pl....  7.14 us
    pallas_call x1, Pallas kernels, attend(): pl.pallas_call(attend_kernel, grid=(HEADS // PAIRED,), in_specs=[tokens]...  6.55 us
    all_to_all x1, starting transfers between devices, on_device(): lax.all_to_all(fresh_back(place, back, near, far, unit, norm), 'x', 0, 0)  6.03 us
    ppermute x1, starting transfers between devices, on_device(): text_part = (keep + lax.ppermute(send, 'h', SWAP).astype(F32)).astype(BF16)  3.4 us
    pallas_call x1, Pallas kernels, pair_tile(): pl.pallas_call(pair_kernel, in_specs=[SMEM, SMEM, VMEM, VMEM, VMEM, VMEM]...  2.45 us
  transfers between devices with their start and end apart: 11, of which 8 were waited for; matrix products, arithmetic and copies ran while one was open for 1% of the time, Pallas kernels for 18%

profile of v7, /device:TPU:2, one launch (start us, length us, event | category | flops | bytes accessed | tf_op | source)
XLA Modules:
  0.0 110.4 jit_solution(4025499126839676258)
XLA Ops:
  0.6 1.8 %first_messages.1 = (bf16[128,2432]{1,0:T(8,128)(2,1)}, bf16[16,1152]{1,0:T(8,128)(2,1)}) custom-call(s32[8]{0:T(128)} %pair_ref.1, s32[8]{0:T(128)} %igroup_ref.1, s32[8]{0:T(128)} %tgroup_ref.1, bf16[8,1024]{1,0:T(8,128)(2,1)} %embed_ref.1, bf16[8,1024]{1,0:T(8,128)(2,1)} %cache_ref.3, bf16[8,1280]{1,0:T(8,128)(2,1)} %bitcast.29), custom_call_target="tpu_custom_call" | custom-call | bytes 3600000 | tf_op jit(solution)/shard_map/first_messages/pallas_call | solution.py:194
  2.4 15.7 %all-to-all-start = ((bf16[16,8,2432]{2,1,0:T(8,128)(2,1)}), bf16[16,8,2432]{2,1,0:T(8,128)(2,1)S(1)}, u32[]{:S(2)}, u32[]{:S(2)}) async-start(bf16[16,8,2432]{2,1,0:T(8,128)(2,1)} %bitcast.28), calls=%async_computation | async-start | bytes 1245184 | tf_op jit(solution)/shard_map/all_to_all | solution.py:41
  18.1 6.6 %attend.1 = (f32[10,257,257]{2,1,0:T(8,128)}, f32[10,8,257]{2,1,0:T(8,128)}, f32[16,128]{1,0:T(8,128)}) custom-call(bf16[1,257,1280]{2,1,0:T(8,128)(2,1)} %q_ref.3, bf16[1,257,1280]{2,1,0:T(8,128)(2,1)} %k_ref.3, bf16[1,257,1280]{2,1,0:T(8,128)(2,1)} %v_ref.3), custom_call_target="tpu_custom_call" | custom-call | bytes 25200000 | tf_op jit(solution)/shard_map/attend/pallas_call | solution.py:106
  24.6 3.4 %collective-permute-start.2 = (f32[16,128]{1,0:T(8,128)}, f32[16,128]{1,0:T(8,128)S(1)}, u32[]{:S(2)}, u32[]{:S(2)}) collective-permute-start(f32[16,128]{1,0:T(8,128)} %get-tuple-element.39.p0_ref), channel_id=1, source_target_pairs={{48,0},{0,16},{16,32},{32,48},{49,1},{1,17},{17,33},{33,49},{50,2}... | collective-permute-start | bytes 24584 | tf_op jit(solution)/shard_map/ppermute | solution.py:527
  28.0 3.0 %collective-permute-start.1 = (f32[16,128]{1,0:T(8,128)}, f32[16,128]{1,0:T(8,128)S(1)}, u32[]{:S(2)}, u32[]{:S(2)}) collective-permute-start(f32[16,128]{1,0:T(8,128)} %get-tuple-element.39.p0_ref), channel_id=1, source_target_pairs={{32,0},{48,16},{0,32},{16,48},{33,1},{49,17},{1,33},{17,49},{34,2}... | collective-permute-start | bytes 24584 | tf_op jit(solution)/shard_map/ppermute | solution.py:527
  31.1 4.1 %collective-permute-start = (f32[16,128]{1,0:T(8,128)}, f32[16,128]{1,0:T(8,128)S(1)}, u32[]{:S(2)}, u32[]{:S(2)}) collective-permute-start(f32[16,128]{1,0:T(8,128)} %get-tuple-element.39.p0_ref), channel_id=1, source_target_pairs={{16,0},{32,16},{48,32},{0,48},{17,1},{33,17},{49,33},{1,49},{18,2}... | collective-permute-start | bytes 24584 | tf_op jit(solution)/shard_map/ppermute | solution.py:527
  35.1 0.0 collective-permute-done.2.p3_ref
  35.1 0.2 collective-permute-done.1.p2_ref
  35.3 1.5 %collective-permute-done.p1_ref = f32[16,128]{1,0:T(8,128)S(1)} collective-permute-done((f32[16,128]{1,0:T(8,128)}, f32[16,128]{1,0:T(8,128)S(1)}, u32[]{:S(2)}, u32[]{:S(2)}) %collective-permute-start) | collective-permute-done | bytes 8224 | tf_op jit(solution)/shard_map/ppermute | solution.py:527
  36.8 0.0 all-to-all-done
  36.8 1.9 %collective-permute-start.3 = (bf16[128,2432]{1,0:T(8,128)(2,1)S(1)}, bf16[128,2432]{1,0:T(8,128)(2,1)S(1)}, u32[]{:S(2)}, u32[]{:S(2)}) collective-permute-start(bf16[128,2432]{1,0:T(8,128)(2,1)S(1)} %bitcast.19), channel_id=1, source_target_pairs={{0,4},{4,0},{1,5},{5,1},{2,6},{6,2},{3,7},{7,3},{8,12},{12,8},{9,1... | collective-permute-start | bytes 1867784 | tf_op jit(solution)/shard_map/ppermute | solution.py:530
  38.7 0.1 stack.32.place_ref
  38.8 1.9 %collective-permute-done.3.far_ref = bf16[128,2432]{1,0:T(8,128)(2,1)S(1)} collective-permute-done((bf16[128,2432]{1,0:T(8,128)(2,1)S(1)}, bf16[128,2432]{1,0:T(8,128)(2,1)S(1)}, u32[]{:S(2)}, u32[]{:S(2)}) %collective-permute-start.3) | collective-permute-done | bytes 622624 | tf_op jit(solution)/shard_map/ppermute | solution.py:530
  40.8 0.0 copy-start.2
  40.8 0.8 copy-done.2
  41.5 0.0 copy-start.3
  41.5 0.7 copy-done.3
  42.2 1.6 %fresh_message.1 = bf16[128,1408]{1,0:T(8,128)(2,1)} custom-call(s32[5]{0:T(128)S(1)} %stack.32.place_ref, f32[16,128]{1,0:T(8,128)S(1)} %copy-done.3, f32[16,128]{1,0:T(8,128)S(1)} %collective-permute-done.p1_ref, f32[16,128]{1,0:T(8,128)S(1)} %collective-permute-done.1.p2_ref, f32[16,128]{1,0:T(8,128)S(1)} %collective-permute-done.2.p3_ref, ...), custom_call_target="tpu_custom_call" | custom-call | bytes 3600000 | tf_op jit(solution)/shard_map/fresh_message/pallas_call | solution.py:234
  43.8 0.0 copy-start
  43.8 12.2 %all-to-all-start.1 = ((bf16[16,8,1408]{2,1,0:T(8,128)(2,1)}), bf16[16,8,1408]{2,1,0:T(8,128)(2,1)S(1)}, u32[]{:S(2)}, u32[]{:S(2)}) async-start(bf16[16,8,1408]{2,1,0:T(8,128)(2,1)} %bitcast.10), calls=%async_computation.1 | async-start | bytes 720896 | tf_op jit(solution)/shard_map/all_to_all | solution.py:41
  57.3 0.1 pad_maximum_fusion.scalar_ref
  57.4 1.6 %turn.1.turned_ref = bf16[256,1024]{1,0:T(8,128)(2,1)S(1)} custom-call(s32[5]{0:T(128)S(1)} %stack.32.place_ref, bf16[128,2432]{1,0:T(8,128)(2,1)S(1)} %bitcast.21, bf16[128,2432]{1,0:T(8,128)(2,1)S(1)} %collective-permute-done.3.far_ref), custom_call_target="tpu_custom_call" | custom-call | bytes 10800000 | tf_op jit(solution)/shard_map/turn/pallas_call | solution.py:264
  59.0 7.7 %all-to-all-done.1 = bf16[16,8,1408]{2,1,0:T(8,128)(2,1)S(1)} async-done(((bf16[16,8,1408]{2,1,0:T(8,128)(2,1)}), bf16[16,8,1408]{2,1,0:T(8,128)(2,1)S(1)}, u32[]{:S(2)}, u32[]{:S(2)}) %all-to-all-start.1) | async-done | bytes 360480 | tf_op jit(solution)/shard_map/all_to_all | solution.py:41
  66.7 2.5 %pair_tile.1 = (bf16[128,1408]{1,0:T(8,128)(2,1)}, bf16[144,1152]{1,0:T(8,128)(2,1)S(1)}, bf16[144,1152]{1,0:T(8,128)(2,1)S(1)}, f32[8,1024]{1,0:T(8,128)S(1)}, f32[8,128]{1,0:T(8,128)S(1)}) custom-call(s32[5]{0:T(128)S(1)} %stack.32.place_ref, f32[2]{0:T(128)S(1)} %pad_maximum_fusion.scalar_ref, bf16[128,1408]{1,0:T(8,128)(2,1)S(1)} %bitcast.26, ...), custom_call_target="tpu_custom_call" | custom-call | bytes 10800000 | tf_op jit(solution)/shard_map/pair_tile/pallas_call | solution.py:362
  69.2 6.0 %all-to-all-start.2 = ((bf16[16,8,1408]{2,1,0:T(8,128)(2,1)}), bf16[16,8,1408]{2,1,0:T(8,128)(2,1)S(1)}, u32[]{:S(2)}, u32[]{:S(2)}) async-start(bf16[16,8,1408]{2,1,0:T(8,128)(2,1)} %bitcast.12), calls=%async_computation.2 | async-start | bytes 720896 | tf_op jit(solution)/shard_map/all_to_all | solution.py:41
  75.2 1.9 %collective-permute-start.4 = (bf16[144,1152]{1,0:T(8,128)(2,1)S(1)}, bf16[144,1152]{1,0:T(8,128)(2,1)S(1)}, u32[]{:S(2)}, u32[]{:S(2)}) collective-permute-start(bf16[144,1152]{1,0:T(8,128)(2,1)S(1)} %get-tuple-element.47), channel_id=1, source_target_pairs={{0,4},{4,0},{1,5},{5,1},{2,6},{6,2},{3,7},{7,3},{8,12},{12,8},{9,1... | collective-permute-start | bytes 995336 | tf_op jit(solution)/shard_map/ppermute | solution.py:537
  77.1 1.6 %collective-permute-done.4.other_ref = bf16[144,1152]{1,0:T(8,128)(2,1)S(1)} collective-permute-done((bf16[144,1152]{1,0:T(8,128)(2,1)S(1)}, bf16[144,1152]{1,0:T(8,128)(2,1)S(1)}, u32[]{:S(2)}, u32[]{:S(2)}) %collective-permute-start.4) | collective-permute-done | bytes 331808 | tf_op jit(solution)/shard_map/ppermute | solution.py:537
  78.7 1.5 %text_tile.1 = (f32[64,1024]{1,0:T(8,128)S(1)}, bf16[64,1024]{1,0:T(8,128)(2,1)S(1)}, f32[8,1024]{1,0:T(8,128)S(1)}) custom-call(s32[5]{0:T(128)S(1)} %stack.32.place_ref, bf16[144,1152]{1,0:T(8,128)(2,1)S(1)} %get-tuple-element.46.own_ref, bf16[144,1152]{1,0:T(8,128)(2,1)S(1)} %collective-permute-done.4.other_ref, f32[8,1024]{1,0:T(8,128)S(1)} %get-tuple-element.48.unit_ref), custom_call_target="tpu_custom_call" | custom-call | bytes 14400000 | tf_op jit(solution)/shard_map/text_tile/pallas_call | solution.py:435
  80.3 3.4 %collective-permute-start.5 = (bf16[64,1024]{1,0:T(8,128)(2,1)S(1)}, bf16[64,1024]{1,0:T(8,128)(2,1)S(1)}, u32[]{:S(2)}, u32[]{:S(2)}) collective-permute-start(bf16[64,1024]{1,0:T(8,128)(2,1)S(1)} %get-tuple-element.54), channel_id=1, source_target_pairs={{0,8},{8,0},{1,9},{9,1},{2,10},{10,2},{3,11},{11,3},{4,12},{12,4},... | collective-permute-start | bytes 393224 | tf_op jit(solution)/shard_map/ppermute | solution.py:541
  83.7 1.4 %all-to-all-done.2 = bf16[16,8,1408]{2,1,0:T(8,128)(2,1)S(1)} async-done(((bf16[16,8,1408]{2,1,0:T(8,128)(2,1)}), bf16[16,8,1408]{2,1,0:T(8,128)(2,1)S(1)}, u32[]{:S(2)}, u32[]{:S(2)}) %all-to-all-start.2) | async-done | bytes 360480 | tf_op jit(solution)/shard_map/all_to_all | solution.py:41
  85.1 1.5 %fresh_back.1 = f32[4,1,1280]{2,1,0:T(1,128)} custom-call(s32[5]{0:T(128)S(1)} %stack.32.place_ref, bf16[128,1408]{1,0:T(8,128)(2,1)S(1)} %bitcast.24, bf16[128,2432]{1,0:T(8,128)(2,1)S(1)} %bitcast.23, bf16[128,2432]{1,0:T(8,128)(2,1)S(1)} %collective-permute-done.3.far_ref, f32[8,1024]{1,0:T(8,128)S(1)} %get-tuple-element.48.unit_ref, ...), custom_call_target="tpu_custom_call" | custom-call | bytes 7200000 | tf_op jit(solution)/shard_map/fresh_back/pallas_call | solution.py:393
  86.5 0.0 copy-start.1
  86.6 6.0 %all-to-all-start.3 = ((f32[4,1,1280]{2,1,0:T(1,128)}), f32[4,1,1280]{2,1,0:T(1,128)S(1)}, u32[]{:S(2)}, u32[]{:S(2)}) async-start(f32[4,1,1280]{2,1,0:T(1,128)} %fresh_back.1), calls=%async_computation.3 | async-start | bytes 40960 | tf_op jit(solution)/shard_map/all_to_all | solution.py:542
  92.6 0.0 collective-permute-done.5
  92.6 0.7 add_convert_fusion
  93.3 0.0 copy-done
  93.3 1.4 %image_end.1 = (f32[8,1024]{1,0:T(8,128)}, f32[1,8]{1,0:T(1,128)}) custom-call(s32[5]{0:T(128)S(1)} %stack.32.place_ref, bf16[128,1408]{1,0:T(8,128)(2,1)S(1)} %bitcast.25, bf16[8,1024]{1,0:T(8,128)(2,1)S(1)} %copy-done, f32[8,1024]{1,0:T(8,128)S(1)} %get-tuple-element.55.plain_ref, f32[8,128]{1,0:T(8,128)S(1)} %get-tuple-element.52.norm_ref), custom_call_target="tpu_custom_call" | custom-call | bytes 3600000 | tf_op jit(solution)/shard_map/image_end/pallas_call | solution.py:472
  94.6 1.9 %all-to-all-done.3.z_ref = f32[4,1,1280]{2,1,0:T(1,128)S(1)} async-done(((f32[4,1,1280]{2,1,0:T(1,128)}), f32[4,1,1280]{2,1,0:T(1,128)S(1)}, u32[]{:S(2)}, u32[]{:S(2)}) %all-to-all-start.3) | async-done | bytes 20512 | tf_op jit(solution)/shard_map/all_to_all | solution.py:542
  96.5 0.0 copy-start.4
  96.5 4.0 %all-to-all-start.4 = ((bf16[8,8,1024]{2,1,0:T(8,128)(2,1)}), bf16[8,8,1024]{2,1,0:T(8,128)(2,1)S(1)}, u32[]{:S(2)}, u32[]{:S(2)}) async-start(bf16[8,8,1024]{2,1,0:T(8,128)(2,1)} %bitcast.14), calls=%async_computation.4 | async-start | bytes 262144 | tf_op jit(solution)/shard_map/all_to_all | solution.py:41
  100.5 0.0 copy-done.4
  100.6 7.1 %attend_back.1 = (bf16[1,257,1280]{2,1,0:T(8,128)(2,1)}, bf16[1,257,1280]{2,1,0:T(8,128)(2,1)}, bf16[1,257,1280]{2,1,0:T(8,128)(2,1)}) custom-call(f32[4,1,1280]{2,1,0:T(1,128)} %copy-done.4, bf16[1,257,1280]{2,1,0:T(8,128)(2,1)} %q_ref.3, bf16[1,257,1280]{2,1,0:T(8,128)(2,1)} %k_ref.3, bf16[1,257,1280]{2,1,0:T(8,128)(2,1)} %v_ref.3, ...), custom_call_target="tpu_custom_call" | custom-call | bytes 21600000 | tf_op jit(solution)/shard_map/attend_back/pallas_call | solution.py:147
  107.7 1.9 %all-to-all-done.4 = bf16[8,8,1024]{2,1,0:T(8,128)(2,1)S(1)} async-done(((bf16[8,8,1024]{2,1,0:T(8,128)(2,1)}), bf16[8,8,1024]{2,1,0:T(8,128)(2,1)S(1)}, u32[]{:S(2)}, u32[]{:S(2)}) %all-to-all-start.4) | async-done | bytes 131104 | tf_op jit(solution)/shard_map/all_to_all | solution.py:41
  109.6 0.0 copy-done.1
  109.6 0.8 text_end.1
Async XLA Ops:
  2.4 34.4 %all-to-all-start = ((bf16[16,8,2432]{2,1,0:T(8,128)(2,1)}), bf16[16,8,2432]{2,1,0:T(8,128)(2,1)S(1)}, u32[]{:S(2)}, u32[]{:S(2)}) async-start(bf16[16,8,2432]{2,1,0:T(8,128)(2,1)} %bitcast.28), calls=%async_computation | async-start | bytes 1245184 | tf_op jit(solution)/shard_map/all_to_all | solution.py:41
  24.6 10.5 %collective-permute-start.2 = (f32[16,128]{1,0:T(8,128)}, f32[16,128]{1,0:T(8,128)S(1)}, u32[]{:S(2)}, u32[]{:S(2)}) collective-permute-start(f32[16,128]{1,0:T(8,128)} %get-tuple-element.39.p0_ref), channel_id=1, source_target_pairs={{48,0},{0,16},{16,32},{32,48},{49,1},{1,17},{17,33},{33,49},{50,2}... | collective-permute-start | bytes 24584 | tf_op jit(solution)/shard_map/ppermute | solution.py:527
  28.0 7.3 %collective-permute-start.1 = (f32[16,128]{1,0:T(8,128)}, f32[16,128]{1,0:T(8,128)S(1)}, u32[]{:S(2)}, u32[]{:S(2)}) collective-permute-start(f32[16,128]{1,0:T(8,128)} %get-tuple-element.39.p0_ref), channel_id=1, source_target_pairs={{32,0},{48,16},{0,32},{16,48},{33,1},{49,17},{1,33},{17,49},{34,2}... | collective-permute-start | bytes 24584 | tf_op jit(solution)/shard_map/ppermute | solution.py:527
  31.1 5.8 %collective-permute-start = (f32[16,128]{1,0:T(8,128)}, f32[16,128]{1,0:T(8,128)S(1)}, u32[]{:S(2)}, u32[]{:S(2)}) collective-permute-start(f32[16,128]{1,0:T(8,128)} %get-tuple-element.39.p0_ref), channel_id=1, source_target_pairs={{16,0},{32,16},{48,32},{0,48},{17,1},{33,17},{49,33},{1,49},{18,2}... | collective-permute-start | bytes 24584 | tf_op jit(solution)/shard_map/ppermute | solution.py:527
  36.8 3.9 %collective-permute-start.3 = (bf16[128,2432]{1,0:T(8,128)(2,1)S(1)}, bf16[128,2432]{1,0:T(8,128)(2,1)S(1)}, u32[]{:S(2)}, u32[]{:S(2)}) collective-permute-start(bf16[128,2432]{1,0:T(8,128)(2,1)S(1)} %bitcast.19), channel_id=1, source_target_pairs={{0,4},{4,0},{1,5},{5,1},{2,6},{6,2},{3,7},{7,3},{8,12},{12,8},{9,1... | collective-permute-start | bytes 1867784 | tf_op jit(solution)/shard_map/ppermute | solution.py:530
  40.8 0.8 copy-start.2
  41.5 0.7 copy-start.3
  43.8 49.5 %copy-start = (bf16[8,1024]{1,0:T(8,128)(2,1)S(1)}, bf16[8,1024]{1,0:T(8,128)(2,1)}, u32[]{:S(2)}) copy-start(bf16[8,1024]{1,0:T(8,128)(2,1)} %cache_ref.3) | copy-start | bytes 49156
  43.8 22.9 %all-to-all-start.1 = ((bf16[16,8,1408]{2,1,0:T(8,128)(2,1)}), bf16[16,8,1408]{2,1,0:T(8,128)(2,1)S(1)}, u32[]{:S(2)}, u32[]{:S(2)}) async-start(bf16[16,8,1408]{2,1,0:T(8,128)(2,1)} %bitcast.10), calls=%async_computation.1 | async-start | bytes 720896 | tf_op jit(solution)/shard_map/all_to_all | solution.py:41
  69.2 15.9 %all-to-all-start.2 = ((bf16[16,8,1408]{2,1,0:T(8,128)(2,1)}), bf16[16,8,1408]{2,1,0:T(8,128)(2,1)S(1)}, u32[]{:S(2)}, u32[]{:S(2)}) async-start(bf16[16,8,1408]{2,1,0:T(8,128)(2,1)} %bitcast.12), calls=%async_computation.2 | async-start | bytes 720896 | tf_op jit(solution)/shard_map/all_to_all | solution.py:41
  75.2 3.5 %collective-permute-start.4 = (bf16[144,1152]{1,0:T(8,128)(2,1)S(1)}, bf16[144,1152]{1,0:T(8,128)(2,1)S(1)}, u32[]{:S(2)}, u32[]{:S(2)}) collective-permute-start(bf16[144,1152]{1,0:T(8,128)(2,1)S(1)} %get-tuple-element.47), channel_id=1, source_target_pairs={{0,4},{4,0},{1,5},{5,1},{2,6},{6,2},{3,7},{7,3},{8,12},{12,8},{9,1... | collective-permute-start | bytes 995336 | tf_op jit(solution)/shard_map/ppermute | solution.py:537
  80.3 12.3 %collective-permute-start.5 = (bf16[64,1024]{1,0:T(8,128)(2,1)S(1)}, bf16[64,1024]{1,0:T(8,128)(2,1)S(1)}, u32[]{:S(2)}, u32[]{:S(2)}) collective-permute-start(bf16[64,1024]{1,0:T(8,128)(2,1)S(1)} %get-tuple-element.54), channel_id=1, source_target_pairs={{0,8},{8,0},{1,9},{9,1},{2,10},{10,2},{3,11},{11,3},{4,12},{12,4},... | collective-permute-start | bytes 393224 | tf_op jit(solution)/shard_map/ppermute | solution.py:541
  86.5 23.1 %copy-start.1 = (bf16[8,1024]{1,0:T(8,128)(2,1)S(1)}, bf16[8,1024]{1,0:T(8,128)(2,1)}, u32[]{:S(2)}) copy-start(bf16[8,1024]{1,0:T(8,128)(2,1)} %embed_ref.1) | copy-start | bytes 49156
  86.6 10.0 %all-to-all-start.3 = ((f32[4,1,1280]{2,1,0:T(1,128)}), f32[4,1,1280]{2,1,0:T(1,128)S(1)}, u32[]{:S(2)}, u32[]{:S(2)}) async-start(f32[4,1,1280]{2,1,0:T(1,128)} %fresh_back.1), calls=%async_computation.3 | async-start | bytes 40960 | tf_op jit(solution)/shard_map/all_to_all | solution.py:542
  96.5 4.0 %copy-start.4 = (f32[4,1,1280]{2,1,0:T(1,128)}, f32[4,1,1280]{2,1,0:T(1,128)S(1)}, u32[]{:S(2)}) copy-start(f32[4,1,1280]{2,1,0:T(1,128)S(1)} %all-to-all-done.3.z_ref) | copy-start | bytes 61444
  96.5 13.1 %all-to-all-start.4 = ((bf16[8,8,1024]{2,1,0:T(8,128)(2,1)}), bf16[8,8,1024]{2,1,0:T(8,128)(2,1)S(1)}, u32[]{:S(2)}, u32[]{:S(2)}) async-start(bf16[8,8,1024]{2,1,0:T(8,128)(2,1)} %bitcast.14), calls=%async_computation.4 | async-start | bytes 262144 | tf_op jit(solution)/shard_map/all_to_all | solution.py:41
